TPU v7x, 512 devices: a whole 4x4x16 slice. The times are simulated.
512 devices in a mesh: il: 8 (over z_lo), xl: 8 (over y, core), gz: 8 (over z_hi, x).
Axes of the slice: x: 4, y: 4, z: 16 (z_hi: 2, z_lo: 8; z = z_hi * 8 + z_lo), core: 2. Of those that a mesh axis runs over, the one named last changes fastest.
Arguments:
- reflect: float32 [320, 320, 1024], P('il', 'xl', 'gz'), may hold values from -6 to 6
- weights: bfloat16 [2, 320, 320, 1024], P(None, 'il', 'xl', 'gz'), may hold values from 0.099609375 to 1
- cell_slot: int32 [2, 320, 320, 1024], P(None, 'il', 'xl', 'gz'), may hold values from 0 to 2, as said below
- factors: bfloat16 [2048, 1536], P(('il', 'xl', 'gz')), may hold values from -0.5390625 to 0.5390625
- reader_list: int32 [8, 8, 8, 3], P('il', 'xl', 'gz'), may hold values from -1 to 2047, as said below
Outputs:
- image: float32 [320, 320, 1024], P('il', 'xl', 'gz')
Inputs may be any that keep to these rules, and one draw needn't show every extreme that they name: `reader_list`: row g of factors belongs to the device at position g // 4 of the devices in order il, xl, gz. A device's list holds 1 to 3 distinct ids first and -1 after them; 3 on some device. Every id belongs to a device with the same il and gz index, and at most 2 ids of a list to one device, 2 reached on some device. `cell_slot`: each entry points into the first part of its device's list, which holds ids.
All inputs are finite; a program needn't handle non-finite values.
Results may differ from a plain program's by a relative error of at most 0.005.
Values may be sent and summed in bfloat16 or wider, within the bound.
No kernel may reach another device: no remote copies, remote signals or barrier semaphores. Data moves between devices by JAX's collectives and lax.ppermute only.
A program may use at most 64 MiB of HBM per device.

v0:
```python
import jax
import jax.numpy as jnp
import numpy as np
from jax import lax
from jax.sharding import PartitionSpec as P

K = 64
R = 8
CP_DEV = 4
NEED = 3


def padded(cells, sides, width):
    for axis, dim in sides:
        count = lax.axis_size(axis)
        ends = count - 1
        head = lax.slice_in_dim(cells, 0, width, axis=dim)
        tail = lax.slice_in_dim(cells, cells.shape[dim] - width, cells.shape[dim], axis=dim)
        cells = jnp.concatenate(
            [
                lax.ppermute(tail, axis, [(i, (i + 1) % count) for i in range(ends)]),
                cells,
                lax.ppermute(head, axis, [((i + 1) % count, i) for i in range(ends)]),
            ],
            axis=dim,
        )
    return cells


def shift_table(length, tap_count):
    offset = np.arange(length + tap_count)[None, :] - np.arange(length)[:, None]
    table = (offset[None, :, :] == np.arange(tap_count)[:, None, None]).astype(np.float32)
    return jnp.asarray(table, jnp.bfloat16)


def banded(filters, table):
    return jnp.einsum("rt,toi->roi", filters, table, preferred_element_type=jnp.float32).astype(
        jnp.bfloat16
    )


def blur_slot(extended, factor_panel, tables, size_x, size_y, size_z):
    filters = factor_panel.reshape(R, 3, K)
    summed = jnp.zeros((size_x, size_y, size_z), jnp.float32)
    for rank_group in range(R // 4):
        chosen = filters[4 * rank_group : 4 * rank_group + 4]
        line_x = jnp.einsum(
            "roi,iyz->royz",
            banded(chosen[:, 0], tables[0]),
            extended,
            preferred_element_type=jnp.float32,
        ).astype(jnp.bfloat16)
        line_y = jnp.einsum(
            "roi,rxiz->rxoz",
            banded(chosen[:, 1], tables[1]),
            line_x,
            preferred_element_type=jnp.float32,
        ).astype(jnp.bfloat16)
        summed = summed + jnp.einsum(
            "roi,rxyi->xyo",
            banded(chosen[:, 2], tables[2]),
            line_y,
            preferred_element_type=jnp.float32,
        )
    return summed


def per_device(reflect, weights, cell_slot, factors, reader_list):
    half_width = K // 2
    size_x, size_y, size_z = reflect.shape
    rounded = reflect.astype(jnp.bfloat16)
    extended = padded(rounded, (("il", 0), ("xl", 1), ("gz", 2)), half_width)
    tables = (shift_table(size_x, K), shift_table(size_y, K), shift_table(size_z, K))
    listed = reader_list.reshape(NEED)
    live_mask = listed >= 0
    live_count = jnp.sum(live_mask.astype(jnp.int32))
    cross_count = lax.axis_size("xl")
    depth_count = lax.axis_size("gz")
    owner_index = jnp.where(live_mask, listed // (CP_DEV * depth_count) % cross_count, 0)
    local_row = jnp.where(live_mask, listed % CP_DEV, 0)
    panel_table = lax.all_gather(factors, "xl", axis=0, tiled=True)
    row_key = owner_index * CP_DEV + local_row
    row_pick = (jnp.arange(cross_count * CP_DEV)[None, :] == row_key[:, None]) & live_mask[:, None]
    panels = jnp.dot(
        row_pick.astype(jnp.bfloat16), panel_table, preferred_element_type=jnp.float32
    ).astype(jnp.bfloat16)

    def add_slot(slot_index, blurred_sum):
        factor_panel = lax.dynamic_index_in_dim(panels, slot_index, 0, keepdims=False)
        weight_map = jnp.sum(
            jnp.where(cell_slot == slot_index, weights.astype(jnp.float32), 0.0), axis=0
        )
        return blurred_sum + weight_map * blur_slot(
            extended, factor_panel, tables, size_x, size_y, size_z
        )

    return lax.fori_loop(
        jnp.zeros((), jnp.int32),
        live_count,
        add_slot,
        jnp.zeros((size_x, size_y, size_z), jnp.float32),
    )


def solution(mesh):
    in_specs = (
        P("il", "xl", "gz"),
        P(None, "il", "xl", "gz"),
        P(None, "il", "xl", "gz"),
        P(("il", "xl", "gz"), None),
        P("il", "xl", "gz", None),
    )
    out_specs = P("il", "xl", "gz")
    return jax.shard_map(
        per_device, mesh=mesh, in_specs=in_specs, out_specs=out_specs, check_vma=False
    )
```

profile of v0, /device:TPU:297, one launch (start us, length us, event | category | flops | bytes accessed | tf_op | source)
XLA Modules:
  0.0 275.8 jit_solution(13777400104067900922)
XLA Ops:
  0.0 1.2 convert_element_type.51
  1.3 2.6 collective-permute-start
  3.9 2.7 collective-permute-start.1
  6.6 5.2 %collective-permute-done = bf16[32,40,128]{2,1,0:T(8,128)(2,1)S(1)} collective-permute-done((bf16[32,40,128]{2,1,0:T(8,128)(2,1)S(1)}, bf16[32,40,128]{2,1,0:T(8,128)(2,1)S(1)}, u32[]{:S(2)}, u32[]{:S(2)}) %collective-permute-start) | collective-permute-done | bytes 327712 | tf_op jit(solution)/shard_map/ppermute | solution.py:21
  11.8 2.3 collective-permute-done.1
  14.2 1.6 fusion.71
  15.8 4.9 %collective-permute-start.2 = (bf16[104,32,128]{2,1,0:T(8,128)(2,1)}, bf16[104,32,128]{2,1,0:T(8,128)(2,1)}, u32[]{:S(2)}, u32[]{:S(2)}) collective-permute-start(bf16[104,32,128]{2,1,0:T(8,128)(2,1)} %get-tuple-element.148), channel_id=1, source_target_pairs={{0,8},{8,16},{16,24},{24,32},{32,40},{40,48},{48,56},{1,9},{9,17},... | collective-permute-start | bytes 2555912 | tf_op jit(solution)/shard_map/ppermute | solution.py:21
  20.7 1.9 collective-permute-start.3
  22.7 3.6 %copy.28 = bf16[104,40,128]{1,2,0:T(8,128)(2,1)S(1)} copy(bf16[104,40,128]{2,1,0:T(8,128)(2,1)} %copy-done.5) | data formatting | bytes 2129920 | tf_op jit(solution)/shard_map/concatenate | solution.py:19
  26.3 4.4 %collective-permute-done.2 = bf16[104,32,128]{2,1,0:T(8,128)(2,1)} collective-permute-done((bf16[104,32,128]{2,1,0:T(8,128)(2,1)}, bf16[104,32,128]{2,1,0:T(8,128)(2,1)}, u32[]{:S(2)}, u32[]{:S(2)}) %collective-permute-start.2) | collective-permute-done | bytes 852000 | tf_op jit(solution)/shard_map/ppermute | solution.py:21
  30.7 3.9 %copy.27 = bf16[104,32,128]{1,2,0:T(8,128)(2,1)} copy(bf16[104,32,128]{2,1,0:T(8,128)(2,1)} %collective-permute-done.2) | data formatting | bytes 1703936 | tf_op jit(solution)/shard_map/ppermute | solution.py:21
  34.5 0.5 collective-permute-done.3
  35.1 3.9 %copy.29 = bf16[104,32,128]{1,2,0:T(8,128)(2,1)} copy(bf16[104,32,128]{2,1,0:T(8,128)(2,1)} %collective-permute-done.3) | data formatting | bytes 1703936 | tf_op jit(solution)/shard_map/ppermute | solution.py:23
  39.0 4.8 %pad_maximum_fusion.4 = (bf16[104,104,32]{1,2,0:T(8,128)(2,1)}, bf16[104,104,32]{1,2,0:T(8,128)(2,1)}) fusion(bf16[104,32,128]{1,2,0:T(8,128)(2,1)} %copy.29, bf16[104,40,128]{1,2,0:T(8,128)(2,1)S(1)} %copy.28, bf16[104,32,128]{1,2,0:T(8,128)(2,1)} %copy.27), kind=kLoop, calls=%fused_computation.51 | loop fusion | flops 4153344 | bytes 4153344 | tf_op jit(solution)/shard_map/slice | solution.py:18
  43.7 3.1 %collective-permute-start.4 = (bf16[104,104,32]{1,2,0:T(8,128)(2,1)}, bf16[104,104,32]{1,2,0:T(8,128)(2,1)}, u32[]{:S(2)}, u32[]{:S(2)}) collective-permute-start(bf16[104,104,32]{1,2,0:T(8,128)(2,1)} %get-tuple-element.146), channel_id=1, source_target_pairs={{0,1},{1,2},{2,3},{3,4},{4,5},{5,6},{6,7},{8,9},{9,10},{10,11},{11... | collective-permute-start | bytes 2076680 | tf_op jit(solution)/shard_map/ppermute | solution.py:21
  46.9 13.0 %collective-permute-start.5 = (bf16[104,104,32]{1,2,0:T(8,128)(2,1)}, bf16[104,104,32]{1,2,0:T(8,128)(2,1)}, u32[]{:S(2)}, u32[]{:S(2)}) collective-permute-start(bf16[104,104,32]{1,2,0:T(8,128)(2,1)} %get-tuple-element.147), channel_id=1, source_target_pairs={{1,0},{2,1},{3,2},{4,3},{5,4},{6,5},{7,6},{9,8},{10,9},{11,10},{12... | collective-permute-start | bytes 2076680 | tf_op jit(solution)/shard_map/ppermute | solution.py:23
  59.9 14.1 %all-gather = bf16[8,4,1536]{2,1,0:T(4,128)(2,1)S(1)} all-gather(bf16[1,4,1536]{2,1,0:T(4,128)(2,1)S(1)} %bitcast.143), channel_id=1, replica_groups=mesh['il'=8,'xl'=8,'gz'=8] {'xl'}, dimensions={0}, use_global_device_ids=true | all-gather | bytes 110592 | tf_op jit(solution)/shard_map/all_gather | solution.py:81
  74.0 0.7 reshape.79
  74.6 0.7 fusion.67
  75.3 1.1 convolution_convert_fusion.8
  76.4 54.8 %collective-permute-done.4 = bf16[104,104,32]{1,2,0:T(8,128)(2,1)} collective-permute-done((bf16[104,104,32]{1,2,0:T(8,128)(2,1)}, bf16[104,104,32]{1,2,0:T(8,128)(2,1)}, u32[]{:S(2)}, u32[]{:S(2)}) %collective-permute-start.4) | collective-permute-done | bytes 692256 | tf_op jit(solution)/shard_map/ppermute | solution.py:21
  131.2 1.0 collective-permute-done.5
  132.3 6.1 %pad_maximum_fusion = bf16[104,104,192]{1,2,0:T(8,128)(2,1)S(1)} fusion(bf16[104,104,32]{1,2,0:T(8,128)(2,1)} %collective-permute-done.5, bf16[104,32,128]{1,2,0:T(8,128)(2,1)} %copy.29, bf16[104,40,128]{1,2,0:T(8,128)(2,1)S(1)} %copy.28, bf16[104,32,128]{1,2,0:T(8,128)(2,1)} %copy.27, bf16[104,104,32]{1,2,0:T(8,128)(2,1)} %collective-permute-done.4), kind=kLoop, calls=%fused_computation.46 | loop fusion | flops 20766720 | bytes 8306688 | tf_op jit(solution)/shard_map/concatenate | solution.py:19
  138.4 5.6 %copy.30 = bf16[104,104,192]{1,0,2:T(8,128)(2,1)} copy(bf16[104,104,192]{1,2,0:T(8,128)(2,1)S(1)} %pad_maximum_fusion) | data formatting | bytes 8306688
  144.0 0.9 broadcast_in_dim.13
  144.9 130.7 %while.12 = (s32[]{:T(128)}, f32[40,40,128]{2,1,0:T(8,128)}, s32[]{:T(128)}, s32[2,40,40,128]{3,2,1,0:T(8,128)}, bf16[2,40,40,128]{3,2,1,0:T(8,128)(2,1)}, /*ind...) while((s32[]{:T(128)}, f32[40,40,128]{2,1,0:T(8,128)}, ...), condition=%wide.region_3.4_spmd.clone.clone, body=%wide.region_1.3_spmd.sunk.clone.clone.sunk | while | flops 2514240512 | bytes 64824612 | solution.py:97
  145.9 1.3 fusion.123
  147.2 7.8 %convolution_convert_fusion.15 = bf16[4,40,104,192]{2,1,3,0:T(8,128)(2,1)} fusion(bf16[104,104,192]{1,0,2:T(8,128)(2,1)} %get-tuple-element.246, bf16[4,40,104,1]{2,0,1,3:T(4,128)(2,1)S(1)} %fusion.123), kind=kOutput, calls=%fused_computation.5.clone.1 | convolution fusion | flops 667729920 | bytes 10576384 | tf_op jit(solution)/shard_map/while/body/roi,iyz->royz/dot_general | solution.py:47
  155.0 0.2 convolution_convert_fusion.17
  155.2 0.5 convolution_convert_fusion.16
  155.7 10.0 %fusion.124 = f32[40,40,128]{2,1,0:T(8,128)} fusion(bf16[4,40,104,192]{2,1,3,0:T(8,128)(2,1)} %convolution_convert_fusion.15, bf16[4,128,192]{1,0,2:T(4,128)(2,1)S(1)} %convolution_convert_fusion.16, bf16[4,40,104]{2,0,1:T(4,128)(2,1)S(1)} %convolution_convert_fusion.17), kind=kOutput, calls=%fused_computation.15.clone.1 | convolution fusion | flops 571392000 | bytes 7438848 | tf_op jit(solution)/shard_map/while/body/roi,rxyi->xyo/dot_general | solution.py:59
  165.8 1.3 fusion.126
  167.1 7.8 %convolution_convert_fusion.18 = bf16[4,40,104,192]{2,1,3,0:T(8,128)(2,1)} fusion(bf16[104,104,192]{1,0,2:T(8,128)(2,1)} %get-tuple-element.246, bf16[4,40,104,1]{2,0,1,3:T(4,128)(2,1)S(1)} %fusion.126), kind=kOutput, calls=%fused_computation.4.clone.1 | convolution fusion | flops 667729920 | bytes 10576384 | tf_op jit(solution)/shard_map/while/body/roi,iyz->royz/dot_general | solution.py:47
  174.9 0.2 convolution_convert_fusion.20
  175.1 0.5 convolution_convert_fusion.19
  175.6 0.7 copy-done.3
  176.3 0.2 copy-done.4
  176.5 1.1 select_reduce_fusion.2
  177.7 10.6 %fusion.127 = f32[40,40,128]{2,1,0:T(8,128)} fusion(f32[40,40,128]{2,1,0:T(8,128)} %get-tuple-element.228, f32[40,40,128]{2,1,0:T(8,128)} %select_reduce_fusion.2, f32[40,40,128]{2,1,0:T(8,128)} %fusion.124, bf16[4,40,104,192]{2,1,3,0:T(8,128)(2,1)} %convolution_convert_fusion.18, bf16[4,128,192]{1,0,2:T(4,128)(2,1)S(1)} %convolution_convert_fusion.19, ...), kind=kOutput, calls=%fused_computation.19.clone.1 | convolution fusion | flops 572006400 | bytes 9896448 | tf_op jit(solution)/shard_map/while/body/roi,rxyi->xyo/dot_general | solution.py:59
  189.1 1.3 fusion.123
  190.4 7.8 %convolution_convert_fusion.15 = bf16[4,40,104,192]{2,1,3,0:T(8,128)(2,1)} fusion(bf16[104,104,192]{1,0,2:T(8,128)(2,1)} %get-tuple-element.246, bf16[4,40,104,1]{2,0,1,3:T(4,128)(2,1)S(1)} %fusion.123), kind=kOutput, calls=%fused_computation.5.clone.1 | convolution fusion | flops 667729920 | bytes 10576384 | tf_op jit(solution)/shard_map/while/body/roi,iyz->royz/dot_general | solution.py:47
  198.2 0.2 convolution_convert_fusion.17
  198.4 0.5 convolution_convert_fusion.16
  198.9 10.0 %fusion.124 = f32[40,40,128]{2,1,0:T(8,128)} fusion(bf16[4,40,104,192]{2,1,3,0:T(8,128)(2,1)} %convolution_convert_fusion.15, bf16[4,128,192]{1,0,2:T(4,128)(2,1)S(1)} %convolution_convert_fusion.16, bf16[4,40,104]{2,0,1:T(4,128)(2,1)S(1)} %convolution_convert_fusion.17), kind=kOutput, calls=%fused_computation.15.clone.1 | convolution fusion | flops 571392000 | bytes 7438848 | tf_op jit(solution)/shard_map/while/body/roi,rxyi->xyo/dot_general | solution.py:59
  209.0 1.3 fusion.126
  210.3 7.8 %convolution_convert_fusion.18 = bf16[4,40,104,192]{2,1,3,0:T(8,128)(2,1)} fusion(bf16[104,104,192]{1,0,2:T(8,128)(2,1)} %get-tuple-element.246, bf16[4,40,104,1]{2,0,1,3:T(4,128)(2,1)S(1)} %fusion.126), kind=kOutput, calls=%fused_computation.4.clone.1 | convolution fusion | flops 667729920 | bytes 10576384 | tf_op jit(solution)/shard_map/while/body/roi,iyz->royz/dot_general | solution.py:47
  218.1 0.2 convolution_convert_fusion.20
  218.3 0.5 convolution_convert_fusion.19
  218.8 0.7 copy-done.3
  219.5 0.2 copy-done.4
  219.8 1.1 select_reduce_fusion.2
  220.9 10.6 %fusion.127 = f32[40,40,128]{2,1,0:T(8,128)} fusion(f32[40,40,128]{2,1,0:T(8,128)} %get-tuple-element.228, f32[40,40,128]{2,1,0:T(8,128)} %select_reduce_fusion.2, f32[40,40,128]{2,1,0:T(8,128)} %fusion.124, bf16[4,40,104,192]{2,1,3,0:T(8,128)(2,1)} %convolution_convert_fusion.18, bf16[4,128,192]{1,0,2:T(4,128)(2,1)S(1)} %convolution_convert_fusion.19, ...), kind=kOutput, calls=%fused_computation.19.clone.1 | convolution fusion | flops 572006400 | bytes 9896448 | tf_op jit(solution)/shard_map/while/body/roi,rxyi->xyo/dot_general | solution.py:59
  232.4 1.3 fusion.123
  233.7 7.8 %convolution_convert_fusion.15 = bf16[4,40,104,192]{2,1,3,0:T(8,128)(2,1)} fusion(bf16[104,104,192]{1,0,2:T(8,128)(2,1)} %get-tuple-element.246, bf16[4,40,104,1]{2,0,1,3:T(4,128)(2,1)S(1)} %fusion.123), kind=kOutput, calls=%fused_computation.5.clone.1 | convolution fusion | flops 667729920 | bytes 10576384 | tf_op jit(solution)/shard_map/while/body/roi,iyz->royz/dot_general | solution.py:47
  241.4 0.2 convolution_convert_fusion.17
  241.6 0.5 convolution_convert_fusion.16
  242.2 10.0 %fusion.124 = f32[40,40,128]{2,1,0:T(8,128)} fusion(bf16[4,40,104,192]{2,1,3,0:T(8,128)(2,1)} %convolution_convert_fusion.15, bf16[4,128,192]{1,0,2:T(4,128)(2,1)S(1)} %convolution_convert_fusion.16, bf16[4,40,104]{2,0,1:T(4,128)(2,1)S(1)} %convolution_convert_fusion.17), kind=kOutput, calls=%fused_computation.15.clone.1 | convolution fusion | flops 571392000 | bytes 7438848 | tf_op jit(solution)/shard_map/while/body/roi,rxyi->xyo/dot_general | solution.py:59
  252.3 1.3 fusion.126
  253.6 7.8 %convolution_convert_fusion.18 = bf16[4,40,104,192]{2,1,3,0:T(8,128)(2,1)} fusion(bf16[104,104,192]{1,0,2:T(8,128)(2,1)} %get-tuple-element.246, bf16[4,40,104,1]{2,0,1,3:T(4,128)(2,1)S(1)} %fusion.126), kind=kOutput, calls=%fused_computation.4.clone.1 | convolution fusion | flops 667729920 | bytes 10576384 | tf_op jit(solution)/shard_map/while/body/roi,iyz->royz/dot_general | solution.py:47
  261.6 0.5 convolution_convert_fusion.19
  262.1 0.7 copy-done.3
  262.8 0.2 copy-done.4
  263.0 1.1 select_reduce_fusion.2
  264.1 10.6 %fusion.127 = f32[40,40,128]{2,1,0:T(8,128)} fusion(f32[40,40,128]{2,1,0:T(8,128)} %get-tuple-element.228, f32[40,40,128]{2,1,0:T(8,128)} %select_reduce_fusion.2, f32[40,40,128]{2,1,0:T(8,128)} %fusion.124, bf16[4,40,104,192]{2,1,3,0:T(8,128)(2,1)} %convolution_convert_fusion.18, bf16[4,128,192]{1,0,2:T(4,128)(2,1)S(1)} %convolution_convert_fusion.19, ...), kind=kOutput, calls=%fused_computation.19.clone.1 | convolution fusion | flops 572006400 | bytes 9896448 | tf_op jit(solution)/shard_map/while/body/roi,rxyi->xyo/dot_general | solution.py:59
  (45 shorter events, 1.3 us)
Async XLA Ops:
  1.3 10.5 %collective-permute-start = (bf16[32,40,128]{2,1,0:T(8,128)(2,1)S(1)}, bf16[32,40,128]{2,1,0:T(8,128)(2,1)S(1)}, u32[]{:S(2)}, u32[]{:S(2)}) collective-permute-start(bf16[32,40,128]{2,1,0:T(8,128)(2,1)S(1)} %get-tuple-element.150), channel_id=1, source_target_pairs={{0,64},{64,128},{128,192},{192,256},{256,320},{320,384},{384,448},... | collective-permute-start | bytes 983048 | tf_op jit(solution)/shard_map/ppermute | solution.py:21
  3.9 10.2 %collective-permute-start.1 = (bf16[32,40,128]{2,1,0:T(8,128)(2,1)S(1)}, bf16[32,40,128]{2,1,0:T(8,128)(2,1)S(1)}, u32[]{:S(2)}, u32[]{:S(2)}) collective-permute-start(bf16[32,40,128]{2,1,0:T(8,128)(2,1)S(1)} %get-tuple-element.151), channel_id=1, source_target_pairs={{64,0},{128,64},{192,128},{256,192},{320,256},{384,320},{448,384},... | collective-permute-start | bytes 983048 | tf_op jit(solution)/shard_map/ppermute | solution.py:23
  14.2 6.5 %copy-start.5 = (bf16[104,40,128]{2,1,0:T(8,128)(2,1)}, bf16[104,40,128]{2,1,0:T(8,128)(2,1)S(1)}, u32[]{:S(2)}) copy-start(bf16[104,40,128]{2,1,0:T(8,128)(2,1)S(1)} %pad_maximum_fusion.1) | copy-start | bytes 3194884
  15.8 14.9 %collective-permute-start.2 = (bf16[104,32,128]{2,1,0:T(8,128)(2,1)}, bf16[104,32,128]{2,1,0:T(8,128)(2,1)}, u32[]{:S(2)}, u32[]{:S(2)}) collective-permute-start(bf16[104,32,128]{2,1,0:T(8,128)(2,1)} %get-tuple-element.148), channel_id=1, source_target_pairs={{0,8},{8,16},{16,24},{24,32},{32,40},{40,48},{48,56},{1,9},{9,17},... | collective-permute-start | bytes 2555912 | tf_op jit(solution)/shard_map/ppermute | solution.py:21
  20.7 14.3 %collective-permute-start.3 = (bf16[104,32,128]{2,1,0:T(8,128)(2,1)}, bf16[104,32,128]{2,1,0:T(8,128)(2,1)}, u32[]{:S(2)}, u32[]{:S(2)}) collective-permute-start(bf16[104,32,128]{2,1,0:T(8,128)(2,1)} %get-tuple-element.149), channel_id=1, source_target_pairs={{8,0},{16,8},{24,16},{32,24},{40,32},{48,40},{56,48},{9,1},{17,9},... | collective-permute-start | bytes 2555912 | tf_op jit(solution)/shard_map/ppermute | solution.py:23
  39.0 20.9 %copy-start.6 = (bf16[4,1536]{1,0:T(4,128)(2,1)S(1)}, bf16[4,1536]{1,0:T(4,128)(2,1)}, u32[]{:S(2)}) copy-start(bf16[4,1536]{1,0:T(4,128)(2,1)} %param.13) | copy-start | bytes 36868
  39.0 35.7 %copy-start.7 = (s32[1,1,1,3]{3,2,1,0:T(1,128)S(1)}, s32[1,1,1,3]{3,2,1,0:T(1,128)}, u32[]{:S(2)}) copy-start(s32[1,1,1,3]{3,2,1,0:T(1,128)} %param.14) | copy-start | bytes 40
  43.7 87.5 %collective-permute-start.4 = (bf16[104,104,32]{1,2,0:T(8,128)(2,1)}, bf16[104,104,32]{1,2,0:T(8,128)(2,1)}, u32[]{:S(2)}, u32[]{:S(2)}) collective-permute-start(bf16[104,104,32]{1,2,0:T(8,128)(2,1)} %get-tuple-element.146), channel_id=1, source_target_pairs={{0,1},{1,2},{2,3},{3,4},{4,5},{5,6},{6,7},{8,9},{9,10},{10,11},{11... | collective-permute-start | bytes 2076680 | tf_op jit(solution)/shard_map/ppermute | solution.py:21
  46.9 85.4 %collective-permute-start.5 = (bf16[104,104,32]{1,2,0:T(8,128)(2,1)}, bf16[104,104,32]{1,2,0:T(8,128)(2,1)}, u32[]{:S(2)}, u32[]{:S(2)}) collective-permute-start(bf16[104,104,32]{1,2,0:T(8,128)(2,1)} %get-tuple-element.147), channel_id=1, source_target_pairs={{1,0},{2,1},{3,2},{4,3},{5,4},{6,5},{7,6},{9,8},{10,9},{11,10},{12... | collective-permute-start | bytes 2076680 | tf_op jit(solution)/shard_map/ppermute | solution.py:23
  138.4 6.5 %copy-start = (bf16[64,128,192]{1,0,2:T(8,128)(2,1)S(1)}, bf16[64,128,192]{1,0,2:T(8,128)(2,1)}, u32[]{:S(2)}) copy-start(bf16[64,128,192]{1,0,2:T(8,128)(2,1)} %constant.61.clone..sunk.3) | copy-start | bytes 9437188
  147.2 7.8 %copy-start.1 = (bf16[64,40,104]{2,0,1:T(8,128)(2,1)S(1)}, bf16[64,40,104]{2,0,1:T(8,128)(2,1)}, u32[]{:S(2)}) copy-start(bf16[64,40,104]{2,0,1:T(8,128)(2,1)} %get-tuple-element.248) | copy-start | bytes 1597444 | tf_op jit(solution)/shard_map/while
  167.1 7.8 %copy-start.2 = (bf16[64,40,104]{2,0,1:T(8,128)(2,1)S(1)}, bf16[64,40,104]{2,0,1:T(8,128)(2,1)}, u32[]{:S(2)}) copy-start(bf16[64,40,104]{2,0,1:T(8,128)(2,1)} %get-tuple-element.248) | copy-start | bytes 1597444 | tf_op jit(solution)/shard_map/while
  174.9 1.4 copy-start.3
  174.9 1.6 copy-start.4
  190.4 7.8 %copy-start.1 = (bf16[64,40,104]{2,0,1:T(8,128)(2,1)S(1)}, bf16[64,40,104]{2,0,1:T(8,128)(2,1)}, u32[]{:S(2)}) copy-start(bf16[64,40,104]{2,0,1:T(8,128)(2,1)} %get-tuple-element.248) | copy-start | bytes 1597444 | tf_op jit(solution)/shard_map/while
  210.3 7.8 %copy-start.2 = (bf16[64,40,104]{2,0,1:T(8,128)(2,1)S(1)}, bf16[64,40,104]{2,0,1:T(8,128)(2,1)}, u32[]{:S(2)}) copy-start(bf16[64,40,104]{2,0,1:T(8,128)(2,1)} %get-tuple-element.248) | copy-start | bytes 1597444 | tf_op jit(solution)/shard_map/while
  218.1 1.4 copy-start.3
  218.1 1.6 copy-start.4
  233.6 7.8 %copy-start.1 = (bf16[64,40,104]{2,0,1:T(8,128)(2,1)S(1)}, bf16[64,40,104]{2,0,1:T(8,128)(2,1)}, u32[]{:S(2)}) copy-start(bf16[64,40,104]{2,0,1:T(8,128)(2,1)} %get-tuple-element.248) | copy-start | bytes 1597444 | tf_op jit(solution)/shard_map/while
  253.6 7.8 %copy-start.2 = (bf16[64,40,104]{2,0,1:T(8,128)(2,1)S(1)}, bf16[64,40,104]{2,0,1:T(8,128)(2,1)}, u32[]{:S(2)}) copy-start(bf16[64,40,104]{2,0,1:T(8,128)(2,1)} %get-tuple-element.248) | copy-start | bytes 1597444 | tf_op jit(solution)/shard_map/while
  261.3 1.4 copy-start.3
  261.3 1.6 copy-start.4
where the time goes:
time: 281 us; the launch traced here: 276 us
  matrix products  122 us (43%)
  waiting for transfers between devices  68.2 us (24%)
  starting transfers between devices  28.3 us (10%)
  local copies, waits for them, and re-layouts  23.8 us (8%)
  other arithmetic  16.3 us (6%)
  blocking collectives  14.1 us (5%)
  loops' own time  3.05 us (1%)
    ppermute x3, waiting for transfers between devices, padded(): lax.ppermute(tail, axis, [(i, (i + 1) % count) for i in range(ends)])  64.3 us
    dot_general x6, matrix products, blur_slot(): jnp.einsum('roi,rxyi->xyo', banded(chosen[:, 2], tables[2]), line_y, pref...  61.8 us
    dot_general x6, matrix products, blur_slot(): jnp.einsum('roi,iyz->royz', banded(chosen[:, 0], tables[0]), extended, pr...  46.7 us
    ppermute x3, starting transfers between devices, padded(): lax.ppermute(head, axis, [((i + 1) % count, i) for i in range(ends)])  17.6 us
    all_gather x1, blocking collectives, per_device(): panel_table = lax.all_gather(factors, 'xl', axis=0, tiled=True)  14.1 us
    dot_general x18, matrix products, banded(): jnp.einsum('rt,toi->roi', filters, table, preferred_element_type=jnp.floa...  12 us
    ppermute x3, starting transfers between devices, padded(): lax.ppermute(tail, axis, [(i, (i + 1) % count) for i in range(ends)])  10.7 us
    unnamed x10, local copies, waits for them, and re-layouts  6.24 us
  transfers between devices with their start and end apart: 6, of which 6 were waited for; matrix products, arithmetic and copies ran while one was open for 4% of the time, Pallas kernels for 0%

commit v1 on v0

--- a/solution.py
+++ b/solution.py
@@ -25,6 +25,20 @@
             axis=dim,
         )
     return cells
+
+
+def gathered(rows, axis):
+    count = lax.axis_size(axis)
+    position = lax.axis_index(axis)
+    bit = 1
+    while bit < count:
+        other = lax.ppermute(rows, axis, [(i, i ^ bit) for i in range(count)])
+        upper = (position & bit) != 0
+        rows = jnp.concatenate(
+            [jnp.where(upper, other, rows), jnp.where(upper, rows, other)], axis=0
+        )
+        bit *= 2
+    return rows
 
 
 def shift_table(length, tap_count):
@@ -69,7 +83,7 @@
     half_width = K // 2
     size_x, size_y, size_z = reflect.shape
     rounded = reflect.astype(jnp.bfloat16)
-    extended = padded(rounded, (("il", 0), ("xl", 1), ("gz", 2)), half_width)
+    extended = padded(rounded, (("gz", 2), ("il", 0), ("xl", 1)), half_width)
     tables = (shift_table(size_x, K), shift_table(size_y, K), shift_table(size_z, K))
     listed = reader_list.reshape(NEED)
     live_mask = listed >= 0
@@ -78,7 +92,7 @@
     depth_count = lax.axis_size("gz")
     owner_index = jnp.where(live_mask, listed // (CP_DEV * depth_count) % cross_count, 0)
     local_row = jnp.where(live_mask, listed % CP_DEV, 0)
-    panel_table = lax.all_gather(factors, "xl", axis=0, tiled=True)
+    panel_table = gathered(factors, "xl")
     row_key = owner_index * CP_DEV + local_row
     row_pick = (jnp.arange(cross_count * CP_DEV)[None, :] == row_key[:, None]) & live_mask[:, None]
     panels = jnp.dot(

time: 281 us -> 283 us (level)
  the two profiles are of different devices: /device:TPU:297 before, /device:TPU:23 now
where the time goes in v1:
time: 283 us; the launch traced here: 282 us
  matrix products  126 us (45%)
  starting transfers between devices  62.6 us (22%)
  waiting for transfers between devices  44.6 us (16%)
  local copies, waits for them, and re-layouts  24.2 us (9%)
  other arithmetic  20.9 us (7%)
  loops' own time  3.05 us (1%)
    dot_general x6, matrix products, blur_slot(): jnp.einsum('roi,rxyi->xyo', banded(chosen[:, 2], tables[2]), line_y, pref...  61.7 us
    ppermute x3, starting transfers between devices, padded(): lax.ppermute(tail, axis, [(i, (i + 1) % count) for i in range(ends)])  49.6 us
    dot_general x6, matrix products, blur_slot(): jnp.einsum('roi,iyz->royz', banded(chosen[:, 0], tables[0]), extended, pr...  38.9 us
    ppermute x3, waiting for transfers between devices, padded(): lax.ppermute(head, axis, [((i + 1) % count, i) for i in range(ends)])  26.2 us
    dot_general x18, matrix products, banded(): jnp.einsum('rt,toi->roi', filters, table, preferred_element_type=jnp.floa...  24.6 us
    ppermute x3, waiting for transfers between devices, gathered(): other = lax.ppermute(rows, axis, [(i, i ^ bit) for i in range(count)])  12.7 us
    concatenate x3, other arithmetic, padded(): jnp.concatenate([lax.ppermute(tail, axis, [(i, (i + 1) % count) for i in...  11.6 us
    unnamed x15, local copies, waits for them, and re-layouts  8.94 us
  transfers between devices with their start and end apart: 9, of which 5 were waited for; matrix products, arithmetic and copies ran while one was open for 8% of the time, Pallas kernels for 0%

profile of v1, /device:TPU:23, one launch (start us, length us, event | category | flops | bytes accessed | tf_op | source)
XLA Modules:
  0.0 281.8 jit_solution(17091111143734313770)
XLA Ops:
  0.0 2.7 collective-permute-start
  2.7 1.2 convert_element_type.51
  4.1 15.4 %collective-permute-start.3 = (bf16[40,40,32]{2,1,0:T(8,128)(2,1)S(1)}, bf16[40,40,32]{2,1,0:T(8,128)(2,1)S(1)}, u32[]{:S(2)}, u32[]{:S(2)}) collective-permute-start(bf16[40,40,32]{2,1,0:T(8,128)(2,1)S(1)} %get-tuple-element.150), channel_id=1, source_target_pairs={{0,1},{1,2},{2,3},{3,4},{4,5},{5,6},{6,7},{8,9},{9,10},{10,11},{11... | collective-permute-start | bytes 307208 | tf_op jit(solution)/shard_map/ppermute | solution.py:21
  19.5 1.9 collective-permute-start.4
  21.4 1.2 bitcast_compare_fusion
  22.6 5.8 %collective-permute-done.3 = bf16[40,40,32]{2,1,0:T(8,128)(2,1)S(1)} collective-permute-done((bf16[40,40,32]{2,1,0:T(8,128)(2,1)S(1)}, bf16[40,40,32]{2,1,0:T(8,128)(2,1)S(1)}, u32[]{:S(2)}, u32[]{:S(2)}) %collective-permute-start.3) | collective-permute-done | bytes 102432 | tf_op jit(solution)/shard_map/ppermute | solution.py:21
  28.3 14.7 %collective-permute-done.4 = bf16[40,40,32]{2,1,0:T(8,128)(2,1)S(1)} collective-permute-done((bf16[40,40,32]{2,1,0:T(8,128)(2,1)S(1)}, bf16[40,40,32]{2,1,0:T(8,128)(2,1)S(1)}, u32[]{:S(2)}, u32[]{:S(2)}) %collective-permute-start.4) | collective-permute-done | bytes 102432 | tf_op jit(solution)/shard_map/ppermute | solution.py:23
  43.5 1.1 fusion.76
  44.6 29.0 %collective-permute-start.5 = (bf16[32,40,192]{2,1,0:T(8,128)(2,1)}, bf16[32,40,192]{2,1,0:T(8,128)(2,1)S(1)}, u32[]{:S(2)}, u32[]{:S(2)}) collective-permute-start(bf16[32,40,192]{2,1,0:T(8,128)(2,1)} %get-tuple-element.148), channel_id=1, source_target_pairs={{0,64},{64,128},{128,192},{192,256},{256,320},{320,384},{384,448},... | collective-permute-start | bytes 1474568 | tf_op jit(solution)/shard_map/ppermute | solution.py:21
  73.6 1.3 collective-permute-start.6
  75.0 0.6 pad_maximum_fusion.4
  75.6 2.9 %collective-permute-start.1 = (bf16[8,1536]{1,0:T(8,128)(2,1)}, bf16[8,1536]{1,0:T(8,128)(2,1)}, u32[]{:S(2)}, u32[]{:S(2)}) collective-permute-start(bf16[8,1536]{1,0:T(8,128)(2,1)} %pad_maximum_fusion.4), channel_id=1, source_target_pairs={{0,16},{8,24},{16,0},{24,8},{32,48},{40,56},{48,32},{56,40},{1,17}... | collective-permute-start | bytes 73736 | tf_op jit(solution)/shard_map/ppermute | solution.py:35
  78.5 1.8 copy.28
  80.3 10.2 %collective-permute-done.6 = bf16[32,40,192]{2,1,0:T(8,128)(2,1)} collective-permute-done((bf16[32,40,192]{2,1,0:T(8,128)(2,1)}, bf16[32,40,192]{2,1,0:T(8,128)(2,1)}, u32[]{:S(2)}, u32[]{:S(2)}) %collective-permute-start.6) | collective-permute-done | bytes 491552 | tf_op jit(solution)/shard_map/ppermute | solution.py:23
  90.5 2.8 copy.29
  93.3 1.9 copy.27
  95.2 3.9 %pad_maximum_fusion.1 = bf16[104,40,192]{0,2,1:T(8,128)(2,1)S(1)} fusion(bf16[32,40,192]{0,2,1:T(8,128)(2,1)} %copy.29, bf16[40,40,192]{0,2,1:T(8,128)(2,1)S(1)} %copy.28, bf16[32,40,192]{0,2,1:T(8,128)(2,1)} %copy.27), kind=kLoop, calls=%fused_computation.48 | loop fusion | flops 4792320 | bytes 3194880 | tf_op jit(solution)/shard_map/concatenate | solution.py:19
  99.1 2.3 fusion.75
  101.4 5.3 %collective-permute-start.7 = (bf16[104,32,192]{0,2,1:T(8,128)(2,1)}, bf16[104,32,192]{0,2,1:T(8,128)(2,1)S(1)}, u32[]{:S(2)}, u32[]{:S(2)}) collective-permute-start(bf16[104,32,192]{0,2,1:T(8,128)(2,1)} %get-tuple-element.146), channel_id=1, source_target_pairs={{0,8},{8,16},{16,24},{24,32},{32,40},{40,48},{48,56},{1,9},{9,17},... | collective-permute-start | bytes 3833864 | tf_op jit(solution)/shard_map/ppermute | solution.py:21
  106.7 1.9 collective-permute-start.8
  108.7 0.8 broadcast_select_fusion.3
  109.4 0.6 copy-done.5
  110.0 0.6 pad_maximum_fusion.3
  110.7 2.2 collective-permute-start.2
  112.9 0.7 fusion.70
  113.6 12.7 %collective-permute-done.2 = bf16[16,1536]{1,0:T(8,128)(2,1)} collective-permute-done((bf16[16,1536]{1,0:T(8,128)(2,1)}, bf16[16,1536]{1,0:T(8,128)(2,1)}, u32[]{:S(2)}, u32[]{:S(2)}) %collective-permute-start.2) | collective-permute-done | bytes 49184 | tf_op jit(solution)/shard_map/ppermute | solution.py:35
  126.3 0.8 broadcast_select_fusion.1
  127.2 0.8 convolution_convert_fusion.8
  128.0 1.3 collective-permute-done.8
  129.3 7.2 %pad_maximum_fusion = bf16[104,104,192]{0,2,1:T(8,128)(2,1)} fusion(bf16[104,32,192]{0,2,1:T(8,128)(2,1)} %collective-permute-done.8, bf16[32,40,192]{0,2,1:T(8,128)(2,1)} %copy.29, bf16[40,40,192]{0,2,1:T(8,128)(2,1)S(1)} %copy.28, bf16[32,40,192]{0,2,1:T(8,128)(2,1)} %copy.27, bf16[104,32,192]{0,2,1:T(8,128)(2,1)S(1)} %collective-permute-done.7), kind=kLoop, calls=%fused_computation.46 | loop fusion | flops 20766720 | bytes 8306688 | tf_op jit(solution)/shard_map/concatenate | solution.py:19
  136.5 8.3 %copy.30 = bf16[104,104,192]{1,0,2:T(8,128)(2,1)} copy(bf16[104,104,192]{0,2,1:T(8,128)(2,1)} %pad_maximum_fusion) | data formatting | bytes 8306688
  144.8 0.9 broadcast_in_dim.13
  145.8 135.8 %while.12 = (s32[]{:T(128)}, f32[40,40,128]{2,1,0:T(8,128)}, s32[]{:T(128)}, s32[2,40,40,128]{3,2,1,0:T(8,128)}, bf16[2,40,40,128]{3,2,1,0:T(8,128)(2,1)}, /*ind...) while((s32[]{:T(128)}, f32[40,40,128]{2,1,0:T(8,128)}, ...), condition=%wide.region_3.4_spmd.clone.clone, body=%wide.region_1.3_spmd.sunk.clone.clone.sunk | while | flops 2514240512 | bytes 77311272 | solution.py:111
  146.9 1.9 fusion.130
  148.8 1.3 fusion.127
  150.1 2.0 convolution_convert_fusion.20
  152.1 1.9 convolution_convert_fusion.17
  154.6 0.5 convolution_convert_fusion.16
  155.1 1.1 select_reduce_fusion.2
  156.2 1.1 copy-done
  157.3 5.2 %convolution_convert_fusion.15 = bf16[4,40,104,192]{2,1,3,0:T(8,128)(2,1)} fusion(bf16[104,104,192]{1,0,2:T(8,128)(2,1)S(1)} %copy-done, bf16[4,40,104,1]{2,0,1,3:T(4,128)(2,1)S(1)} %fusion.127), kind=kOutput, calls=%fused_computation.5.clone.1 | convolution fusion | flops 667729920 | bytes 10576384 | tf_op jit(solution)/shard_map/while/body/roi,iyz->royz/dot_general | solution.py:61
  162.6 10.0 %fusion.128 = f32[40,40,128]{2,1,0:T(8,128)} fusion(bf16[4,40,104,192]{2,1,3,0:T(8,128)(2,1)} %convolution_convert_fusion.15, bf16[4,128,192]{1,0,2:T(4,128)(2,1)S(1)} %convolution_convert_fusion.16, bf16[4,40,104]{2,0,1:T(4,128)(2,1)} %convolution_convert_fusion.17), kind=kOutput, calls=%fused_computation.15.clone.1 | convolution fusion | flops 571392000 | bytes 7438848 | tf_op jit(solution)/shard_map/while/body/roi,rxyi->xyo/dot_general | solution.py:73
  172.5 7.7 %convolution_convert_fusion.18 = bf16[4,40,104,192]{2,1,3,0:T(8,128)(2,1)} fusion(bf16[104,104,192]{1,0,2:T(8,128)(2,1)} %get-tuple-element.252, bf16[4,40,104,1]{2,0,1,3:T(4,128)(2,1)} %fusion.130), kind=kOutput, calls=%fused_computation.4.clone.1 | convolution fusion | flops 667729920 | bytes 10576384 | tf_op jit(solution)/shard_map/while/body/roi,iyz->royz/dot_general | solution.py:61
  180.3 10.6 %fusion.131 = f32[40,40,128]{2,1,0:T(8,128)} fusion(f32[40,40,128]{2,1,0:T(8,128)} %get-tuple-element.234, f32[40,40,128]{2,1,0:T(8,128)} %select_reduce_fusion.2, f32[40,40,128]{2,1,0:T(8,128)} %fusion.128, bf16[4,40,104,192]{2,1,3,0:T(8,128)(2,1)} %convolution_convert_fusion.18, bf16[4,128,192]{1,0,2:T(4,128)(2,1)S(1)} %convolution_convert_fusion.19, ...), kind=kOutput, calls=%fused_computation.19.clone.1 | convolution fusion | flops 572006400 | bytes 9896448 | tf_op jit(solution)/shard_map/while/body/roi,rxyi->xyo/dot_general | solution.py:73
  191.8 1.9 fusion.130
  193.7 1.3 fusion.127
  195.0 2.0 convolution_convert_fusion.20
  197.1 1.9 convolution_convert_fusion.17
  200.0 1.1 select_reduce_fusion.2
  201.2 1.1 copy-done
  202.3 5.2 %convolution_convert_fusion.15 = bf16[4,40,104,192]{2,1,3,0:T(8,128)(2,1)} fusion(bf16[104,104,192]{1,0,2:T(8,128)(2,1)S(1)} %copy-done, bf16[4,40,104,1]{2,0,1,3:T(4,128)(2,1)S(1)} %fusion.127), kind=kOutput, calls=%fused_computation.5.clone.1 | convolution fusion | flops 667729920 | bytes 10576384 | tf_op jit(solution)/shard_map/while/body/roi,iyz->royz/dot_general | solution.py:61
  207.5 10.0 %fusion.128 = f32[40,40,128]{2,1,0:T(8,128)} fusion(bf16[4,40,104,192]{2,1,3,0:T(8,128)(2,1)} %convolution_convert_fusion.15, bf16[4,128,192]{1,0,2:T(4,128)(2,1)S(1)} %convolution_convert_fusion.16, bf16[4,40,104]{2,0,1:T(4,128)(2,1)} %convolution_convert_fusion.17), kind=kOutput, calls=%fused_computation.15.clone.1 | convolution fusion | flops 571392000 | bytes 7438848 | tf_op jit(solution)/shard_map/while/body/roi,rxyi->xyo/dot_general | solution.py:73
  217.5 7.7 %convolution_convert_fusion.18 = bf16[4,40,104,192]{2,1,3,0:T(8,128)(2,1)} fusion(bf16[104,104,192]{1,0,2:T(8,128)(2,1)} %get-tuple-element.252, bf16[4,40,104,1]{2,0,1,3:T(4,128)(2,1)} %fusion.130), kind=kOutput, calls=%fused_computation.4.clone.1 | convolution fusion | flops 667729920 | bytes 10576384 | tf_op jit(solution)/shard_map/while/body/roi,iyz->royz/dot_general | solution.py:61
  225.2 10.6 %fusion.131 = f32[40,40,128]{2,1,0:T(8,128)} fusion(f32[40,40,128]{2,1,0:T(8,128)} %get-tuple-element.234, f32[40,40,128]{2,1,0:T(8,128)} %select_reduce_fusion.2, f32[40,40,128]{2,1,0:T(8,128)} %fusion.128, bf16[4,40,104,192]{2,1,3,0:T(8,128)(2,1)} %convolution_convert_fusion.18, bf16[4,128,192]{1,0,2:T(4,128)(2,1)S(1)} %convolution_convert_fusion.19, ...), kind=kOutput, calls=%fused_computation.19.clone.1 | convolution fusion | flops 572006400 | bytes 9896448 | tf_op jit(solution)/shard_map/while/body/roi,rxyi->xyo/dot_general | solution.py:73
  236.8 1.9 fusion.130
  238.7 1.3 fusion.127
  240.0 2.0 convolution_convert_fusion.20
  242.0 1.9 convolution_convert_fusion.17
  245.0 1.1 select_reduce_fusion.2
  246.1 1.1 copy-done
  247.2 5.2 %convolution_convert_fusion.15 = bf16[4,40,104,192]{2,1,3,0:T(8,128)(2,1)} fusion(bf16[104,104,192]{1,0,2:T(8,128)(2,1)S(1)} %copy-done, bf16[4,40,104,1]{2,0,1,3:T(4,128)(2,1)S(1)} %fusion.127), kind=kOutput, calls=%fused_computation.5.clone.1 | convolution fusion | flops 667729920 | bytes 10576384 | tf_op jit(solution)/shard_map/while/body/roi,iyz->royz/dot_general | solution.py:61
  252.4 10.0 %fusion.128 = f32[40,40,128]{2,1,0:T(8,128)} fusion(bf16[4,40,104,192]{2,1,3,0:T(8,128)(2,1)} %convolution_convert_fusion.15, bf16[4,128,192]{1,0,2:T(4,128)(2,1)S(1)} %convolution_convert_fusion.16, bf16[4,40,104]{2,0,1:T(4,128)(2,1)} %convolution_convert_fusion.17), kind=kOutput, calls=%fused_computation.15.clone.1 | convolution fusion | flops 571392000 | bytes 7438848 | tf_op jit(solution)/shard_map/while/body/roi,rxyi->xyo/dot_general | solution.py:73
  262.4 7.7 %convolution_convert_fusion.18 = bf16[4,40,104,192]{2,1,3,0:T(8,128)(2,1)} fusion(bf16[104,104,192]{1,0,2:T(8,128)(2,1)} %get-tuple-element.252, bf16[4,40,104,1]{2,0,1,3:T(4,128)(2,1)} %fusion.130), kind=kOutput, calls=%fused_computation.4.clone.1 | convolution fusion | flops 667729920 | bytes 10576384 | tf_op jit(solution)/shard_map/while/body/roi,iyz->royz/dot_general | solution.py:61
  270.1 10.6 %fusion.131 = f32[40,40,128]{2,1,0:T(8,128)} fusion(f32[40,40,128]{2,1,0:T(8,128)} %get-tuple-element.234, f32[40,40,128]{2,1,0:T(8,128)} %select_reduce_fusion.2, f32[40,40,128]{2,1,0:T(8,128)} %fusion.128, bf16[4,40,104,192]{2,1,3,0:T(8,128)(2,1)} %convolution_convert_fusion.18, bf16[4,128,192]{1,0,2:T(4,128)(2,1)S(1)} %convolution_convert_fusion.19, ...), kind=kOutput, calls=%fused_computation.19.clone.1 | convolution fusion | flops 572006400 | bytes 9896448 | tf_op jit(solution)/shard_map/while/body/roi,rxyi->xyo/dot_general | solution.py:73
  (61 shorter events, 4.2 us)
Async XLA Ops:
  0.0 74.9 %copy-start.9 = (bf16[4,1536]{1,0:T(4,128)(2,1)S(1)}, bf16[4,1536]{1,0:T(4,128)(2,1)}, u32[]{:S(2)}) copy-start(bf16[4,1536]{1,0:T(4,128)(2,1)} %param.13) | copy-start | bytes 36868
  0.0 74.9 %collective-permute-start = (bf16[4,1536]{1,0:T(4,128)(2,1)}, bf16[4,1536]{1,0:T(4,128)(2,1)S(1)}, u32[]{:S(2)}, u32[]{:S(2)}) collective-permute-start(bf16[4,1536]{1,0:T(4,128)(2,1)} %param.13), channel_id=1, source_target_pairs={{0,8},{8,0},{16,24},{24,16},{32,40},{40,32},{48,56},{56,48},{1,9},... | collective-permute-start | bytes 36872 | tf_op jit(solution)/shard_map/ppermute | solution.py:35
  4.1 24.2 %collective-permute-start.3 = (bf16[40,40,32]{2,1,0:T(8,128)(2,1)S(1)}, bf16[40,40,32]{2,1,0:T(8,128)(2,1)S(1)}, u32[]{:S(2)}, u32[]{:S(2)}) collective-permute-start(bf16[40,40,32]{2,1,0:T(8,128)(2,1)S(1)} %get-tuple-element.150), channel_id=1, source_target_pairs={{0,1},{1,2},{2,3},{3,4},{4,5},{5,6},{6,7},{8,9},{9,10},{10,11},{11... | collective-permute-start | bytes 307208 | tf_op jit(solution)/shard_map/ppermute | solution.py:21
  19.5 23.5 %collective-permute-start.4 = (bf16[40,40,32]{2,1,0:T(8,128)(2,1)S(1)}, bf16[40,40,32]{2,1,0:T(8,128)(2,1)S(1)}, u32[]{:S(2)}, u32[]{:S(2)}) collective-permute-start(bf16[40,40,32]{2,1,0:T(8,128)(2,1)S(1)} %get-tuple-element.151), channel_id=1, source_target_pairs={{1,0},{2,1},{3,2},{4,3},{5,4},{6,5},{7,6},{9,8},{10,9},{11,10},{12... | collective-permute-start | bytes 307208 | tf_op jit(solution)/shard_map/ppermute | solution.py:23
  44.6 48.6 %collective-permute-start.5 = (bf16[32,40,192]{2,1,0:T(8,128)(2,1)}, bf16[32,40,192]{2,1,0:T(8,128)(2,1)S(1)}, u32[]{:S(2)}, u32[]{:S(2)}) collective-permute-start(bf16[32,40,192]{2,1,0:T(8,128)(2,1)} %get-tuple-element.148), channel_id=1, source_target_pairs={{0,64},{64,128},{128,192},{192,256},{256,320},{320,384},{384,448},... | collective-permute-start | bytes 1474568 | tf_op jit(solution)/shard_map/ppermute | solution.py:21
  73.6 16.9 %collective-permute-start.6 = (bf16[32,40,192]{2,1,0:T(8,128)(2,1)}, bf16[32,40,192]{2,1,0:T(8,128)(2,1)}, u32[]{:S(2)}, u32[]{:S(2)}) collective-permute-start(bf16[32,40,192]{2,1,0:T(8,128)(2,1)} %get-tuple-element.149), channel_id=1, source_target_pairs={{64,0},{128,64},{192,128},{256,192},{320,256},{384,320},{448,384},... | collective-permute-start | bytes 1474568 | tf_op jit(solution)/shard_map/ppermute | solution.py:23
  74.9 20.2 %copy-start.7 = (bf16[4,1536]{1,0:T(4,128)(2,1)}, bf16[4,1536]{1,0:T(4,128)(2,1)S(1)}, u32[]{:S(2)}) copy-start(bf16[4,1536]{1,0:T(4,128)(2,1)S(1)} %get-tuple-element.157) | copy-start | bytes 36868
  75.6 33.1 %collective-permute-start.1 = (bf16[8,1536]{1,0:T(8,128)(2,1)}, bf16[8,1536]{1,0:T(8,128)(2,1)}, u32[]{:S(2)}, u32[]{:S(2)}) collective-permute-start(bf16[8,1536]{1,0:T(8,128)(2,1)} %pad_maximum_fusion.4), channel_id=1, source_target_pairs={{0,16},{8,24},{16,0},{24,8},{32,48},{40,56},{48,32},{56,40},{1,17}... | collective-permute-start | bytes 73736 | tf_op jit(solution)/shard_map/ppermute | solution.py:35
  99.1 9.6 %copy-start.8 = (bf16[4,1536]{1,0:T(4,128)(2,1)S(1)}, bf16[4,1536]{1,0:T(4,128)(2,1)}, u32[]{:S(2)}) copy-start(bf16[4,1536]{1,0:T(4,128)(2,1)} %copy-done.7) | copy-start | bytes 36868
  99.1 13.8 %copy-start.10 = (s32[1,1,1,3]{3,2,1,0:T(1,128)S(1)}, s32[1,1,1,3]{3,2,1,0:T(1,128)}, u32[]{:S(2)}) copy-start(s32[1,1,1,3]{3,2,1,0:T(1,128)} %param.14) | copy-start | bytes 40
  101.4 26.5 %collective-permute-start.7 = (bf16[104,32,192]{0,2,1:T(8,128)(2,1)}, bf16[104,32,192]{0,2,1:T(8,128)(2,1)S(1)}, u32[]{:S(2)}, u32[]{:S(2)}) collective-permute-start(bf16[104,32,192]{0,2,1:T(8,128)(2,1)} %get-tuple-element.146), channel_id=1, source_target_pairs={{0,8},{8,16},{16,24},{24,32},{32,40},{40,48},{48,56},{1,9},{9,17},... | collective-permute-start | bytes 3833864 | tf_op jit(solution)/shard_map/ppermute | solution.py:21
  106.7 22.6 %collective-permute-start.8 = (bf16[104,32,192]{0,2,1:T(8,128)(2,1)}, bf16[104,32,192]{0,2,1:T(8,128)(2,1)}, u32[]{:S(2)}, u32[]{:S(2)}) collective-permute-start(bf16[104,32,192]{0,2,1:T(8,128)(2,1)} %get-tuple-element.147), channel_id=1, source_target_pairs={{8,0},{16,8},{24,16},{32,24},{40,32},{48,40},{56,48},{9,1},{17,9},... | collective-permute-start | bytes 3833864 | tf_op jit(solution)/shard_map/ppermute | solution.py:23
  109.4 0.6 copy-start.5
  109.4 1.2 copy-start.6
  110.7 15.6 %collective-permute-start.2 = (bf16[16,1536]{1,0:T(8,128)(2,1)}, bf16[16,1536]{1,0:T(8,128)(2,1)}, u32[]{:S(2)}, u32[]{:S(2)}) collective-permute-start(bf16[16,1536]{1,0:T(8,128)(2,1)} %pad_maximum_fusion.3), channel_id=1, source_target_pairs={{0,32},{8,40},{16,48},{24,56},{32,0},{40,8},{48,16},{56,24},{1,33}... | collective-permute-start | bytes 147464 | tf_op jit(solution)/shard_map/ppermute | solution.py:35
  136.5 9.3 %copy-start.1 = (bf16[64,128,192]{1,0,2:T(8,128)(2,1)S(1)}, bf16[64,128,192]{1,0,2:T(8,128)(2,1)}, u32[]{:S(2)}) copy-start(bf16[64,128,192]{1,0,2:T(8,128)(2,1)} %constant.69.clone..sunk.3) | copy-start | bytes 9437188
  150.1 5.0 %copy-start.2 = (s32[2,40,40,128]{3,2,1,0:T(8,128)S(1)}, s32[2,40,40,128]{3,2,1,0:T(8,128)}, u32[]{:S(2)}) copy-start(s32[2,40,40,128]{3,2,1,0:T(8,128)} %get-tuple-element.249) | copy-start | bytes 4915204 | tf_op jit(solution)/shard_map/while
  150.1 5.0 %copy-start.3 = (bf16[2,40,40,128]{3,2,1,0:T(8,128)(2,1)S(1)}, bf16[2,40,40,128]{3,2,1,0:T(8,128)(2,1)}, u32[]{:S(2)}) copy-start(bf16[2,40,40,128]{3,2,1,0:T(8,128)(2,1)} %get-tuple-element.250) | copy-start | bytes 2457604 | tf_op jit(solution)/shard_map/while
  154.6 2.8 copy-start
  172.5 7.7 %copy-start.4 = (bf16[4,40,104]{2,0,1:T(4,128)(2,1)S(1)}, bf16[4,40,104]{2,0,1:T(4,128)(2,1)}, u32[]{:S(2)}) copy-start(bf16[4,40,104]{2,0,1:T(4,128)(2,1)} %convolution_convert_fusion.20) | copy-start | bytes 99844 | tf_op jit(solution)/shard_map/while
  195.0 5.0 %copy-start.2 = (s32[2,40,40,128]{3,2,1,0:T(8,128)S(1)}, s32[2,40,40,128]{3,2,1,0:T(8,128)}, u32[]{:S(2)}) copy-start(s32[2,40,40,128]{3,2,1,0:T(8,128)} %get-tuple-element.249) | copy-start | bytes 4915204 | tf_op jit(solution)/shard_map/while
  195.0 5.0 %copy-start.3 = (bf16[2,40,40,128]{3,2,1,0:T(8,128)(2,1)S(1)}, bf16[2,40,40,128]{3,2,1,0:T(8,128)(2,1)}, u32[]{:S(2)}) copy-start(bf16[2,40,40,128]{3,2,1,0:T(8,128)(2,1)} %get-tuple-element.250) | copy-start | bytes 2457604 | tf_op jit(solution)/shard_map/while
  199.5 2.8 copy-start
  217.5 7.7 %copy-start.4 = (bf16[4,40,104]{2,0,1:T(4,128)(2,1)S(1)}, bf16[4,40,104]{2,0,1:T(4,128)(2,1)}, u32[]{:S(2)}) copy-start(bf16[4,40,104]{2,0,1:T(4,128)(2,1)} %convolution_convert_fusion.20) | copy-start | bytes 99844 | tf_op jit(solution)/shard_map/while
  239.9 5.0 %copy-start.2 = (s32[2,40,40,128]{3,2,1,0:T(8,128)S(1)}, s32[2,40,40,128]{3,2,1,0:T(8,128)}, u32[]{:S(2)}) copy-start(s32[2,40,40,128]{3,2,1,0:T(8,128)} %get-tuple-element.249) | copy-start | bytes 4915204 | tf_op jit(solution)/shard_map/while
  240.0 5.0 %copy-start.3 = (bf16[2,40,40,128]{3,2,1,0:T(8,128)(2,1)S(1)}, bf16[2,40,40,128]{3,2,1,0:T(8,128)(2,1)}, u32[]{:S(2)}) copy-start(bf16[2,40,40,128]{3,2,1,0:T(8,128)(2,1)} %get-tuple-element.250) | copy-start | bytes 2457604 | tf_op jit(solution)/shard_map/while
  244.4 2.8 copy-start
  262.4 7.7 %copy-start.4 = (bf16[4,40,104]{2,0,1:T(4,128)(2,1)S(1)}, bf16[4,40,104]{2,0,1:T(4,128)(2,1)}, u32[]{:S(2)}) copy-start(bf16[4,40,104]{2,0,1:T(4,128)(2,1)} %convolution_convert_fusion.20) | copy-start | bytes 99844 | tf_op jit(solution)/shard_map/while

commit v2 on v1

v2 whole, which is shorter than its diff:
```python
import jax
import jax.numpy as jnp
import numpy as np
from jax import lax
from jax.experimental import pallas as pl
from jax.experimental.pallas import tpu as pltpu
from jax.sharding import PartitionSpec as P

K = 64
R = 8
CP_DEV = 4
NEED = 3
HALF = 32
X, Y, Z = 40, 40, 128
XB = X // 8
EXT = 104
GROUPS = EXT // 4
ROWS = 2 * EXT
NARROW = 128
TOP = 32


def x_table():
    table = np.zeros((K, XB, 2, 8, 2, EXT), np.float32)
    for b in range(XB):
        for o in range(8):
            for t in range(K):
                for s in range(2):
                    table[t, b, s, o, s, b * 8 + o + t] = 1
    return jnp.asarray(table.reshape(K, XB * 16, ROWS), jnp.bfloat16)


def y_table(first, count, low, high):
    table = np.zeros((K, count, high - low, 8), np.float32)
    for o in range(count):
        for t in range(K):
            table[t, o, first + o + t - low, :] = 1
    return jnp.asarray(table.reshape(K, count, (high - low) * 8), jnp.bfloat16)


def z_table():
    table = np.zeros((K, Z + 2 * HALF, Z), np.float32)
    for o in range(Z):
        for t in range(K):
            i = o + t
            place = i - HALF if HALF <= i < HALF + Z else (Z + i if i < HALF else i)
            table[t, place, o] = 1
    return jnp.asarray(table, jnp.bfloat16)


def spread(filters, table):
    return jnp.einsum("rt,tmk->rmk", filters, table, preferred_element_type=jnp.float32).astype(
        jnp.bfloat16
    )


def same_lane(columns):
    return jnp.asarray(np.arange(columns)[None, :] % 8 == np.arange(8)[:, None], jnp.bfloat16)


def roll_half(value):
    return pltpu.roll(value, 64, 1)


def blur_kernel(
    live_ref, left_ref, own_ref, right_ref, a1_ref, a2_ref, a2b_ref, mask_ref, bz_ref,
    weights_ref, slot_ref, out_ref, line_x, line_y, band_y,
):
    out_ref[...] = jnp.zeros_like(out_ref)
    low_x = lax.broadcasted_iota(jnp.int32, (16, NARROW), 1) < 64
    low_y = lax.broadcasted_iota(jnp.int32, (256, NARROW), 1) < 64
    low_b = lax.broadcasted_iota(jnp.int32, (64, NARROW), 1) < 64

    def one_slot(slot, carry):
        def stage_x(part, offset):
            def step(i, carry):
                g = 2 * i
                rhs = jnp.concatenate(
                    [part[g, 0], part[g, 1], part[g + 1, 0], part[g + 1, 1], part[g, 2], part[g + 1, 2]],
                    axis=1,
                )
                made = jnp.dot(a1_ref[slot], rhs, preferred_element_type=jnp.float32)
                base = pl.multiple_of((offset + g) * 32, 64)
                for r in range(R):
                    for b in range(XB):
                        rows = slice((r * XB + b) * 16, (r * XB + b + 1) * 16)
                        for k in range(4):
                            line_x[r, pl.ds(base + k * 16, 16), b * 128 : (b + 1) * 128] = made[
                                rows, k * 128 : (k + 1) * 128
                            ].astype(jnp.bfloat16)
                    for k in range(2):
                        tails = [
                            made[(r * XB + b) * 16 : (r * XB + b + 1) * 16, 512 + k * 128 : 640 + k * 128]
                            for b in range(XB)
                        ]
                        turned = [roll_half(t) for t in tails]
                        at = pl.ds(base + k * 32, 16)
                        after = pl.ds(base + k * 32 + 16, 16)
                        for c in range(2):
                            lanes = slice((5 + c) * 128, (6 + c) * 128)
                            line_x[r, at, lanes] = jnp.where(low_x, tails[2 * c], turned[2 * c + 1]).astype(jnp.bfloat16)
                            line_x[r, after, lanes] = jnp.where(low_x, turned[2 * c], tails[2 * c + 1]).astype(jnp.bfloat16)
                        lanes = slice(7 * 128, 8 * 128)
                        line_x[r, at, lanes] = (tails[4] if r % 2 == 0 else turned[4]).astype(jnp.bfloat16)
                        line_x[r, after, lanes] = (turned[4] if r % 2 == 0 else tails[4]).astype(jnp.bfloat16)
                return carry

            lax.fori_loop(0, part.shape[0] // 2, step, 0)

        stage_x(left_ref, 0)
        stage_x(own_ref, 8)
        stage_x(right_ref, 18)

        def pair(q, carry):
            tops, ends = [], []
            for h in range(2):
                r = 2 * q + h
                top = a2_ref[slot * R + r]
                for o in range(8):
                    band_y[h, o * TOP : (o + 1) * TOP, :] = top * mask_ref[o : o + 1, :]
                tops.append(jnp.dot(band_y[h], line_x[r, 0:768, :], preferred_element_type=jnp.float32))
                ends.append(jnp.dot(a2b_ref[slot * R + r], line_x[r, 256:832, :], preferred_element_type=jnp.float32))
            for made, count, start, low in ((tops, 256, 0, low_y), (ends, 64, 1280, low_b)):
                lanes = pl.multiple_of(q * 384, 128)
                for b in range(XB):
                    rows = slice(start + b * count, start + (b + 1) * count)
                    for h in range(2):
                        line_y[rows, pl.ds(lanes + h * 128, 128)] = made[h][:, b * 128 : (b + 1) * 128].astype(jnp.bfloat16)
                tail = pl.ds(lanes + 256, 128)
                for c in range(2):
                    first = made[0][:, (5 + c) * 128 : (6 + c) * 128]
                    second = made[1][:, (5 + c) * 128 : (6 + c) * 128]
                    rows = slice(start + 2 * c * count, start + (2 * c + 1) * count)
                    line_y[rows, tail] = jnp.where(low, first, roll_half(second)).astype(jnp.bfloat16)
                    rows = slice(start + (2 * c + 1) * count, start + (2 * c + 2) * count)
                    line_y[rows, tail] = jnp.where(low, roll_half(first), second).astype(jnp.bfloat16)
                rows = slice(start + 4 * count, start + 5 * count)
                line_y[rows, tail] = jnp.where(low, made[0][:, 896:1024], made[1][:, 896:1024]).astype(jnp.bfloat16)
            return carry

        lax.fori_loop(0, R // 2, pair, 0)

        done = jnp.dot(line_y[...], bz_ref[slot], preferred_element_type=jnp.float32)
        for low, high, made in ((0, TOP, done[:1280]), (TOP, Y, done[1280:])):
            weight = jnp.zeros((X, high - low, Z), jnp.float32)
            for j in range(2):
                here = slot_ref[j, :, low:high, :] == slot
                weight = weight + jnp.where(here, weights_ref[j, :, low:high, :].astype(jnp.float32), 0.0)
            out_ref[:, low:high, :] += weight * made.reshape(X, high - low, Z)
        return carry

    lax.fori_loop(0, live_ref[0], one_slot, 0)


def blur(live, left, own, right, bands, weights, cell_slot):
    a1, a2, a2b, bz = bands
    vmem = pl.BlockSpec(memory_space=pltpu.VMEM)
    mask = same_lane(768)
    return pl.pallas_call(
        blur_kernel,
        out_shape=jax.ShapeDtypeStruct((X, Y, Z), jnp.float32),
        in_specs=[pl.BlockSpec(memory_space=pltpu.SMEM)] + [vmem] * 10,
        out_specs=vmem,
        scratch_shapes=[
            pltpu.VMEM((R, 832, 1024), jnp.bfloat16),
            pltpu.VMEM((1600, 1536), jnp.bfloat16),
            pltpu.VMEM((2, 256, 768), jnp.bfloat16),
        ],
        compiler_params=pltpu.CompilerParams(vmem_limit_bytes=60 * 1024 * 1024),
    )(live, left, own, right, a1, a2, a2b, mask, bz, weights, cell_slot)


def make_bands(panels):
    filters = panels.reshape(NEED * R, 3, K)
    a1 = spread(filters[:, 0], x_table()).reshape(NEED, R * XB * 16, ROWS)
    a2 = spread(filters[:, 1], y_table(0, TOP, 0, 96))
    ends = spread(filters[:, 1], y_table(TOP, Y - TOP, 32, 104))
    a2b = (ends[:, None] * same_lane(576)[None, :, None, :]).reshape(NEED * R, 64, 576)
    bz = spread(filters[:, 2], z_table()).reshape(NEED, R // 2, 2, Z + 2 * HALF, Z)
    bz = jnp.concatenate(
        [bz[:, :, 0, :Z], bz[:, :, 1, :Z], bz[:, :, 0, Z:], bz[:, :, 1, Z:]], axis=2
    ).reshape(NEED, R * (Z + 2 * HALF), Z)
    return a1, a2, a2b, bz


def gathered(rows, axis):
    count = lax.axis_size(axis)
    position = lax.axis_index(axis)
    bit = 1
    while bit < count:
        other = lax.ppermute(rows, axis, [(i, i ^ bit) for i in range(count)])
        upper = (position & bit) != 0
        rows = jnp.concatenate(
            [jnp.where(upper, other, rows), jnp.where(upper, rows, other)], axis=0
        )
        bit *= 2
    return rows


def both_ways(to_next, to_last, axis):
    count = lax.axis_size(axis)
    ends = count - 1
    return (
        lax.ppermute(to_next, axis, [(i, (i + 1) % count) for i in range(ends)]),
        lax.ppermute(to_last, axis, [((i + 1) % count, i) for i in range(ends)]),
    )


def halo(reflect):
    own = reflect.astype(jnp.bfloat16).transpose(1, 0, 2)
    parts = own.reshape(5, 2, 2, 2, X, Z)

    def packed(cells):
        return jnp.concatenate([cells[:, a, b] for a in range(2) for b in range(2)], axis=-1)

    left, right = both_ways(packed(parts[..., Z - HALF :]), packed(parts[..., :HALF]), "gz")
    tails = []
    for a in range(2):
        pieces = []
        for b in range(2):
            lanes = slice((2 * a + b) * HALF, (2 * a + b + 1) * HALF)
            pieces += [left[..., lanes], right[..., lanes]]
        tails.append(jnp.concatenate(pieces, axis=-1))
    tail = jnp.stack(tails, axis=1).reshape(10, 2, X, NARROW)
    block = jnp.concatenate([own.reshape(10, 4, X, Z), tail], axis=1)
    before, after = both_ways(block[:, :, X - HALF :], block[:, :, :HALF], "il")
    block = jnp.concatenate([before, block, after], axis=2).reshape(10, 3, ROWS, NARROW)
    left, right = both_ways(block[2:], block[:8], "xl")
    return left, block, right


def per_device(reflect, weights, cell_slot, factors, reader_list):
    listed = reader_list.reshape(NEED)
    live_mask = listed >= 0
    live_count = jnp.sum(live_mask.astype(jnp.int32))
    cross_count = lax.axis_size("xl")
    depth_count = lax.axis_size("gz")
    owner_index = jnp.where(live_mask, listed // (CP_DEV * depth_count) % cross_count, 0)
    local_row = jnp.where(live_mask, listed % CP_DEV, 0)
    panel_table = gathered(factors, "xl")
    row_key = owner_index * CP_DEV + local_row
    row_pick = (jnp.arange(cross_count * CP_DEV)[None, :] == row_key[:, None]) & live_mask[:, None]
    panels = jnp.dot(
        row_pick.astype(jnp.bfloat16), panel_table, preferred_element_type=jnp.float32
    ).astype(jnp.bfloat16)
    bands = make_bands(panels)
    left, own, right = halo(reflect)
    return blur(live_count.reshape(1), left, own, right, bands, weights, cell_slot)


def solution(mesh):
    in_specs = (
        P("il", "xl", "gz"),
        P(None, "il", "xl", "gz"),
        P(None, "il", "xl", "gz"),
        P(("il", "xl", "gz"), None),
        P("il", "xl", "gz", None),
    )
    out_specs = P("il", "xl", "gz")
    return jax.shard_map(
        per_device, mesh=mesh, in_specs=in_specs, out_specs=out_specs, check_vma=False
    )
```

time: 283 us -> 138 us (0.49)
  the two profiles are of different devices: /device:TPU:23 before, /device:TPU:47 now
where the time goes in v2:
time: 138 us
  Pallas kernels  49.8 us (36%)
  starting transfers between devices  37.9 us (27%)
  waiting for transfers between devices  29.3 us (21%)
  local copies, waits for them, and re-layouts  8.52 us (6%)
  other arithmetic  7.72 us (6%)
  matrix products  4.02 us (3%)
    pallas_call x1, Pallas kernels, blur(): pl.pallas_call(blur_kernel, out_shape=jax.ShapeDtypeStruct((X, Y, Z), jnp...  49.8 us
    ppermute x3, starting transfers between devices, both_ways(): lax.ppermute(to_next, axis, [(i, (i + 1) % count) for i in range(ends)])  21.9 us
    ppermute x3, waiting for transfers between devices, both_ways(): lax.ppermute(to_last, axis, [((i + 1) % count, i) for i in range(ends)])  12.9 us
    ppermute x3, waiting for transfers between devices, both_ways(): lax.ppermute(to_next, axis, [(i, (i + 1) % count) for i in range(ends)])  12.2 us
    ppermute x3, starting transfers between devices, gathered(): other = lax.ppermute(rows, axis, [(i, i ^ bit) for i in range(count)])  8.72 us
    ppermute x3, starting transfers between devices, both_ways(): lax.ppermute(to_last, axis, [((i + 1) % count, i) for i in range(ends)])  7.23 us
    ppermute x3, waiting for transfers between devices, gathered(): other = lax.ppermute(rows, axis, [(i, i ^ bit) for i in range(count)])  4.16 us
    dot_general x4, matrix products, spread(): jnp.einsum('rt,tmk->rmk', filters, table, preferred_element_type=jnp.floa...  3.82 us
  transfers between devices with their start and end apart: 9, of which 7 were waited for; matrix products, arithmetic and copies ran while one was open for 11% of the time, Pallas kernels for 0%

profile of v2, /device:TPU:47, one launch (start us, length us, event | category | flops | bytes accessed | tf_op | source)
XLA Modules:
  0.0 137.5 jit_solution(10284369869387976953)
XLA Ops:
  0.0 0.0 copy-start.7
  0.0 0.0 copy-start.6
  0.0 0.0 copy-start.8
  0.0 2.7 %collective-permute-start.6 = (bf16[4,1536]{1,0:T(4,128)(2,1)}, bf16[4,1536]{1,0:T(4,128)(2,1)S(1)}, u32[]{:S(2)}, u32[]{:S(2)}) collective-permute-start(bf16[4,1536]{1,0:T(4,128)(2,1)} %param.14), channel_id=1, source_target_pairs={{0,8},{8,0},{16,24},{24,16},{32,40},{40,32},{48,56},{56,48},{1,9},... | collective-permute-start | bytes 36872 | tf_op jit(solution)/shard_map/ppermute | solution.py:191
  2.7 1.2 convert_element_type.23
  3.9 0.7 slice_bitcast_fusion.7
  4.7 0.6 pad_maximum_fusion.4
  5.3 14.5 %collective-permute-start = (bf16[5,2,40,128]{3,1,0,2:T(2,128)(2,1)S(1)}, bf16[5,2,40,128]{3,1,0,2:T(2,128)(2,1)S(1)}, u32[]{:S(2)}, u32[]{:S(2)}) collective-permute-start(bf16[5,2,40,128]{3,1,0,2:T(2,128)(2,1)S(1)} %pad_maximum_fusion.4), channel_id=1, source_target_pairs={{0,1},{1,2},{2,3},{3,4},{4,5},{5,6},{6,7},{8,9},{9,10},{10,11},{11... | collective-permute-start | bytes 307208 | tf_op jit(solution)/shard_map/ppermute | solution.py:204
  19.8 0.6 pad_maximum_fusion.5
  20.4 1.9 %collective-permute-start.1 = (bf16[5,2,40,128]{3,1,0,2:T(2,128)(2,1)S(1)}, bf16[5,2,40,128]{3,1,0,2:T(2,128)(2,1)S(1)}, u32[]{:S(2)}, u32[]{:S(2)}) collective-permute-start(bf16[5,2,40,128]{3,1,0,2:T(2,128)(2,1)S(1)} %pad_maximum_fusion.5), channel_id=1, source_target_pairs={{1,0},{2,1},{3,2},{4,3},{5,4},{6,5},{7,6},{9,8},{10,9},{11,10},{12... | collective-permute-start | bytes 307208 | tf_op jit(solution)/shard_map/ppermute | solution.py:205
  22.4 0.0 copy-done.7
  22.4 0.0 collective-permute-done.6
  22.4 0.0 copy-done.6
  22.5 2.1 %collective-permute-start.7 = (bf16[8,1536]{1,0:T(8,128)(2,1)S(1)}, bf16[8,1536]{1,0:T(8,128)(2,1)S(1)}, u32[]{:S(2)}, u32[]{:S(2)}) collective-permute-start(bf16[8,1536]{1,0:T(8,128)(2,1)S(1)} %pad_maximum_fusion.7), channel_id=1, source_target_pairs={{0,16},{8,24},{16,0},{24,8},{32,48},{40,56},{48,32},{56,40},{1,17}... | collective-permute-start | bytes 73736 | tf_op jit(solution)/shard_map/ppermute | solution.py:191
  24.6 0.0 copy-done.8
  24.6 0.6 fusion.11
  25.2 1.8 %collective-permute-done.7 = bf16[8,1536]{1,0:T(8,128)(2,1)S(1)} collective-permute-done((bf16[8,1536]{1,0:T(8,128)(2,1)S(1)}, bf16[8,1536]{1,0:T(8,128)(2,1)S(1)}, u32[]{:S(2)}, u32[]{:S(2)}) %collective-permute-start.7) | collective-permute-done | bytes 24608 | tf_op jit(solution)/shard_map/ppermute | solution.py:191
  27.1 3.9 %collective-permute-start.8 = (bf16[16,1536]{1,0:T(8,128)(2,1)S(1)}, bf16[16,1536]{1,0:T(8,128)(2,1)S(1)}, u32[]{:S(2)}, u32[]{:S(2)}) collective-permute-start(bf16[16,1536]{1,0:T(8,128)(2,1)S(1)} %pad_maximum_fusion.6), channel_id=1, source_target_pairs={{0,32},{8,40},{16,48},{24,56},{32,0},{40,8},{48,16},{56,24},{1,33}... | collective-permute-start | bytes 147464 | tf_op jit(solution)/shard_map/ppermute | solution.py:191
  31.0 0.1 copy.39
  31.1 2.3 %collective-permute-done.8 = bf16[16,1536]{1,0:T(8,128)(2,1)S(1)} collective-permute-done((bf16[16,1536]{1,0:T(8,128)(2,1)S(1)}, bf16[16,1536]{1,0:T(8,128)(2,1)S(1)}, u32[]{:S(2)}, u32[]{:S(2)}) %collective-permute-start.8) | collective-permute-done | bytes 49184 | tf_op jit(solution)/shard_map/ppermute | solution.py:191
  33.4 0.2 convolution_convert_fusion
  33.6 0.1 reshape.113
  33.8 0.0 copy-start.2
  33.8 2.6 %convolution_convert_fusion.1 = bf16[24,192,128]{2,0,1:T(8,128)(2,1)S(1)} fusion(bf16[64,192,128]{2,0,1:T(8,128)(2,1)} %constant.68.clone, bf16[24,1,64]{2,1,0:T(2,128)(2,1)S(1)} %get-tuple-element.33), kind=kOutput, calls=%fused_computation.4 | convolution fusion | flops 76087296 | bytes 4328448 | tf_op jit(solution)/shard_map/rt,tmk->rmk/dot_general | solution.py:52
  36.4 0.1 copy-done.2
  36.5 0.5 convolution_convert_fusion.2
  37.0 0.0 collective-permute-done
  37.0 0.4 fusion.17
  37.4 6.6 %collective-permute-done.1 = bf16[5,2,40,128]{3,1,0,2:T(2,128)(2,1)S(1)} collective-permute-done((bf16[5,2,40,128]{3,1,0,2:T(2,128)(2,1)S(1)}, bf16[5,2,40,128]{3,1,0,2:T(2,128)(2,1)S(1)}, u32[]{:S(2)}, u32[]{:S(2)}) %collective-permute-start.1) | collective-permute-done | bytes 102432 | tf_op jit(solution)/shard_map/ppermute | solution.py:205
  43.9 0.4 fusion.18
  44.4 1.3 maximum_bitcast_fusion
  45.6 0.0 copy-start.1
  45.6 0.3 pad_maximum_fusion.3
  46.0 0.2 fusion
  46.1 2.1 %collective-permute-start.2 = (bf16[10,6,32,128]{3,2,1,0:T(8,128)(2,1)S(1)}, bf16[10,6,32,128]{3,2,1,0:T(8,128)(2,1)S(1)}, u32[]{:S(2)}, u32[]{:S(2)}) collective-permute-start(bf16[10,6,32,128]{3,2,1,0:T(8,128)(2,1)S(1)} %get-tuple-element.11), channel_id=1, source_target_pairs={{0,64},{64,128},{128,192},{192,256},{256,320},{320,384},{384,448},... | collective-permute-start | bytes 1474568 | tf_op jit(solution)/shard_map/ppermute | solution.py:204
  48.2 3.4 %collective-permute-start.3 = (bf16[10,6,32,128]{3,2,1,0:T(8,128)(2,1)S(1)}, bf16[10,6,32,128]{3,2,1,0:T(8,128)(2,1)S(1)}, u32[]{:S(2)}, u32[]{:S(2)}) collective-permute-start(bf16[10,6,32,128]{3,2,1,0:T(8,128)(2,1)S(1)} %get-tuple-element.12), channel_id=1, source_target_pairs={{64,0},{128,64},{192,128},{256,192},{320,256},{384,320},{448,384},... | collective-permute-start | bytes 1474568 | tf_op jit(solution)/shard_map/ppermute | solution.py:205
  51.6 0.5 fusion.16
  52.2 0.0 copy-done.1
  52.2 0.6 fusion.4
  52.7 6.7 %collective-permute-done.2 = bf16[10,6,32,128]{3,2,1,0:T(8,128)(2,1)S(1)} collective-permute-done((bf16[10,6,32,128]{3,2,1,0:T(8,128)(2,1)S(1)}, bf16[10,6,32,128]{3,2,1,0:T(8,128)(2,1)S(1)}, u32[]{:S(2)}, u32[]{:S(2)}) %collective-permute-start.2) | collective-permute-done | bytes 491552 | tf_op jit(solution)/shard_map/ppermute | solution.py:204
  59.5 1.9 %collective-permute-done.3 = bf16[10,6,32,128]{3,2,1,0:T(8,128)(2,1)S(1)} collective-permute-done((bf16[10,6,32,128]{3,2,1,0:T(8,128)(2,1)S(1)}, bf16[10,6,32,128]{3,2,1,0:T(8,128)(2,1)S(1)}, u32[]{:S(2)}, u32[]{:S(2)}) %collective-permute-start.3) | collective-permute-done | bytes 491552 | tf_op jit(solution)/shard_map/ppermute | solution.py:205
  61.4 0.1 pad_maximum_fusion
  61.5 0.0 copy-start
  61.5 0.0 copy-start.5
  61.5 0.3 fusion.14
  61.8 0.8 copy-done
  62.7 5.4 %collective-permute-start.4 = (bf16[8,3,208,128]{3,2,1,0:T(8,128)(2,1)S(1)}, bf16[8,3,208,128]{3,2,1,0:T(8,128)(2,1)S(1)}, u32[]{:S(2)}, u32[]{:S(2)}) collective-permute-start(bf16[8,3,208,128]{3,2,1,0:T(8,128)(2,1)S(1)} %bitcast.104), channel_id=1, source_target_pairs={{0,8},{8,16},{16,24},{24,32},{32,40},{40,48},{48,56},{1,9},{9,17},... | collective-permute-start | bytes 3833864 | tf_op jit(solution)/shard_map/ppermute | solution.py:204
  68.1 1.9 %collective-permute-start.5 = (bf16[8,3,208,128]{3,2,1,0:T(8,128)(2,1)S(1)}, bf16[8,3,208,128]{3,2,1,0:T(8,128)(2,1)S(1)}, u32[]{:S(2)}, u32[]{:S(2)}) collective-permute-start(bf16[8,3,208,128]{3,2,1,0:T(8,128)(2,1)S(1)} %bitcast.103), channel_id=1, source_target_pairs={{8,0},{16,8},{24,16},{32,24},{40,32},{48,40},{56,48},{9,1},{17,9},... | collective-permute-start | bytes 3833864 | tf_op jit(solution)/shard_map/ppermute | solution.py:205
  70.0 0.0 copy-done.5
  70.0 0.2 convolution_convert_fusion.3
  70.3 1.3 copy.76.a2_ref
  71.5 1.2 copy.41
  72.7 0.1 copy_bitcast_fusion.2
  72.8 1.1 fusion.15
  73.9 0.2 copy_bitcast_fusion
  74.1 1.2 pad_maximum_fusion.1
  75.3 1.5 %bitcast_multiply_fusion.a2b_ref = bf16[24,64,576]{2,1,0:T(8,128)(2,1)} fusion(bf16[64,576]{1,0:T(8,128)(2,1)S(1)} %broadcast_bitcast_fusion, bf16[24,8,576]{2,1,0:T(8,128)(2,1)S(1)} %copy.44), kind=kLoop, calls=%fused_computation.2 | loop fusion | flops 884736 | bytes 2064384 | tf_op jit(solution)/shard_map/mul | solution.py:178
  76.8 5.5 %collective-permute-done.4.left_ref = bf16[8,3,208,128]{3,2,1,0:T(8,128)(2,1)S(1)} collective-permute-done((bf16[8,3,208,128]{3,2,1,0:T(8,128)(2,1)S(1)}, bf16[8,3,208,128]{3,2,1,0:T(8,128)(2,1)S(1)}, u32[]{:S(2)}, u32[]{:S(2)}) %collective-permute-start.4) | collective-permute-done | bytes 1277984 | tf_op jit(solution)/shard_map/ppermute | solution.py:204
  82.3 0.0 copy-start.3
  82.3 4.4 %collective-permute-done.5.right_ref = bf16[8,3,208,128]{3,2,1,0:T(8,128)(2,1)S(1)} collective-permute-done((bf16[8,3,208,128]{3,2,1,0:T(8,128)(2,1)S(1)}, bf16[8,3,208,128]{3,2,1,0:T(8,128)(2,1)S(1)}, u32[]{:S(2)}, u32[]{:S(2)}) %collective-permute-start.5) | collective-permute-done | bytes 1277984 | tf_op jit(solution)/shard_map/ppermute | solution.py:205
  86.7 0.0 copy-start.4
  86.7 0.0 copy-done.3
  86.7 1.1 copy-done.4
  87.8 49.8 %shard_map.109 = f32[40,40,128]{2,1,0:T(8,128)} custom-call(s32[1]{0:T(128)} %bitcast.1.live_ref, bf16[8,3,208,128]{3,2,1,0:T(8,128)(2,1)} %copy-done.3, bf16[10,3,208,128]{3,2,1,0:T(8,128)(2,1)} %bitcast.94, bf16[8,3,208,128]{3,2,1,0:T(8,128)(2,1)} %copy-done.4, bf16[3,640,208]{2,1,0:T(8,128)(2,1)} %bitcast.100, bf16[24,32,768]{2,1,0:T(8,128)(2,1)} %copy.76.a2_ref, ...), custom_call_target="tpu_custom_call" | custom-call | tf_op jit(solution)/shard_map/pallas_call | solution.py:159
  (10 shorter events, 0.2 us)
Async XLA Ops:
  0.0 22.4 %copy-start.7 = (bf16[8,576]{1,0:T(8,128)(2,1)S(1)}, bf16[8,576]{1,0:T(8,128)(2,1)}, u32[]{:S(2)}) copy-start(bf16[8,576]{1,0:T(8,128)(2,1)} %constant.67.clone) | copy-start | bytes 27652
  0.0 22.4 %copy-start.6 = (bf16[4,1536]{1,0:T(4,128)(2,1)S(1)}, bf16[4,1536]{1,0:T(4,128)(2,1)}, u32[]{:S(2)}) copy-start(bf16[4,1536]{1,0:T(4,128)(2,1)} %param.14) | copy-start | bytes 36868
  0.0 24.6 %copy-start.8 = (s32[1,1,1,3]{3,2,1,0:T(1,128)S(1)}, s32[1,1,1,3]{3,2,1,0:T(1,128)}, u32[]{:S(2)}) copy-start(s32[1,1,1,3]{3,2,1,0:T(1,128)} %param.15) | copy-start | bytes 40
  0.0 22.4 %collective-permute-start.6 = (bf16[4,1536]{1,0:T(4,128)(2,1)}, bf16[4,1536]{1,0:T(4,128)(2,1)S(1)}, u32[]{:S(2)}, u32[]{:S(2)}) collective-permute-start(bf16[4,1536]{1,0:T(4,128)(2,1)} %param.14), channel_id=1, source_target_pairs={{0,8},{8,0},{16,24},{24,16},{32,40},{40,32},{48,56},{56,48},{1,9},... | collective-permute-start | bytes 36872 | tf_op jit(solution)/shard_map/ppermute | solution.py:191
  5.3 31.6 %collective-permute-start = (bf16[5,2,40,128]{3,1,0,2:T(2,128)(2,1)S(1)}, bf16[5,2,40,128]{3,1,0,2:T(2,128)(2,1)S(1)}, u32[]{:S(2)}, u32[]{:S(2)}) collective-permute-start(bf16[5,2,40,128]{3,1,0,2:T(2,128)(2,1)S(1)} %pad_maximum_fusion.4), channel_id=1, source_target_pairs={{0,1},{1,2},{2,3},{3,4},{4,5},{5,6},{6,7},{8,9},{9,10},{10,11},{11... | collective-permute-start | bytes 307208 | tf_op jit(solution)/shard_map/ppermute | solution.py:204
  20.4 23.5 %collective-permute-start.1 = (bf16[5,2,40,128]{3,1,0,2:T(2,128)(2,1)S(1)}, bf16[5,2,40,128]{3,1,0,2:T(2,128)(2,1)S(1)}, u32[]{:S(2)}, u32[]{:S(2)}) collective-permute-start(bf16[5,2,40,128]{3,1,0,2:T(2,128)(2,1)S(1)} %pad_maximum_fusion.5), channel_id=1, source_target_pairs={{1,0},{2,1},{3,2},{4,3},{5,4},{6,5},{7,6},{9,8},{10,9},{11,10},{12... | collective-permute-start | bytes 307208 | tf_op jit(solution)/shard_map/ppermute | solution.py:205
  22.5 4.6 %collective-permute-start.7 = (bf16[8,1536]{1,0:T(8,128)(2,1)S(1)}, bf16[8,1536]{1,0:T(8,128)(2,1)S(1)}, u32[]{:S(2)}, u32[]{:S(2)}) collective-permute-start(bf16[8,1536]{1,0:T(8,128)(2,1)S(1)} %pad_maximum_fusion.7), channel_id=1, source_target_pairs={{0,16},{8,24},{16,0},{24,8},{32,48},{40,56},{48,32},{56,40},{1,17}... | collective-permute-start | bytes 73736 | tf_op jit(solution)/shard_map/ppermute | solution.py:191
  27.1 6.3 %collective-permute-start.8 = (bf16[16,1536]{1,0:T(8,128)(2,1)S(1)}, bf16[16,1536]{1,0:T(8,128)(2,1)S(1)}, u32[]{:S(2)}, u32[]{:S(2)}) collective-permute-start(bf16[16,1536]{1,0:T(8,128)(2,1)S(1)} %pad_maximum_fusion.6), channel_id=1, source_target_pairs={{0,32},{8,40},{16,48},{24,56},{32,0},{40,8},{48,16},{56,24},{1,33}... | collective-permute-start | bytes 147464 | tf_op jit(solution)/shard_map/ppermute | solution.py:191
  33.8 2.7 %copy-start.2 = (bf16[64,80,208]{2,0,1:T(8,128)(2,1)S(1)}, bf16[64,80,208]{2,0,1:T(8,128)(2,1)}, u32[]{:S(2)}) copy-start(bf16[64,80,208]{2,0,1:T(8,128)(2,1)} %constant.64.clone) | copy-start | bytes 6389764
  45.6 6.5 %copy-start.1 = (bf16[64,32,768]{2,0,1:T(8,128)(2,1)S(1)}, bf16[64,32,768]{2,0,1:T(8,128)(2,1)}, u32[]{:S(2)}) copy-start(bf16[64,32,768]{2,0,1:T(8,128)(2,1)} %constant.65.clone) | copy-start | bytes 9437188
  46.1 13.3 %collective-permute-start.2 = (bf16[10,6,32,128]{3,2,1,0:T(8,128)(2,1)S(1)}, bf16[10,6,32,128]{3,2,1,0:T(8,128)(2,1)S(1)}, u32[]{:S(2)}, u32[]{:S(2)}) collective-permute-start(bf16[10,6,32,128]{3,2,1,0:T(8,128)(2,1)S(1)} %get-tuple-element.11), channel_id=1, source_target_pairs={{0,64},{64,128},{128,192},{192,256},{256,320},{320,384},{384,448},... | collective-permute-start | bytes 1474568 | tf_op jit(solution)/shard_map/ppermute | solution.py:204
  48.2 13.2 %collective-permute-start.3 = (bf16[10,6,32,128]{3,2,1,0:T(8,128)(2,1)S(1)}, bf16[10,6,32,128]{3,2,1,0:T(8,128)(2,1)S(1)}, u32[]{:S(2)}, u32[]{:S(2)}) collective-permute-start(bf16[10,6,32,128]{3,2,1,0:T(8,128)(2,1)S(1)} %get-tuple-element.12), channel_id=1, source_target_pairs={{64,0},{128,64},{192,128},{256,192},{320,256},{384,320},{448,384},... | collective-permute-start | bytes 1474568 | tf_op jit(solution)/shard_map/ppermute | solution.py:205
  61.5 1.1 copy-start
  61.5 8.5 %copy-start.5 = (bf16[64,8,576]{2,0,1:T(8,128)(2,1)S(1)}, bf16[64,8,576]{2,0,1:T(8,128)(2,1)}, u32[]{:S(2)}) copy-start(bf16[64,8,576]{2,0,1:T(8,128)(2,1)} %constant.66.clone) | copy-start | bytes 1769476
  62.7 19.6 %collective-permute-start.4 = (bf16[8,3,208,128]{3,2,1,0:T(8,128)(2,1)S(1)}, bf16[8,3,208,128]{3,2,1,0:T(8,128)(2,1)S(1)}, u32[]{:S(2)}, u32[]{:S(2)}) collective-permute-start(bf16[8,3,208,128]{3,2,1,0:T(8,128)(2,1)S(1)} %bitcast.104), channel_id=1, source_target_pairs={{0,8},{8,16},{16,24},{24,32},{32,40},{40,48},{48,56},{1,9},{9,17},... | collective-permute-start | bytes 3833864 | tf_op jit(solution)/shard_map/ppermute | solution.py:204
  68.1 18.6 %collective-permute-start.5 = (bf16[8,3,208,128]{3,2,1,0:T(8,128)(2,1)S(1)}, bf16[8,3,208,128]{3,2,1,0:T(8,128)(2,1)S(1)}, u32[]{:S(2)}, u32[]{:S(2)}) collective-permute-start(bf16[8,3,208,128]{3,2,1,0:T(8,128)(2,1)S(1)} %bitcast.103), channel_id=1, source_target_pairs={{8,0},{16,8},{24,16},{32,24},{40,32},{48,40},{56,48},{9,1},{17,9},... | collective-permute-start | bytes 3833864 | tf_op jit(solution)/shard_map/ppermute | solution.py:205
  82.3 4.4 %copy-start.3 = (bf16[8,3,208,128]{3,2,1,0:T(8,128)(2,1)}, bf16[8,3,208,128]{3,2,1,0:T(8,128)(2,1)S(1)}, u32[]{:S(2)}) copy-start(bf16[8,3,208,128]{3,2,1,0:T(8,128)(2,1)S(1)} %collective-permute-done.4.left_ref) | copy-start | bytes 3833860
  86.7 1.1 copy-start.4

commit v3 on v2

--- a/solution.py
+++ b/solution.py
@@ -21,12 +21,15 @@
 
 
 def x_table():
-    table = np.zeros((K, XB, 2, 8, 2, EXT), np.float32)
+    table = np.zeros((K, XB, 2, 8, ROWS), np.float32)
     for b in range(XB):
         for o in range(8):
             for t in range(K):
-                for s in range(2):
-                    table[t, b, s, o, s, b * 8 + o + t] = 1
+                x = b * 8 + o + t
+                for start, count in ((0, HALF), (HALF, X), (HALF + X, HALF)):
+                    if start <= x < start + count:
+                        for s in range(2):
+                            table[t, b, s, o, 2 * start + s * count + x - start] = 1
     return jnp.asarray(table.reshape(K, XB * 16, ROWS), jnp.bfloat16)
 
 
@@ -63,7 +66,7 @@
 
 
 def blur_kernel(
-    live_ref, left_ref, own_ref, right_ref, a1_ref, a2_ref, a2b_ref, mask_ref, bz_ref,
+    live_ref, left_ref, own_ref, right_ref, left_tail, own_tail, right_tail, a1_ref, a2_ref, a2b_ref, mask_ref, bz_ref,
     weights_ref, slot_ref, out_ref, line_x, line_y, band_y,
 ):
     out_ref[...] = jnp.zeros_like(out_ref)
@@ -72,11 +75,11 @@
     low_b = lax.broadcasted_iota(jnp.int32, (64, NARROW), 1) < 64
 
     def one_slot(slot, carry):
-        def stage_x(part, offset):
+        def stage_x(part, tail, offset):
             def step(i, carry):
                 g = 2 * i
                 rhs = jnp.concatenate(
-                    [part[g, 0], part[g, 1], part[g + 1, 0], part[g + 1, 1], part[g, 2], part[g + 1, 2]],
+                    [part[4 * i], part[4 * i + 1], part[4 * i + 2], part[4 * i + 3], tail[g], tail[g + 1]],
                     axis=1,
                 )
                 made = jnp.dot(a1_ref[slot], rhs, preferred_element_type=jnp.float32)
@@ -105,11 +108,11 @@
                         line_x[r, after, lanes] = (turned[4] if r % 2 == 0 else tails[4]).astype(jnp.bfloat16)
                 return carry
 
-            lax.fori_loop(0, part.shape[0] // 2, step, 0)
-
-        stage_x(left_ref, 0)
-        stage_x(own_ref, 8)
-        stage_x(right_ref, 18)
+            lax.fori_loop(0, part.shape[0] // 4, step, 0)
+
+        stage_x(left_ref, left_tail, 0)
+        stage_x(own_ref, own_tail, 8)
+        stage_x(right_ref, right_tail, 18)
 
         def pair(q, carry):
             tops, ends = [], []
@@ -152,14 +155,14 @@
     lax.fori_loop(0, live_ref[0], one_slot, 0)
 
 
-def blur(live, left, own, right, bands, weights, cell_slot):
+def blur(live, cells, bands, weights, cell_slot):
     a1, a2, a2b, bz = bands
     vmem = pl.BlockSpec(memory_space=pltpu.VMEM)
     mask = same_lane(768)
     return pl.pallas_call(
         blur_kernel,
         out_shape=jax.ShapeDtypeStruct((X, Y, Z), jnp.float32),
-        in_specs=[pl.BlockSpec(memory_space=pltpu.SMEM)] + [vmem] * 10,
+        in_specs=[pl.BlockSpec(memory_space=pltpu.SMEM)] + [vmem] * 13,
         out_specs=vmem,
         scratch_shapes=[
             pltpu.VMEM((R, 832, 1024), jnp.bfloat16),
@@ -167,7 +170,7 @@
             pltpu.VMEM((2, 256, 768), jnp.bfloat16),
         ],
         compiler_params=pltpu.CompilerParams(vmem_limit_bytes=60 * 1024 * 1024),
-    )(live, left, own, right, a1, a2, a2b, mask, bz, weights, cell_slot)
+    )(live, *cells, a1, a2, a2b, mask, bz, weights, cell_slot)
 
 
 def make_bands(panels):
@@ -206,27 +209,108 @@
     )
 
 
+def lane_part():
+    return lax.broadcasted_iota(jnp.int32, (1, NARROW), 1) // HALF
+
+
+def cut_kernel(reflect_ref, own_ref, next_ref, last_ref, deeper_ref, shallower_ref):
+    part = lane_part()
+    for g in range(Y // 8):
+        rows = [reflect_ref[:, 8 * g + k, :] for k in range(8)]
+        for pair in range(4):
+            two = rows[2 * pair : 2 * pair + 2]
+            own_ref[4 * g + pair] = jnp.concatenate(two, axis=0).astype(jnp.bfloat16)
+            next_ref[4 * g + pair] = jnp.concatenate([v[X - HALF :] for v in two], axis=0).astype(jnp.bfloat16)
+            last_ref[4 * g + pair] = jnp.concatenate([v[:HALF] for v in two], axis=0).astype(jnp.bfloat16)
+        for ref, first in ((deeper_ref, Z - HALF), (shallower_ref, 0)):
+            packed = []
+            for s in range(2):
+                value = None
+                for k in range(4):
+                    shift = (k * HALF - first) % NARROW
+                    turned = rows[2 * k + s]
+                    turned = pltpu.roll(turned, shift, 1) if shift else turned
+                    value = turned if value is None else jnp.where(part == k, turned, value)
+                packed.append(value)
+            ref[g] = jnp.concatenate(packed, axis=0).astype(jnp.bfloat16)
+
+
+def cut(reflect):
+    shapes = [(20, 80, Z), (20, 64, Z), (20, 64, Z), (5, 80, NARROW), (5, 80, NARROW)]
+    vmem = pl.BlockSpec(memory_space=pltpu.VMEM)
+    return pl.pallas_call(
+        cut_kernel,
+        out_shape=[jax.ShapeDtypeStruct(shape, jnp.bfloat16) for shape in shapes],
+        in_specs=[vmem],
+        out_specs=[vmem] * 5,
+    )(reflect)
+
+
+def tail_kernel(left_ref, right_ref, after_ref, own_ref, next_ref, last_ref):
+    part = lane_part()
+    for g in range(5):
+        left = left_ref[g].astype(jnp.float32)
+        right = right_ref[g].astype(jnp.float32)
+        for a in range(2):
+            value = left if a == 0 else pltpu.roll(left, 64, 1)
+            for k, (source, at) in enumerate(((right, 2 * a), (left, 2 * a + 1), (right, 2 * a + 1)), 1):
+                shift = ((k - at) * HALF) % NARROW
+                turned = pltpu.roll(source, shift, 1) if shift else source
+                value = jnp.where(part == k, turned, value)
+            own_ref[2 * g + a] = value.astype(jnp.bfloat16)
+            next_ref[2 * g + a] = jnp.concatenate(
+                [value[X - HALF : X], value[2 * X - HALF :]], axis=0
+            ).astype(jnp.bfloat16)
+            last_ref[2 * g + a] = jnp.concatenate(
+                [value[:HALF], value[X : X + HALF]], axis=0
+            ).astype(jnp.bfloat16)
+
+
+def unpack_tail(left, right, after):
+    shapes = [(10, 80, NARROW), (10, 64, NARROW), (10, 64, NARROW)]
+    vmem = pl.BlockSpec(memory_space=pltpu.VMEM)
+    return pl.pallas_call(
+        tail_kernel,
+        out_shape=[jax.ShapeDtypeStruct(shape, jnp.bfloat16) for shape in shapes],
+        in_specs=[vmem, vmem, pl.BlockSpec(memory_space=pl.ANY)],
+        out_specs=[vmem] * 3,
+    )(left, right, after)
+
+
+def join_kernel(before_ref, own_ref, after_ref, all_ref, next_ref, last_ref):
+    count = own_ref.shape[0]
+    edge = next_ref.shape[0]
+    for ref, start in ((all_ref, 0), (next_ref, count - edge), (last_ref, 0)):
+        rows = slice(start, start + ref.shape[0])
+        ref[:, 0:64, :] = before_ref[rows]
+        ref[:, 64:144, :] = own_ref[rows]
+        ref[:, 144:208, :] = after_ref[rows]
+
+
+def join(before, own, after):
+    count = own.shape[0]
+    counts = (count, count * 4 // 5, count * 4 // 5)
+    vmem = pl.BlockSpec(memory_space=pltpu.VMEM)
+    return pl.pallas_call(
+        join_kernel,
+        out_shape=[jax.ShapeDtypeStruct((n, ROWS, NARROW), jnp.bfloat16) for n in counts],
+        in_specs=[vmem] * 3,
+        out_specs=[vmem] * 3,
+        compiler_params=pltpu.CompilerParams(vmem_limit_bytes=32 * 1024 * 1024),
+    )(before, own, after)
+
+
 def halo(reflect):
-    own = reflect.astype(jnp.bfloat16).transpose(1, 0, 2)
-    parts = own.reshape(5, 2, 2, 2, X, Z)
-
-    def packed(cells):
-        return jnp.concatenate([cells[:, a, b] for a in range(2) for b in range(2)], axis=-1)
-
-    left, right = both_ways(packed(parts[..., Z - HALF :]), packed(parts[..., :HALF]), "gz")
-    tails = []
-    for a in range(2):
-        pieces = []
-        for b in range(2):
-            lanes = slice((2 * a + b) * HALF, (2 * a + b + 1) * HALF)
-            pieces += [left[..., lanes], right[..., lanes]]
-        tails.append(jnp.concatenate(pieces, axis=-1))
-    tail = jnp.stack(tails, axis=1).reshape(10, 2, X, NARROW)
-    block = jnp.concatenate([own.reshape(10, 4, X, Z), tail], axis=1)
-    before, after = both_ways(block[:, :, X - HALF :], block[:, :, :HALF], "il")
-    block = jnp.concatenate([before, block, after], axis=2).reshape(10, 3, ROWS, NARROW)
-    left, right = both_ways(block[2:], block[:8], "xl")
-    return left, block, right
+    own, to_next, to_last, deeper, shallower = cut(reflect)
+    above, below = both_ways(deeper, shallower, "gz")
+    before, after = both_ways(to_next, to_last, "il")
+    main, to_next, to_last = join(before, own, after)
+    left, right = both_ways(to_next, to_last, "xl")
+    tail, to_next, to_last = unpack_tail(above, below, main)
+    before, after = both_ways(to_next, to_last, "il")
+    tail, to_next, to_last = join(before, tail, after)
+    left_tail, right_tail = both_ways(to_next, to_last, "xl")
+    return left, main, right, left_tail, tail, right_tail
 
 
 def per_device(reflect, weights, cell_slot, factors, reader_list):
@@ -244,8 +328,7 @@
         row_pick.astype(jnp.bfloat16), panel_table, preferred_element_type=jnp.float32
     ).astype(jnp.bfloat16)
     bands = make_bands(panels)
-    left, own, right = halo(reflect)
-    return blur(live_count.reshape(1), left, own, right, bands, weights, cell_slot)
+    return blur(live_count.reshape(1), halo(reflect), bands, weights, cell_slot)
 
 
 def solution(mesh):

time: 138 us -> 136 us (0.986)
  the two profiles are of different devices: /device:TPU:47 before, /device:TPU:417 now
where the time goes in v3:
time: 136 us; the launch traced here: 135 us
  Pallas kernels  54.7 us (40%)
  starting transfers between devices  51.9 us (38%)
  local copies, waits for them, and re-layouts  13.2 us (10%)
  matrix products  5.92 us (4%)
  other arithmetic  5.39 us (4%)
  waiting for transfers between devices  3.47 us (3%)
    pallas_call x1, Pallas kernels, blur(): pl.pallas_call(blur_kernel, out_shape=jax.ShapeDtypeStruct((X, Y, Z), jnp...  49.7 us
    ppermute x5, starting transfers between devices, both_ways(): lax.ppermute(to_last, axis, [((i + 1) % count, i) for i in range(ends)])  22.6 us
    ppermute x5, starting transfers between devices, both_ways(): lax.ppermute(to_next, axis, [(i, (i + 1) % count) for i in range(ends)])  18.7 us
    ppermute x3, starting transfers between devices, gathered(): other = lax.ppermute(rows, axis, [(i, i ^ bit) for i in range(count)])  10.6 us
    dot_general x4, matrix products, spread(): jnp.einsum('rt,tmk->rmk', filters, table, preferred_element_type=jnp.floa...  5.73 us
    unnamed x30, local copies, waits for them, and re-layouts  4.52 us
  transfers between devices with their start and end apart: 13, of which 3 were waited for; matrix products, arithmetic and copies ran while one was open for 15% of the time, Pallas kernels for 2%

profile of v3, /device:TPU:417, one launch (start us, length us, event | category | flops | bytes accessed | tf_op | source)
XLA Modules:
  0.0 134.9 jit_solution(12643420970190453461)
XLA Ops:
  0.0 2.6 %collective-permute-start.10 = (bf16[4,1536]{1,0:T(4,128)(2,1)}, bf16[4,1536]{1,0:T(4,128)(2,1)S(1)}, u32[]{:S(2)}, u32[]{:S(2)}) collective-permute-start(bf16[4,1536]{1,0:T(4,128)(2,1)} %param.14), channel_id=1, source_target_pairs={{0,8},{8,0},{16,24},{24,16},{32,40},{40,32},{48,56},{56,48},{1,9},... | collective-permute-start | bytes 36872 | tf_op jit(solution)/shard_map/ppermute | solution.py:194
  2.6 2.7 %shard_map.109 = (bf16[20,80,128]{2,1,0:T(8,128)(2,1)}, bf16[20,64,128]{2,1,0:T(8,128)(2,1)}, bf16[20,64,128]{2,1,0:T(8,128)(2,1)}, bf16[5,80,128]{2,1,0:T(8,128)(2,1)}, bf16[5,80,128]{2,1,0:T(8,128)(2,1)}) custom-call(f32[40,40,128]{2,1,0:T(8,128)} %reflect_ref.1), custom_call_target="tpu_custom_call" | custom-call | tf_op jit(solution)/shard_map/pallas_call | solution.py:241
  5.2 3.1 %collective-permute-start.4 = (bf16[5,80,128]{2,1,0:T(8,128)(2,1)}, bf16[5,80,128]{2,1,0:T(8,128)(2,1)}, u32[]{:S(2)}, u32[]{:S(2)}) collective-permute-start(bf16[5,80,128]{2,1,0:T(8,128)(2,1)} %get-tuple-element.25), channel_id=1, source_target_pairs={{0,1},{1,2},{2,3},{3,4},{4,5},{5,6},{6,7},{8,9},{9,10},{10,11},{11... | collective-permute-start | bytes 307208 | tf_op jit(solution)/shard_map/ppermute | solution.py:207
  8.4 13.0 %collective-permute-start.5 = (bf16[5,80,128]{2,1,0:T(8,128)(2,1)}, bf16[5,80,128]{2,1,0:T(8,128)(2,1)}, u32[]{:S(2)}, u32[]{:S(2)}) collective-permute-start(bf16[5,80,128]{2,1,0:T(8,128)(2,1)} %get-tuple-element.26), channel_id=1, source_target_pairs={{1,0},{2,1},{3,2},{4,3},{5,4},{6,5},{7,6},{9,8},{10,9},{11,10},{12... | collective-permute-start | bytes 307208 | tf_op jit(solution)/shard_map/ppermute | solution.py:208
  21.4 2.6 %collective-permute-start = (bf16[20,64,128]{2,1,0:T(8,128)(2,1)}, bf16[20,64,128]{2,1,0:T(8,128)(2,1)S(1)}, u32[]{:S(2)}, u32[]{:S(2)}) collective-permute-start(bf16[20,64,128]{2,1,0:T(8,128)(2,1)} %get-tuple-element.19), channel_id=1, source_target_pairs={{0,64},{64,128},{128,192},{192,256},{256,320},{320,384},{384,448},... | collective-permute-start | bytes 983048 | tf_op jit(solution)/shard_map/ppermute | solution.py:207
  24.0 2.6 %collective-permute-start.1 = (bf16[20,64,128]{2,1,0:T(8,128)(2,1)}, bf16[20,64,128]{2,1,0:T(8,128)(2,1)S(1)}, u32[]{:S(2)}, u32[]{:S(2)}) collective-permute-start(bf16[20,64,128]{2,1,0:T(8,128)(2,1)} %get-tuple-element.21), channel_id=1, source_target_pairs={{64,0},{128,64},{192,128},{256,192},{320,256},{384,320},{448,384},... | collective-permute-start | bytes 983048 | tf_op jit(solution)/shard_map/ppermute | solution.py:208
  26.7 1.4 %broadcast_bitcast_fusion = bf16[64,576]{1,0:T(8,128)(2,1)} fusion(bf16[8,576]{1,0:T(8,128)(2,1)} %constant.67.clone), kind=kLoop, calls=%fused_computation.17 | loop fusion | bytes 82944 | tf_op jit(solution)/shard_map/mul | solution.py:181
  28.0 0.0 collective-permute-done.10
  28.0 0.7 broadcast_select_fusion.5
  28.8 3.2 %collective-permute-start.11 = (bf16[8,1536]{1,0:T(8,128)(2,1)S(1)}, bf16[8,1536]{1,0:T(8,128)(2,1)S(1)}, u32[]{:S(2)}, u32[]{:S(2)}) collective-permute-start(bf16[8,1536]{1,0:T(8,128)(2,1)S(1)} %pad_maximum_fusion.2), channel_id=1, source_target_pairs={{0,16},{8,24},{16,0},{24,8},{32,48},{40,56},{48,32},{56,40},{1,17}... | collective-permute-start | bytes 73736 | tf_op jit(solution)/shard_map/ppermute | solution.py:194
  32.0 0.7 bitcast_compare_fusion
  32.6 1.0 collective-permute-done.11
  33.7 4.8 %collective-permute-start.12 = (bf16[16,1536]{1,0:T(8,128)(2,1)S(1)}, bf16[16,1536]{1,0:T(8,128)(2,1)S(1)}, u32[]{:S(2)}, u32[]{:S(2)}) collective-permute-start(bf16[16,1536]{1,0:T(8,128)(2,1)S(1)} %pad_maximum_fusion.1), channel_id=1, source_target_pairs={{0,32},{8,40},{16,48},{24,56},{32,0},{40,8},{48,16},{56,24},{1,33}... | collective-permute-start | bytes 147464 | tf_op jit(solution)/shard_map/ppermute | solution.py:194
  38.5 1.3 fusion.10
  39.8 0.2 collective-permute-done.12
  40.0 0.2 convolution_convert_fusion
  40.2 0.1 reshape.95
  40.4 2.4 %convolution_convert_fusion.1 = bf16[24,192,128]{2,0,1:T(8,128)(2,1)S(1)} fusion(bf16[64,192,128]{2,0,1:T(8,128)(2,1)} %constant.68.clone, bf16[24,1,64]{2,1,0:T(2,128)(2,1)S(1)} %get-tuple-element.41), kind=kOutput, calls=%fused_computation.3 | convolution fusion | flops 76087296 | bytes 4328448 | tf_op jit(solution)/shard_map/rt,tmk->rmk/dot_general | solution.py:55
  42.8 0.0 copy-start.6
  42.8 1.1 fusion.13
  43.9 0.0 copy-start.5
  43.9 0.6 copy-done.6
  44.5 1.4 %convolution_convert_fusion.2 = bf16[24,80,208]{2,0,1:T(8,128)(2,1)} fusion(bf16[64,80,208]{2,0,1:T(8,128)(2,1)S(1)} %copy-done.6, bf16[24,1,64]{2,1,0:T(2,128)(2,1)S(1)} %get-tuple-element.43), kind=kOutput, calls=%fused_computation.4 | convolution fusion | flops 51517440 | bytes 2931712 | tf_op jit(solution)/shard_map/rt,tmk->rmk/dot_general | solution.py:55
  46.0 0.0 copy-done.5
  46.0 0.6 fusion.3
  46.6 0.0 copy-start.2
  46.6 1.1 copy_bitcast_fusion
  47.7 1.4 %fusion.14 = (bf16[3,4,1,64,128]{4,2,1,0,3:T(2,128)(2,1)}, bf16[3,4,1,64,128]{4,2,1,0,3:T(2,128)(2,1)}) fusion(bf16[3,4,2,192,128]{4,2,1,0,3:T(2,128)(2,1)S(1)} %bitcast.52), kind=kLoop, calls=%fused_computation.49 | loop fusion | bytes 786432 | tf_op jit(solution)/shard_map/slice | solution.py:184
  49.1 0.0 collective-permute-done.before_ref
  49.1 0.0 collective-permute-done.1.after_ref
  49.1 0.0 copy-done.2
  49.1 0.2 shard_map.110
  49.3 0.0 copy-start
  49.3 1.0 copy-done
  50.3 0.0 collective-permute-done.4.left_ref
  50.3 0.0 collective-permute-done.5.right_ref
  50.3 2.0 %shard_map.111 = (bf16[10,80,128]{2,1,0:T(8,128)(2,1)}, bf16[10,64,128]{2,1,0:T(8,128)(2,1)}, bf16[10,64,128]{2,1,0:T(8,128)(2,1)}) custom-call(bf16[5,80,128]{2,1,0:T(8,128)(2,1)} %collective-permute-done.4.left_ref, bf16[5,80,128]{2,1,0:T(8,128)(2,1)} %collective-permute-done.5.right_ref, bf16[20,208,128]{2,1,0:T(8,128)(2,1)} %copy-done), custom_call_target="tpu_custom_call" | custom-call | tf_op jit(solution)/shard_map/pallas_call | solution.py:272
  52.4 2.6 %collective-permute-start.6 = (bf16[10,64,128]{2,1,0:T(8,128)(2,1)}, bf16[10,64,128]{2,1,0:T(8,128)(2,1)S(1)}, u32[]{:S(2)}, u32[]{:S(2)}) collective-permute-start(bf16[10,64,128]{2,1,0:T(8,128)(2,1)} %get-tuple-element.27), channel_id=1, source_target_pairs={{0,64},{64,128},{128,192},{192,256},{256,320},{320,384},{384,448},... | collective-permute-start | bytes 491528 | tf_op jit(solution)/shard_map/ppermute | solution.py:207
  55.0 3.1 %collective-permute-start.7 = (bf16[10,64,128]{2,1,0:T(8,128)(2,1)}, bf16[10,64,128]{2,1,0:T(8,128)(2,1)S(1)}, u32[]{:S(2)}, u32[]{:S(2)}) collective-permute-start(bf16[10,64,128]{2,1,0:T(8,128)(2,1)} %get-tuple-element.29), channel_id=1, source_target_pairs={{64,0},{128,64},{192,128},{256,192},{320,256},{384,320},{448,384},... | collective-permute-start | bytes 491528 | tf_op jit(solution)/shard_map/ppermute | solution.py:208
  58.1 6.5 %collective-permute-start.2 = (bf16[16,208,128]{2,1,0:T(8,128)(2,1)S(1)}, bf16[16,208,128]{2,1,0:T(8,128)(2,1)S(1)}, u32[]{:S(2)}, u32[]{:S(2)}) collective-permute-start(bf16[16,208,128]{2,1,0:T(8,128)(2,1)S(1)} %get-tuple-element.22), channel_id=1, source_target_pairs={{0,8},{8,16},{16,24},{24,32},{32,40},{40,48},{48,56},{1,9},{9,17},... | collective-permute-start | bytes 2555912 | tf_op jit(solution)/shard_map/ppermute | solution.py:207
  64.7 1.9 %collective-permute-start.3 = (bf16[16,208,128]{2,1,0:T(8,128)(2,1)S(1)}, bf16[16,208,128]{2,1,0:T(8,128)(2,1)S(1)}, u32[]{:S(2)}, u32[]{:S(2)}) collective-permute-start(bf16[16,208,128]{2,1,0:T(8,128)(2,1)S(1)} %get-tuple-element.24), channel_id=1, source_target_pairs={{8,0},{16,8},{24,16},{32,24},{40,32},{48,40},{56,48},{9,1},{17,9},... | collective-permute-start | bytes 2555912 | tf_op jit(solution)/shard_map/ppermute | solution.py:208
  66.6 1.3 convolution_convert_fusion.3
  67.9 0.0 collective-permute-done.6.before_ref
  67.9 0.0 collective-permute-done.7.after_ref
  67.9 0.0 copy-start.3
  67.9 0.9 copy-done.3
  68.8 0.1 shard_map.112
  69.0 0.0 copy-start.1
  69.0 3.8 %collective-permute-start.8 = (bf16[8,208,128]{2,1,0:T(8,128)(2,1)S(1)}, bf16[8,208,128]{2,1,0:T(8,128)(2,1)S(1)}, u32[]{:S(2)}, u32[]{:S(2)}) collective-permute-start(bf16[8,208,128]{2,1,0:T(8,128)(2,1)S(1)} %get-tuple-element.30), channel_id=1, source_target_pairs={{0,8},{8,16},{16,24},{24,32},{32,40},{40,48},{48,56},{1,9},{9,17},... | collective-permute-start | bytes 1277960 | tf_op jit(solution)/shard_map/ppermute | solution.py:207
  72.8 1.9 %collective-permute-start.9 = (bf16[8,208,128]{2,1,0:T(8,128)(2,1)S(1)}, bf16[8,208,128]{2,1,0:T(8,128)(2,1)S(1)}, u32[]{:S(2)}, u32[]{:S(2)}) collective-permute-start(bf16[8,208,128]{2,1,0:T(8,128)(2,1)S(1)} %get-tuple-element.32), channel_id=1, source_target_pairs={{8,0},{16,8},{24,16},{32,24},{40,32},{48,40},{56,48},{9,1},{17,9},... | collective-permute-start | bytes 1277960 | tf_op jit(solution)/shard_map/ppermute | solution.py:208
  74.7 0.0 copy-done.9
  74.7 1.1 copy_bitcast_fusion.2
  75.9 0.0 copy-done.4
  75.9 1.2 copy.23
  77.1 1.3 copy.51.a2_ref
  78.3 1.1 pad_maximum_fusion
  79.5 1.5 %bitcast_multiply_fusion.a2b_ref = bf16[24,64,576]{2,1,0:T(8,128)(2,1)} fusion(bf16[64,576]{1,0:T(8,128)(2,1)S(1)} %copy-done.14, bf16[24,8,576]{2,1,0:T(8,128)(2,1)S(1)} %copy.26), kind=kLoop, calls=%fused_computation.2 | loop fusion | flops 884736 | bytes 2064384 | tf_op jit(solution)/shard_map/mul | solution.py:181
  81.0 0.0 collective-permute-done.8.left_tail
  81.0 2.3 %collective-permute-done.9.right_tail = bf16[8,208,128]{2,1,0:T(8,128)(2,1)S(1)} collective-permute-done((bf16[8,208,128]{2,1,0:T(8,128)(2,1)S(1)}, bf16[8,208,128]{2,1,0:T(8,128)(2,1)S(1)}, u32[]{:S(2)}, u32[]{:S(2)}) %collective-permute-start.9) | collective-permute-done | bytes 426016 | tf_op jit(solution)/shard_map/ppermute | solution.py:208
  83.2 0.0 collective-permute-done.2.left_ref
  83.2 0.0 collective-permute-done.3.right_ref
  83.2 0.9 copy-done.10
  84.2 1.0 copy-done.11
  85.2 49.7 %shard_map.113 = f32[40,40,128]{2,1,0:T(8,128)} custom-call(s32[1]{0:T(128)} %bitcast.1.live_ref, bf16[16,208,128]{2,1,0:T(8,128)(2,1)} %copy-done.10, bf16[20,208,128]{2,1,0:T(8,128)(2,1)} %copy-done, bf16[16,208,128]{2,1,0:T(8,128)(2,1)} %copy-done.11, bf16[8,208,128]{2,1,0:T(8,128)(2,1)} %copy-done.12, bf16[10,208,128]{2,1,0:T(8,128)(2,1)} %copy-done.1, ...), custom_call_target="tpu_custom_call" | custom-call | tf_op jit(solution)/shard_map/pallas_call | solution.py:162
  (21 shorter events, 0.2 us)
Async XLA Ops:
  0.0 28.0 %collective-permute-start.10 = (bf16[4,1536]{1,0:T(4,128)(2,1)}, bf16[4,1536]{1,0:T(4,128)(2,1)S(1)}, u32[]{:S(2)}, u32[]{:S(2)}) collective-permute-start(bf16[4,1536]{1,0:T(4,128)(2,1)} %param.14), channel_id=1, source_target_pairs={{0,8},{8,0},{16,24},{24,16},{32,40},{40,32},{48,56},{56,48},{1,9},... | collective-permute-start | bytes 36872 | tf_op jit(solution)/shard_map/ppermute | solution.py:194
  5.2 45.1 %collective-permute-start.4 = (bf16[5,80,128]{2,1,0:T(8,128)(2,1)}, bf16[5,80,128]{2,1,0:T(8,128)(2,1)}, u32[]{:S(2)}, u32[]{:S(2)}) collective-permute-start(bf16[5,80,128]{2,1,0:T(8,128)(2,1)} %get-tuple-element.25), channel_id=1, source_target_pairs={{0,1},{1,2},{2,3},{3,4},{4,5},{5,6},{6,7},{8,9},{9,10},{10,11},{11... | collective-permute-start | bytes 307208 | tf_op jit(solution)/shard_map/ppermute | solution.py:207
  8.4 42.0 %collective-permute-start.5 = (bf16[5,80,128]{2,1,0:T(8,128)(2,1)}, bf16[5,80,128]{2,1,0:T(8,128)(2,1)}, u32[]{:S(2)}, u32[]{:S(2)}) collective-permute-start(bf16[5,80,128]{2,1,0:T(8,128)(2,1)} %get-tuple-element.26), channel_id=1, source_target_pairs={{1,0},{2,1},{3,2},{4,3},{5,4},{6,5},{7,6},{9,8},{10,9},{11,10},{12... | collective-permute-start | bytes 307208 | tf_op jit(solution)/shard_map/ppermute | solution.py:208
  21.4 27.8 %collective-permute-start = (bf16[20,64,128]{2,1,0:T(8,128)(2,1)}, bf16[20,64,128]{2,1,0:T(8,128)(2,1)S(1)}, u32[]{:S(2)}, u32[]{:S(2)}) collective-permute-start(bf16[20,64,128]{2,1,0:T(8,128)(2,1)} %get-tuple-element.19), channel_id=1, source_target_pairs={{0,64},{64,128},{128,192},{192,256},{256,320},{320,384},{384,448},... | collective-permute-start | bytes 983048 | tf_op jit(solution)/shard_map/ppermute | solution.py:207
  24.0 25.1 %collective-permute-start.1 = (bf16[20,64,128]{2,1,0:T(8,128)(2,1)}, bf16[20,64,128]{2,1,0:T(8,128)(2,1)S(1)}, u32[]{:S(2)}, u32[]{:S(2)}) collective-permute-start(bf16[20,64,128]{2,1,0:T(8,128)(2,1)} %get-tuple-element.21), channel_id=1, source_target_pairs={{64,0},{128,64},{192,128},{256,192},{320,256},{384,320},{448,384},... | collective-permute-start | bytes 983048 | tf_op jit(solution)/shard_map/ppermute | solution.py:208
  28.8 4.9 %collective-permute-start.11 = (bf16[8,1536]{1,0:T(8,128)(2,1)S(1)}, bf16[8,1536]{1,0:T(8,128)(2,1)S(1)}, u32[]{:S(2)}, u32[]{:S(2)}) collective-permute-start(bf16[8,1536]{1,0:T(8,128)(2,1)S(1)} %pad_maximum_fusion.2), channel_id=1, source_target_pairs={{0,16},{8,24},{16,0},{24,8},{32,48},{40,56},{48,32},{56,40},{1,17}... | collective-permute-start | bytes 73736 | tf_op jit(solution)/shard_map/ppermute | solution.py:194
  33.7 6.3 %collective-permute-start.12 = (bf16[16,1536]{1,0:T(8,128)(2,1)S(1)}, bf16[16,1536]{1,0:T(8,128)(2,1)S(1)}, u32[]{:S(2)}, u32[]{:S(2)}) collective-permute-start(bf16[16,1536]{1,0:T(8,128)(2,1)S(1)} %pad_maximum_fusion.1), channel_id=1, source_target_pairs={{0,32},{8,40},{16,48},{24,56},{32,0},{40,8},{48,16},{56,24},{1,33}... | collective-permute-start | bytes 147464 | tf_op jit(solution)/shard_map/ppermute | solution.py:194
  42.8 1.7 %copy-start.6 = (bf16[64,80,208]{2,0,1:T(8,128)(2,1)S(1)}, bf16[64,80,208]{2,0,1:T(8,128)(2,1)}, u32[]{:S(2)}) copy-start(bf16[64,80,208]{2,0,1:T(8,128)(2,1)} %constant.64.clone) | copy-start | bytes 6389764
  43.9 2.1 %copy-start.5 = (bf16[64,32,768]{2,0,1:T(8,128)(2,1)S(1)}, bf16[64,32,768]{2,0,1:T(8,128)(2,1)}, u32[]{:S(2)}) copy-start(bf16[64,32,768]{2,0,1:T(8,128)(2,1)} %constant.65.clone) | copy-start | bytes 9437188
  46.6 2.6 %copy-start.2 = (bf16[20,80,128]{2,1,0:T(8,128)(2,1)S(1)}, bf16[20,80,128]{2,1,0:T(8,128)(2,1)}, u32[]{:S(2)}) copy-start(bf16[20,80,128]{2,1,0:T(8,128)(2,1)} %get-tuple-element.20.own_ref) | copy-start | bytes 1228804
  49.3 1.0 copy-start
  50.3 24.4 %copy-start.9 = (bf16[3,4,1,64,128]{4,2,1,0,3:T(2,128)(2,1)S(1)}, bf16[3,4,1,64,128]{4,2,1,0,3:T(2,128)(2,1)}, u32[]{:S(2)}) copy-start(bf16[3,4,1,64,128]{4,2,1,0,3:T(2,128)(2,1)} %get-tuple-element.35) | copy-start | bytes 589828
  52.4 15.5 %collective-permute-start.6 = (bf16[10,64,128]{2,1,0:T(8,128)(2,1)}, bf16[10,64,128]{2,1,0:T(8,128)(2,1)S(1)}, u32[]{:S(2)}, u32[]{:S(2)}) collective-permute-start(bf16[10,64,128]{2,1,0:T(8,128)(2,1)} %get-tuple-element.27), channel_id=1, source_target_pairs={{0,64},{64,128},{128,192},{192,256},{256,320},{320,384},{384,448},... | collective-permute-start | bytes 491528 | tf_op jit(solution)/shard_map/ppermute | solution.py:207
  55.0 12.9 %collective-permute-start.7 = (bf16[10,64,128]{2,1,0:T(8,128)(2,1)}, bf16[10,64,128]{2,1,0:T(8,128)(2,1)S(1)}, u32[]{:S(2)}, u32[]{:S(2)}) collective-permute-start(bf16[10,64,128]{2,1,0:T(8,128)(2,1)} %get-tuple-element.29), channel_id=1, source_target_pairs={{64,0},{128,64},{192,128},{256,192},{320,256},{384,320},{448,384},... | collective-permute-start | bytes 491528 | tf_op jit(solution)/shard_map/ppermute | solution.py:208
  58.1 25.1 %collective-permute-start.2 = (bf16[16,208,128]{2,1,0:T(8,128)(2,1)S(1)}, bf16[16,208,128]{2,1,0:T(8,128)(2,1)S(1)}, u32[]{:S(2)}, u32[]{:S(2)}) collective-permute-start(bf16[16,208,128]{2,1,0:T(8,128)(2,1)S(1)} %get-tuple-element.22), channel_id=1, source_target_pairs={{0,8},{8,16},{16,24},{24,32},{32,40},{40,48},{48,56},{1,9},{9,17},... | collective-permute-start | bytes 2555912 | tf_op jit(solution)/shard_map/ppermute | solution.py:207
  64.7 18.6 %collective-permute-start.3 = (bf16[16,208,128]{2,1,0:T(8,128)(2,1)S(1)}, bf16[16,208,128]{2,1,0:T(8,128)(2,1)S(1)}, u32[]{:S(2)}, u32[]{:S(2)}) collective-permute-start(bf16[16,208,128]{2,1,0:T(8,128)(2,1)S(1)} %get-tuple-element.24), channel_id=1, source_target_pairs={{8,0},{16,8},{24,16},{32,24},{40,32},{48,40},{56,48},{9,1},{17,9},... | collective-permute-start | bytes 2555912 | tf_op jit(solution)/shard_map/ppermute | solution.py:208
  67.9 0.9 copy-start.3
  68.8 7.0 %copy-start.4 = (bf16[24,80,208]{2,0,1:T(8,128)(2,1)S(1)}, bf16[24,80,208]{2,0,1:T(8,128)(2,1)}, u32[]{:S(2)}) copy-start(bf16[24,80,208]{2,0,1:T(8,128)(2,1)} %convolution_convert_fusion.2) | copy-start | bytes 2396164
  69.0 9.3 %copy-start.1 = (bf16[10,208,128]{2,1,0:T(8,128)(2,1)}, bf16[10,208,128]{2,1,0:T(8,128)(2,1)S(1)}, u32[]{:S(2)}) copy-start(bf16[10,208,128]{2,1,0:T(8,128)(2,1)S(1)} %get-tuple-element.31.own_tail) | copy-start | bytes 1597444
  69.0 12.0 %collective-permute-start.8 = (bf16[8,208,128]{2,1,0:T(8,128)(2,1)S(1)}, bf16[8,208,128]{2,1,0:T(8,128)(2,1)S(1)}, u32[]{:S(2)}, u32[]{:S(2)}) collective-permute-start(bf16[8,208,128]{2,1,0:T(8,128)(2,1)S(1)} %get-tuple-element.30), channel_id=1, source_target_pairs={{0,8},{8,16},{16,24},{24,32},{32,40},{40,48},{48,56},{1,9},{9,17},... | collective-permute-start | bytes 1277960 | tf_op jit(solution)/shard_map/ppermute | solution.py:207
  72.8 10.4 %collective-permute-start.9 = (bf16[8,208,128]{2,1,0:T(8,128)(2,1)S(1)}, bf16[8,208,128]{2,1,0:T(8,128)(2,1)S(1)}, u32[]{:S(2)}, u32[]{:S(2)}) collective-permute-start(bf16[8,208,128]{2,1,0:T(8,128)(2,1)S(1)} %get-tuple-element.32), channel_id=1, source_target_pairs={{8,0},{16,8},{24,16},{32,24},{40,32},{48,40},{56,48},{9,1},{17,9},... | collective-permute-start | bytes 1277960 | tf_op jit(solution)/shard_map/ppermute | solution.py:208
  75.8 2.5 %copy-start.7 = (bf16[3,4,128,128]{3,2,1,0:T(8,128)(2,1)S(1)}, bf16[3,4,128,128]{3,2,1,0:T(8,128)(2,1)}, u32[]{:S(2)}) copy-start(bf16[3,4,128,128]{3,2,1,0:T(8,128)(2,1)} %get-tuple-element.50) | copy-start | bytes 1179652
  75.8 2.5 %copy-start.8 = (bf16[3,4,128,128]{3,2,1,0:T(8,128)(2,1)S(1)}, bf16[3,4,128,128]{3,2,1,0:T(8,128)(2,1)}, u32[]{:S(2)}) copy-start(bf16[3,4,128,128]{3,2,1,0:T(8,128)(2,1)} %get-tuple-element.51) | copy-start | bytes 1179652
  77.0 2.4 %copy-start.14 = (bf16[64,576]{1,0:T(8,128)(2,1)S(1)}, bf16[64,576]{1,0:T(8,128)(2,1)}, u32[]{:S(2)}) copy-start(bf16[64,576]{1,0:T(8,128)(2,1)} %broadcast_bitcast_fusion) | copy-start | bytes 221188
  81.0 4.2 %copy-start.12 = (bf16[8,208,128]{2,1,0:T(8,128)(2,1)}, bf16[8,208,128]{2,1,0:T(8,128)(2,1)S(1)}, u32[]{:S(2)}) copy-start(bf16[8,208,128]{2,1,0:T(8,128)(2,1)S(1)} %collective-permute-done.8.left_tail) | copy-start | bytes 1277956
  83.2 1.9 %copy-start.13 = (bf16[8,208,128]{2,1,0:T(8,128)(2,1)}, bf16[8,208,128]{2,1,0:T(8,128)(2,1)S(1)}, u32[]{:S(2)}) copy-start(bf16[8,208,128]{2,1,0:T(8,128)(2,1)S(1)} %collective-permute-done.9.right_tail) | copy-start | bytes 1277956
  83.2 0.9 copy-start.10
  84.2 1.0 copy-start.11

commit v4 on v3

--- a/solution.py
+++ b/solution.py
@@ -12,53 +12,155 @@
 NEED = 3
 HALF = 32
 X, Y, Z = 40, 40, 128
-XB = X // 8
+XO = 4
+XB = X // XO
+LANES = XB * 192
 EXT = 104
-GROUPS = EXT // 4
 ROWS = 2 * EXT
 NARROW = 128
 TOP = 32
 
 
-def x_table():
-    table = np.zeros((K, XB, 2, 8, ROWS), np.float32)
-    for b in range(XB):
-        for o in range(8):
-            for t in range(K):
-                x = b * 8 + o + t
-                for start, count in ((0, HALF), (HALF, X), (HALF + X, HALF)):
-                    if start <= x < start + count:
-                        for s in range(2):
-                            table[t, b, s, o, 2 * start + s * count + x - start] = 1
-    return jnp.asarray(table.reshape(K, XB * 16, ROWS), jnp.bfloat16)
-
-
-def y_table(first, count, low, high):
-    table = np.zeros((K, count, high - low, 8), np.float32)
-    for o in range(count):
-        for t in range(K):
-            table[t, o, first + o + t - low, :] = 1
-    return jnp.asarray(table.reshape(K, count, (high - low) * 8), jnp.bfloat16)
-
-
-def z_table():
-    table = np.zeros((K, Z + 2 * HALF, Z), np.float32)
-    for o in range(Z):
-        for t in range(K):
-            i = o + t
-            place = i - HALF if HALF <= i < HALF + Z else (Z + i if i < HALF else i)
-            table[t, place, o] = 1
-    return jnp.asarray(table, jnp.bfloat16)
-
-
-def spread(filters, table):
-    return jnp.einsum("rt,tmk->rmk", filters, table, preferred_element_type=jnp.float32).astype(
-        jnp.bfloat16
+def same_lane():
+    return jnp.asarray(np.arange(EXT * XO)[None, :] % XO == np.arange(XO)[:, None], jnp.bfloat16)
+
+
+def tap_maps():
+    reverse = np.zeros((128, 128), np.float32)
+    repeat = np.zeros((128, 256), np.float32)
+    for t in range(K):
+        reverse[t, -t % 128] = 1
+        repeat[t, XO * t : XO * (t + 1)] = 1
+    return jnp.asarray(np.concatenate([reverse, repeat], axis=1), jnp.bfloat16)
+
+
+def bands_kernel(list_ref, table_ref, map_ref, a1_ref, a2_ref, a2b_ref, bz_ref, table, taps, long):
+    for tile in range(12):
+        table[tile] = table_ref[:, tile * 128 : (tile + 1) * 128].astype(jnp.float32)
+    lane = lax.broadcasted_iota(jnp.int32, (1, 128), 1)
+    for slot in range(NEED):
+        listed = jnp.maximum(list_ref[slot], 0)
+        key = (listed // (CP_DEV * 8)) % 8 * CP_DEV + listed % CP_DEV
+        for r in range(R):
+            for axis in range(3):
+                tile, half = divmod(3 * r + axis, 2)
+                piece = table[tile, pl.ds(key, 1), :]
+                if half:
+                    piece = pltpu.roll(piece, 64, 1)
+                at = axis * NEED * R + slot * R + r
+                taps[at : at + 1, :] = jnp.where(lane < K, piece, 0.0)
+    mapped = jnp.dot(
+        taps[...].astype(jnp.bfloat16), map_ref[...], preferred_element_type=jnp.float32
     )
-
-
-def same_lane(columns):
-    return jnp.asarray(np.arange(columns)[None, :] % 8 == np.arange(8)[:, None], jnp.bfloat16)
+    for tile in range(3):
+        long[tile] = mapped[:, tile * 128 : (tile + 1) * 128]
+
+    row8 = lax.broadcasted_iota(jnp.int32, (8, 128), 0)
+    lane8 = lax.broadcasted_iota(jnp.int32, (8, 128), 1)
+    low = row8 < 4
+
+    def between(first, last):
+        return (lane8 >= first) & (lane8 < last)
+
+    plain = low & between(0, 32)
+    by_32 = (low & between(64, 104)) | (~low & between(32, 64))
+    by_72 = ~low & between(104, 128)
+    end_72 = (low & between(16, 48)) | (~low & between(0, 16))
+    end_104 = ~low & between(48, 80)
+    row_z = lax.broadcasted_iota(jnp.int32, (128, 128), 0)
+    lane_z = lax.broadcasted_iota(jnp.int32, (128, 128), 1)
+    inside = lane_z <= row_z
+    row_y = lax.broadcasted_iota(jnp.int32, (TOP, 128), 0)
+    lane_y = lax.broadcasted_iota(jnp.int32, (TOP, 128), 1)
+    after = lane_y >= XO * row_y
+    after8 = lane8 >= XO * row8
+
+    def one_term(i, carry):
+        slot = i // R
+        r = i % R
+        row = jnp.broadcast_to(taps[pl.ds(i, 1), :], (8, 128))
+        base = pltpu.roll(row, 0, 1, stride=1, stride_axis=0)
+        base = jnp.where(low, base, pltpu.roll(base, 124, 1))
+        for b in range(0, XB, 2):
+            ends = ([], [])
+            for c in (b, b + 1):
+                turned = [
+                    pltpu.roll(base, (XO * c + k) % 128, 1) if (XO * c + k) % 128 else base
+                    for k in (0, 32, 72, 104)
+                ]
+                ends[0].append(
+                    jnp.where(plain, turned[0], jnp.where(by_32, turned[1], jnp.where(by_72, turned[2], 0.0)))
+                )
+                ends[1].append(jnp.where(end_72, turned[2], jnp.where(end_104, turned[3], 0.0)))
+            rows = pl.ds(pl.multiple_of(r * (XB * 8) + b * 8, 16), 16)
+            a1_ref[slot, rows, 0:128] = jnp.concatenate(ends[0], axis=0).astype(jnp.bfloat16)
+            a1_ref[slot, rows, 128:ROWS] = jnp.concatenate(ends[1], axis=0)[:, : ROWS - 128].astype(jnp.bfloat16)
+        halves = [
+            pltpu.roll(
+                jnp.broadcast_to(long[k, pl.ds(NEED * R + i, 1), :], (TOP, 128)),
+                0, 1, stride=XO, stride_axis=0,
+            )
+            for k in (1, 2)
+        ]
+        zero = jnp.zeros((TOP, 128), jnp.float32)
+        tiles = [
+            jnp.where(after, halves[0], 0.0),
+            jnp.where(after, halves[1], halves[0]),
+            jnp.where(after, 0.0, halves[1]),
+            zero,
+        ]
+        for k in range(4):
+            width = min(128, EXT * XO - 128 * k)
+            a2_ref[i, :, 128 * k : 128 * k + width] = tiles[k][:, :width].astype(jnp.bfloat16)
+        ends = [
+            jnp.zeros((8, 128), jnp.float32),
+            jnp.where(after8, halves[0][:8], 0.0),
+            jnp.where(after8, halves[1][:8], halves[0][:8]),
+            jnp.where(after8, 0.0, halves[1][:8]),
+        ]
+        for k in range(4):
+            width = min(128, EXT * XO - 128 * k)
+            for o in range(0, XO, 2):
+                two = jnp.concatenate(
+                    [jnp.where(lane8 % XO == c, ends[k], 0.0) for c in (o, o + 1)], axis=0
+                )
+                a2b_ref[i, 8 * o : 8 * o + 16, 128 * k : 128 * k + width] = two[:, :width].astype(jnp.bfloat16)
+        row = jnp.broadcast_to(long[0, pl.ds(2 * NEED * R + i, 1), :], (128, 128))
+        turned = pltpu.roll(row, 0, 1, stride=1, stride_axis=0)
+        first = jnp.where(inside, turned, 0.0).astype(jnp.bfloat16)
+        second = jnp.where(inside, 0.0, turned).astype(jnp.bfloat16)
+        start = (r // 2) * (2 * (Z + 2 * HALF))
+        own = pl.multiple_of(start + (r % 2) * Z, 128)
+        bz_ref[slot, pl.ds(own, 96), :] = first[32:]
+        bz_ref[slot, pl.ds(own + 96, 32), :] = second[:32]
+        ends = pl.multiple_of(start + 2 * Z + (r % 2) * 2 * HALF, 64)
+        bz_ref[slot, pl.ds(ends, 32), :] = first[:32]
+        bz_ref[slot, pl.ds(ends + 32, 32), :] = second[32:64]
+        return carry
+
+    lax.fori_loop(0, NEED * R, one_term, 0)
+
+
+def make_bands(listed, table):
+    shapes = [
+        (NEED, R * XB * 8, ROWS),
+        (NEED * R, TOP, EXT * XO),
+        (NEED * R, XO * (Y - TOP), EXT * XO),
+        (NEED, R * (Z + 2 * HALF), Z),
+    ]
+    vmem = pl.BlockSpec(memory_space=pltpu.VMEM)
+    return pl.pallas_call(
+        bands_kernel,
+        out_shape=[jax.ShapeDtypeStruct(shape, jnp.bfloat16) for shape in shapes],
+        in_specs=[pl.BlockSpec(memory_space=pltpu.SMEM), vmem, vmem],
+        out_specs=[vmem] * 4,
+        scratch_shapes=[
+            pltpu.VMEM((12, 32, 128), jnp.float32),
+            pltpu.VMEM((3 * NEED * R, 128), jnp.float32),
+            pltpu.VMEM((3, 3 * NEED * R, 128), jnp.float32),
+        ],
+        compiler_params=pltpu.CompilerParams(vmem_limit_bytes=32 * 1024 * 1024),
+    )(listed, table, tap_maps())
 
 
 def roll_half(value):
@@ -70,9 +172,9 @@
     weights_ref, slot_ref, out_ref, line_x, line_y, band_y,
 ):
     out_ref[...] = jnp.zeros_like(out_ref)
-    low_x = lax.broadcasted_iota(jnp.int32, (16, NARROW), 1) < 64
-    low_y = lax.broadcasted_iota(jnp.int32, (256, NARROW), 1) < 64
-    low_b = lax.broadcasted_iota(jnp.int32, (64, NARROW), 1) < 64
+    low_x = lax.broadcasted_iota(jnp.int32, (8, NARROW), 1) < 64
+    low_y = lax.broadcasted_iota(jnp.int32, (TOP * XO, NARROW), 1) < 64
+    low_b = lax.broadcasted_iota(jnp.int32, ((Y - TOP) * XO, NARROW), 1) < 64
 
     def one_slot(slot, carry):
         def stage_x(part, tail, offset):
@@ -83,29 +185,28 @@
                     axis=1,
                 )
                 made = jnp.dot(a1_ref[slot], rhs, preferred_element_type=jnp.float32)
-                base = pl.multiple_of((offset + g) * 32, 64)
+                base = pl.multiple_of((offset + g) * 16, 32)
+
+                def cell(r, b, k):
+                    row = (r * XB + b) * 8
+                    return made[row : row + 8, k * 128 : (k + 1) * 128]
+
+                def put(r, k, column, first, second):
+                    line_x[r, pl.ds(base + k * 16, 16), column * 128 : (column + 1) * 128] = (
+                        jnp.concatenate([first, second], axis=0).astype(jnp.bfloat16)
+                    )
+
                 for r in range(R):
-                    for b in range(XB):
-                        rows = slice((r * XB + b) * 16, (r * XB + b + 1) * 16)
-                        for k in range(4):
-                            line_x[r, pl.ds(base + k * 16, 16), b * 128 : (b + 1) * 128] = made[
-                                rows, k * 128 : (k + 1) * 128
-                            ].astype(jnp.bfloat16)
                     for k in range(2):
-                        tails = [
-                            made[(r * XB + b) * 16 : (r * XB + b + 1) * 16, 512 + k * 128 : 640 + k * 128]
-                            for b in range(XB)
-                        ]
-                        turned = [roll_half(t) for t in tails]
-                        at = pl.ds(base + k * 32, 16)
-                        after = pl.ds(base + k * 32 + 16, 16)
-                        for c in range(2):
-                            lanes = slice((5 + c) * 128, (6 + c) * 128)
-                            line_x[r, at, lanes] = jnp.where(low_x, tails[2 * c], turned[2 * c + 1]).astype(jnp.bfloat16)
-                            line_x[r, after, lanes] = jnp.where(low_x, turned[2 * c], tails[2 * c + 1]).astype(jnp.bfloat16)
-                        lanes = slice(7 * 128, 8 * 128)
-                        line_x[r, at, lanes] = (tails[4] if r % 2 == 0 else turned[4]).astype(jnp.bfloat16)
-                        line_x[r, after, lanes] = (turned[4] if r % 2 == 0 else tails[4]).astype(jnp.bfloat16)
+                        for b in range(XB):
+                            put(r, k, b, cell(r, b, 2 * k), cell(r, b, 2 * k + 1))
+                        for c in range(XB // 2):
+                            one, two = cell(r, 2 * c, 4 + k), cell(r, 2 * c + 1, 4 + k)
+                            put(
+                                r, k, XB + c,
+                                jnp.where(low_x, one, roll_half(two)),
+                                jnp.where(low_x, roll_half(one), two),
+                            )
                 return carry
 
             lax.fori_loop(0, part.shape[0] // 4, step, 0)
@@ -115,30 +216,31 @@
         stage_x(right_ref, right_tail, 18)
 
         def pair(q, carry):
-            tops, ends = [], []
+            made = []
             for h in range(2):
                 r = 2 * q + h
                 top = a2_ref[slot * R + r]
-                for o in range(8):
+                for o in range(XO):
                     band_y[h, o * TOP : (o + 1) * TOP, :] = top * mask_ref[o : o + 1, :]
-                tops.append(jnp.dot(band_y[h], line_x[r, 0:768, :], preferred_element_type=jnp.float32))
-                ends.append(jnp.dot(a2b_ref[slot * R + r], line_x[r, 256:832, :], preferred_element_type=jnp.float32))
-            for made, count, start, low in ((tops, 256, 0, low_y), (ends, 64, 1280, low_b)):
-                lanes = pl.multiple_of(q * 384, 128)
+                band_y[h, TOP * XO :, :] = a2b_ref[slot * R + r]
+                made.append(jnp.dot(band_y[h], line_x[r], preferred_element_type=jnp.float32))
+            lanes = pl.multiple_of(q * 384, 128)
+            tail = pl.ds(lanes + 256, 128)
+            for first, count, start, low in ((0, TOP * XO, 0, low_y), (TOP * XO, (Y - TOP) * XO, TOP * X, low_b)):
+
+                def cell(h, column):
+                    return made[h][first : first + count, column * 128 : (column + 1) * 128]
+
+                def rows(b):
+                    return slice(start + b * count, start + (b + 1) * count)
+
                 for b in range(XB):
-                    rows = slice(start + b * count, start + (b + 1) * count)
                     for h in range(2):
-                        line_y[rows, pl.ds(lanes + h * 128, 128)] = made[h][:, b * 128 : (b + 1) * 128].astype(jnp.bfloat16)
-                tail = pl.ds(lanes + 256, 128)
-                for c in range(2):
-                    first = made[0][:, (5 + c) * 128 : (6 + c) * 128]
-                    second = made[1][:, (5 + c) * 128 : (6 + c) * 128]
-                    rows = slice(start + 2 * c * count, start + (2 * c + 1) * count)
-                    line_y[rows, tail] = jnp.where(low, first, roll_half(second)).astype(jnp.bfloat16)
-                    rows = slice(start + (2 * c + 1) * count, start + (2 * c + 2) * count)
-                    line_y[rows, tail] = jnp.where(low, roll_half(first), second).astype(jnp.bfloat16)
-                rows = slice(start + 4 * count, start + 5 * count)
-                line_y[rows, tail] = jnp.where(low, made[0][:, 896:1024], made[1][:, 896:1024]).astype(jnp.bfloat16)
+                        line_y[rows(b), pl.ds(lanes + h * 128, 128)] = cell(h, b).astype(jnp.bfloat16)
+                for c in range(XB // 2):
+                    one, two = cell(0, XB + c), cell(1, XB + c)
+                    line_y[rows(2 * c), tail] = jnp.where(low, one, roll_half(two)).astype(jnp.bfloat16)
+                    line_y[rows(2 * c + 1), tail] = jnp.where(low, roll_half(one), two).astype(jnp.bfloat16)
             return carry
 
         lax.fori_loop(0, R // 2, pair, 0)
@@ -158,32 +260,19 @@
 def blur(live, cells, bands, weights, cell_slot):
     a1, a2, a2b, bz = bands
     vmem = pl.BlockSpec(memory_space=pltpu.VMEM)
-    mask = same_lane(768)
+    mask = same_lane()
     return pl.pallas_call(
         blur_kernel,
         out_shape=jax.ShapeDtypeStruct((X, Y, Z), jnp.float32),
         in_specs=[pl.BlockSpec(memory_space=pltpu.SMEM)] + [vmem] * 13,
         out_specs=vmem,
         scratch_shapes=[
-            pltpu.VMEM((R, 832, 1024), jnp.bfloat16),
+            pltpu.VMEM((R, EXT * XO, LANES), jnp.bfloat16),
             pltpu.VMEM((1600, 1536), jnp.bfloat16),
-            pltpu.VMEM((2, 256, 768), jnp.bfloat16),
+            pltpu.VMEM((2, Y * XO, EXT * XO), jnp.bfloat16),
         ],
         compiler_params=pltpu.CompilerParams(vmem_limit_bytes=60 * 1024 * 1024),
     )(live, *cells, a1, a2, a2b, mask, bz, weights, cell_slot)
-
-
-def make_bands(panels):
-    filters = panels.reshape(NEED * R, 3, K)
-    a1 = spread(filters[:, 0], x_table()).reshape(NEED, R * XB * 16, ROWS)
-    a2 = spread(filters[:, 1], y_table(0, TOP, 0, 96))
-    ends = spread(filters[:, 1], y_table(TOP, Y - TOP, 32, 104))
-    a2b = (ends[:, None] * same_lane(576)[None, :, None, :]).reshape(NEED * R, 64, 576)
-    bz = spread(filters[:, 2], z_table()).reshape(NEED, R // 2, 2, Z + 2 * HALF, Z)
-    bz = jnp.concatenate(
-        [bz[:, :, 0, :Z], bz[:, :, 1, :Z], bz[:, :, 0, Z:], bz[:, :, 1, Z:]], axis=2
-    ).reshape(NEED, R * (Z + 2 * HALF), Z)
-    return a1, a2, a2b, bz
 
 
 def gathered(rows, axis):
@@ -315,19 +404,8 @@
 
 def per_device(reflect, weights, cell_slot, factors, reader_list):
     listed = reader_list.reshape(NEED)
-    live_mask = listed >= 0
-    live_count = jnp.sum(live_mask.astype(jnp.int32))
-    cross_count = lax.axis_size("xl")
-    depth_count = lax.axis_size("gz")
-    owner_index = jnp.where(live_mask, listed // (CP_DEV * depth_count) % cross_count, 0)
-    local_row = jnp.where(live_mask, listed % CP_DEV, 0)
-    panel_table = gathered(factors, "xl")
-    row_key = owner_index * CP_DEV + local_row
-    row_pick = (jnp.arange(cross_count * CP_DEV)[None, :] == row_key[:, None]) & live_mask[:, None]
-    panels = jnp.dot(
-        row_pick.astype(jnp.bfloat16), panel_table, preferred_element_type=jnp.float32
-    ).astype(jnp.bfloat16)
-    bands = make_bands(panels)
+    live_count = jnp.sum((listed >= 0).astype(jnp.int32))
+    bands = make_bands(listed, gathered(factors, "xl"))
     return blur(live_count.reshape(1), halo(reflect), bands, weights, cell_slot)
 
 

time: 136 us -> 127 us (0.934)
  the two profiles are of different devices: /device:TPU:417 before, /device:TPU:71 now
where the time goes in v4:
time: 127 us
  starting transfers between devices  53.2 us (42%)
  Pallas kernels  53 us (42%)
  waiting for transfers between devices  9.5 us (7%)
  local copies, waits for them, and re-layouts  9.35 us (7%)
  other arithmetic  1.4 us (1%)
    pallas_call x1, Pallas kernels, blur(): pl.pallas_call(blur_kernel, out_shape=jax.ShapeDtypeStruct((X, Y, Z), jnp...  41.4 us
    ppermute x5, starting transfers between devices, both_ways(): lax.ppermute(to_next, axis, [(i, (i + 1) % count) for i in range(ends)])  31 us
    ppermute x5, starting transfers between devices, both_ways(): lax.ppermute(to_last, axis, [((i + 1) % count, i) for i in range(ends)])  11.7 us
    ppermute x3, starting transfers between devices, gathered(): other = lax.ppermute(rows, axis, [(i, i ^ bit) for i in range(count)])  10.6 us
    unnamed x30, local copies, waits for them, and re-layouts  9.35 us
    pallas_call x1, Pallas kernels, make_bands(): pl.pallas_call(bands_kernel, out_shape=[jax.ShapeDtypeStruct(shape, jnp.b...  6.58 us
    ppermute x5, waiting for transfers between devices, both_ways(): lax.ppermute(to_next, axis, [(i, (i + 1) % count) for i in range(ends)])  5.08 us
    ppermute x5, waiting for transfers between devices, both_ways(): lax.ppermute(to_last, axis, [((i + 1) % count, i) for i in range(ends)])  3.39 us
  transfers between devices with their start and end apart: 13, of which 4 were waited for; matrix products, arithmetic and copies ran while one was open for 1% of the time, Pallas kernels for 8%

profile of v4, /device:TPU:71, one launch (start us, length us, event | category | flops | bytes accessed | tf_op | source)
XLA Modules:
  0.0 126.7 jit_solution(15267719026608535742)
XLA Ops:
  0.0 2.6 %collective-permute-start.10 = (bf16[4,1536]{1,0:T(4,128)(2,1)}, bf16[4,1536]{1,0:T(4,128)(2,1)S(1)}, u32[]{:S(2)}, u32[]{:S(2)}) collective-permute-start(bf16[4,1536]{1,0:T(4,128)(2,1)} %param.10), channel_id=1, source_target_pairs={{0,8},{8,0},{16,24},{24,16},{32,40},{40,32},{48,56},{56,48},{1,9},... | collective-permute-start | bytes 36872 | tf_op jit(solution)/shard_map/ppermute | solution.py:283
  2.6 1.0 collective-permute-done.10
  3.6 0.7 broadcast_select_fusion.5
  4.4 3.2 %collective-permute-start.11 = (bf16[8,1536]{1,0:T(8,128)(2,1)S(1)}, bf16[8,1536]{1,0:T(8,128)(2,1)S(1)}, u32[]{:S(2)}, u32[]{:S(2)}) collective-permute-start(bf16[8,1536]{1,0:T(8,128)(2,1)S(1)} %pad_maximum_fusion.2), channel_id=1, source_target_pairs={{0,16},{8,24},{16,0},{24,8},{32,48},{40,56},{48,32},{56,40},{1,17}... | collective-permute-start | bytes 73736 | tf_op jit(solution)/shard_map/ppermute | solution.py:283
  7.6 2.7 %shard_map.73 = (bf16[20,80,128]{2,1,0:T(8,128)(2,1)}, bf16[20,64,128]{2,1,0:T(8,128)(2,1)}, bf16[20,64,128]{2,1,0:T(8,128)(2,1)}, bf16[5,80,128]{2,1,0:T(8,128)(2,1)}, bf16[5,80,128]{2,1,0:T(8,128)(2,1)}) custom-call(f32[40,40,128]{2,1,0:T(8,128)} %reflect_ref.1), custom_call_target="tpu_custom_call" | custom-call | tf_op jit(solution)/shard_map/pallas_call | solution.py:330
  10.2 13.5 %collective-permute-start.4 = (bf16[5,80,128]{2,1,0:T(8,128)(2,1)}, bf16[5,80,128]{2,1,0:T(8,128)(2,1)S(1)}, u32[]{:S(2)}, u32[]{:S(2)}) collective-permute-start(bf16[5,80,128]{2,1,0:T(8,128)(2,1)} %get-tuple-element.29), channel_id=1, source_target_pairs={{0,1},{1,2},{2,3},{3,4},{4,5},{5,6},{6,7},{8,9},{9,10},{10,11},{11... | collective-permute-start | bytes 307208 | tf_op jit(solution)/shard_map/ppermute | solution.py:296
  23.8 1.9 %collective-permute-start.5 = (bf16[5,80,128]{2,1,0:T(8,128)(2,1)}, bf16[5,80,128]{2,1,0:T(8,128)(2,1)S(1)}, u32[]{:S(2)}, u32[]{:S(2)}) collective-permute-start(bf16[5,80,128]{2,1,0:T(8,128)(2,1)} %get-tuple-element.30), channel_id=1, source_target_pairs={{1,0},{2,1},{3,2},{4,3},{5,4},{6,5},{7,6},{9,8},{10,9},{11,10},{12... | collective-permute-start | bytes 307208 | tf_op jit(solution)/shard_map/ppermute | solution.py:297
  25.7 2.6 %collective-permute-start = (bf16[20,64,128]{2,1,0:T(8,128)(2,1)}, bf16[20,64,128]{2,1,0:T(8,128)(2,1)S(1)}, u32[]{:S(2)}, u32[]{:S(2)}) collective-permute-start(bf16[20,64,128]{2,1,0:T(8,128)(2,1)} %get-tuple-element.23), channel_id=1, source_target_pairs={{0,64},{64,128},{128,192},{192,256},{256,320},{320,384},{384,448},... | collective-permute-start | bytes 983048 | tf_op jit(solution)/shard_map/ppermute | solution.py:296
  28.4 2.6 %collective-permute-start.1 = (bf16[20,64,128]{2,1,0:T(8,128)(2,1)}, bf16[20,64,128]{2,1,0:T(8,128)(2,1)S(1)}, u32[]{:S(2)}, u32[]{:S(2)}) collective-permute-start(bf16[20,64,128]{2,1,0:T(8,128)(2,1)} %get-tuple-element.25), channel_id=1, source_target_pairs={{64,0},{128,64},{192,128},{256,192},{320,256},{384,320},{448,384},... | collective-permute-start | bytes 983048 | tf_op jit(solution)/shard_map/ppermute | solution.py:297
  31.0 0.0 collective-permute-done.11
  31.0 5.1 %collective-permute-done.before_ref = bf16[20,64,128]{2,1,0:T(8,128)(2,1)S(1)} collective-permute-done((bf16[20,64,128]{2,1,0:T(8,128)(2,1)}, bf16[20,64,128]{2,1,0:T(8,128)(2,1)S(1)}, u32[]{:S(2)}, u32[]{:S(2)}) %collective-permute-start) | collective-permute-done | bytes 327712 | tf_op jit(solution)/shard_map/ppermute | solution.py:296
  36.1 2.4 %collective-permute-done.1.after_ref = bf16[20,64,128]{2,1,0:T(8,128)(2,1)S(1)} collective-permute-done((bf16[20,64,128]{2,1,0:T(8,128)(2,1)}, bf16[20,64,128]{2,1,0:T(8,128)(2,1)S(1)}, u32[]{:S(2)}, u32[]{:S(2)}) %collective-permute-start.1) | collective-permute-done | bytes 327712 | tf_op jit(solution)/shard_map/ppermute | solution.py:297
  38.5 0.0 copy-start.6
  38.5 1.0 copy-done.6
  39.5 0.0 copy-start.9
  39.5 0.2 shard_map.74
  39.7 0.0 copy-start
  39.7 1.0 copy-done
  40.6 0.0 copy-start.8
  40.7 0.0 collective-permute-done.4.left_ref
  40.7 0.0 copy-start.13
  40.7 1.0 collective-permute-done.5.right_ref
  41.7 0.0 copy-start.14
  41.7 0.0 copy-done.13
  41.7 0.6 copy-done.14
  42.3 2.0 %shard_map.75 = (bf16[10,80,128]{2,1,0:T(8,128)(2,1)}, bf16[10,64,128]{2,1,0:T(8,128)(2,1)}, bf16[10,64,128]{2,1,0:T(8,128)(2,1)}) custom-call(bf16[5,80,128]{2,1,0:T(8,128)(2,1)} %copy-done.13, bf16[5,80,128]{2,1,0:T(8,128)(2,1)} %copy-done.14, bf16[20,208,128]{2,1,0:T(8,128)(2,1)} %copy-done), custom_call_target="tpu_custom_call" | custom-call | tf_op jit(solution)/shard_map/pallas_call | solution.py:361
  44.3 5.9 %collective-permute-start.6 = (bf16[10,64,128]{2,1,0:T(8,128)(2,1)}, bf16[10,64,128]{2,1,0:T(8,128)(2,1)S(1)}, u32[]{:S(2)}, u32[]{:S(2)}) collective-permute-start(bf16[10,64,128]{2,1,0:T(8,128)(2,1)} %get-tuple-element.31), channel_id=1, source_target_pairs={{0,64},{64,128},{128,192},{192,256},{256,320},{320,384},{384,448},... | collective-permute-start | bytes 491528 | tf_op jit(solution)/shard_map/ppermute | solution.py:296
  50.2 3.3 %collective-permute-start.7 = (bf16[10,64,128]{2,1,0:T(8,128)(2,1)}, bf16[10,64,128]{2,1,0:T(8,128)(2,1)S(1)}, u32[]{:S(2)}, u32[]{:S(2)}) collective-permute-start(bf16[10,64,128]{2,1,0:T(8,128)(2,1)} %get-tuple-element.33), channel_id=1, source_target_pairs={{64,0},{128,64},{192,128},{256,192},{320,256},{384,320},{448,384},... | collective-permute-start | bytes 491528 | tf_op jit(solution)/shard_map/ppermute | solution.py:297
  53.5 5.6 %collective-permute-start.2 = (bf16[16,208,128]{2,1,0:T(8,128)(2,1)S(1)}, bf16[16,208,128]{2,1,0:T(8,128)(2,1)S(1)}, u32[]{:S(2)}, u32[]{:S(2)}) collective-permute-start(bf16[16,208,128]{2,1,0:T(8,128)(2,1)S(1)} %get-tuple-element.26), channel_id=1, source_target_pairs={{0,8},{8,16},{16,24},{24,32},{32,40},{40,48},{48,56},{1,9},{9,17},... | collective-permute-start | bytes 2555912 | tf_op jit(solution)/shard_map/ppermute | solution.py:296
  59.0 1.9 %collective-permute-start.3 = (bf16[16,208,128]{2,1,0:T(8,128)(2,1)S(1)}, bf16[16,208,128]{2,1,0:T(8,128)(2,1)}, u32[]{:S(2)}, u32[]{:S(2)}) collective-permute-start(bf16[16,208,128]{2,1,0:T(8,128)(2,1)S(1)} %get-tuple-element.28), channel_id=1, source_target_pairs={{8,0},{16,8},{24,16},{32,24},{40,32},{48,40},{56,48},{9,1},{17,9},... | collective-permute-start | bytes 2555912 | tf_op jit(solution)/shard_map/ppermute | solution.py:297
  61.0 4.8 %collective-permute-start.12 = (bf16[16,1536]{1,0:T(8,128)(2,1)S(1)}, bf16[16,1536]{1,0:T(8,128)(2,1)S(1)}, u32[]{:S(2)}, u32[]{:S(2)}) collective-permute-start(bf16[16,1536]{1,0:T(8,128)(2,1)S(1)} %pad_maximum_fusion.1), channel_id=1, source_target_pairs={{0,32},{8,40},{16,48},{24,56},{32,0},{40,8},{48,16},{56,24},{1,33}... | collective-permute-start | bytes 147464 | tf_op jit(solution)/shard_map/ppermute | solution.py:283
  65.8 0.0 copy-done.9
  65.8 0.6 fusion
  66.4 0.0 collective-permute-done.6.before_ref
  66.4 0.0 collective-permute-done.7.after_ref
  66.4 0.0 copy-start.7
  66.4 0.9 copy-done.7
  67.4 0.1 shard_map.76
  67.5 0.0 copy-start.5
  67.5 0.8 copy-done.5
  68.3 3.3 %collective-permute-start.8 = (bf16[8,208,128]{2,1,0:T(8,128)(2,1)S(1)}, bf16[8,208,128]{2,1,0:T(8,128)(2,1)S(1)}, u32[]{:S(2)}, u32[]{:S(2)}) collective-permute-start(bf16[8,208,128]{2,1,0:T(8,128)(2,1)S(1)} %get-tuple-element.34), channel_id=1, source_target_pairs={{0,8},{8,16},{16,24},{24,32},{32,40},{40,48},{48,56},{1,9},{9,17},... | collective-permute-start | bytes 1277960 | tf_op jit(solution)/shard_map/ppermute | solution.py:296
  71.6 1.9 %collective-permute-start.9 = (bf16[8,208,128]{2,1,0:T(8,128)(2,1)S(1)}, bf16[8,208,128]{2,1,0:T(8,128)(2,1)S(1)}, u32[]{:S(2)}, u32[]{:S(2)}) collective-permute-start(bf16[8,208,128]{2,1,0:T(8,128)(2,1)S(1)} %get-tuple-element.36), channel_id=1, source_target_pairs={{8,0},{16,8},{24,16},{32,24},{40,32},{48,40},{56,48},{9,1},{17,9},... | collective-permute-start | bytes 1277960 | tf_op jit(solution)/shard_map/ppermute | solution.py:297
  73.6 0.0 collective-permute-done.12
  73.6 0.0 copy-done.8
  73.6 6.6 %shard_map.77 = (bf16[3,640,208]{2,1,0:T(8,128)(2,1)S(1)}, bf16[24,32,416]{2,1,0:T(8,128)(2,1)S(1)}, bf16[24,32,416]{2,1,0:T(8,128)(2,1)S(1)}, bf16[3,1536,128]{2,1,0:T(8,128)(2,1)S(1)}) custom-call(s32[3]{0:T(128)S(1)} %bitcast.3, bf16[32,1536]{1,0:T(8,128)(2,1)S(1)} %pad_maximum_fusion.table_ref, bf16[128,384]{1,0:T(8,128)(2,1)S(1)} %copy-done.8), custom_call_target="tpu_custom_call" | custom-call | tf_op jit(solution)/shard_map/pallas_call | solution.py:152
  80.2 0.0 copy-start.1
  80.2 1.0 copy-done.1
  81.2 0.0 copy-start.2
  81.3 1.0 copy-done.2
  82.2 0.0 copy-start.3
  82.2 0.9 copy-done.3
  83.1 0.0 copy-start.4
  83.1 0.9 copy-done.4
  84.0 0.0 collective-permute-done.8.left_tail
  84.0 0.0 copy-start.11
  84.0 0.0 collective-permute-done.9.right_tail
  84.0 0.0 copy-start.12
  84.0 0.0 collective-permute-done.2.left_ref
  84.0 0.0 copy-start.10
  84.1 0.0 collective-permute-done.3.right_ref
  84.1 0.7 copy-done.11
  84.8 0.2 copy-done.12
  85.0 0.3 copy-done.10
  85.3 41.4 %shard_map.78 = f32[40,40,128]{2,1,0:T(8,128)} custom-call(s32[1]{0:T(128)} %bitcast.1.live_ref, bf16[16,208,128]{2,1,0:T(8,128)(2,1)} %copy-done.10, bf16[20,208,128]{2,1,0:T(8,128)(2,1)} %copy-done, bf16[16,208,128]{2,1,0:T(8,128)(2,1)} %collective-permute-done.3.right_ref, bf16[8,208,128]{2,1,0:T(8,128)(2,1)} %copy-done.11, ...), custom_call_target="tpu_custom_call" | custom-call | tf_op jit(solution)/shard_map/pallas_call | solution.py:264
  (5 shorter events, 0.1 us)
Async XLA Ops:
  0.0 3.6 %collective-permute-start.10 = (bf16[4,1536]{1,0:T(4,128)(2,1)}, bf16[4,1536]{1,0:T(4,128)(2,1)S(1)}, u32[]{:S(2)}, u32[]{:S(2)}) collective-permute-start(bf16[4,1536]{1,0:T(4,128)(2,1)} %param.10), channel_id=1, source_target_pairs={{0,8},{8,0},{16,24},{24,16},{32,40},{40,32},{48,56},{56,48},{1,9},... | collective-permute-start | bytes 36872 | tf_op jit(solution)/shard_map/ppermute | solution.py:283
  4.4 26.7 %collective-permute-start.11 = (bf16[8,1536]{1,0:T(8,128)(2,1)S(1)}, bf16[8,1536]{1,0:T(8,128)(2,1)S(1)}, u32[]{:S(2)}, u32[]{:S(2)}) collective-permute-start(bf16[8,1536]{1,0:T(8,128)(2,1)S(1)} %pad_maximum_fusion.2), channel_id=1, source_target_pairs={{0,16},{8,24},{16,0},{24,8},{32,48},{40,56},{48,32},{56,40},{1,17}... | collective-permute-start | bytes 73736 | tf_op jit(solution)/shard_map/ppermute | solution.py:283
  10.2 30.4 %collective-permute-start.4 = (bf16[5,80,128]{2,1,0:T(8,128)(2,1)}, bf16[5,80,128]{2,1,0:T(8,128)(2,1)S(1)}, u32[]{:S(2)}, u32[]{:S(2)}) collective-permute-start(bf16[5,80,128]{2,1,0:T(8,128)(2,1)} %get-tuple-element.29), channel_id=1, source_target_pairs={{0,1},{1,2},{2,3},{3,4},{4,5},{5,6},{6,7},{8,9},{9,10},{10,11},{11... | collective-permute-start | bytes 307208 | tf_op jit(solution)/shard_map/ppermute | solution.py:296
  23.8 17.9 %collective-permute-start.5 = (bf16[5,80,128]{2,1,0:T(8,128)(2,1)}, bf16[5,80,128]{2,1,0:T(8,128)(2,1)S(1)}, u32[]{:S(2)}, u32[]{:S(2)}) collective-permute-start(bf16[5,80,128]{2,1,0:T(8,128)(2,1)} %get-tuple-element.30), channel_id=1, source_target_pairs={{1,0},{2,1},{3,2},{4,3},{5,4},{6,5},{7,6},{9,8},{10,9},{11,10},{12... | collective-permute-start | bytes 307208 | tf_op jit(solution)/shard_map/ppermute | solution.py:297
  25.7 10.4 %collective-permute-start = (bf16[20,64,128]{2,1,0:T(8,128)(2,1)}, bf16[20,64,128]{2,1,0:T(8,128)(2,1)S(1)}, u32[]{:S(2)}, u32[]{:S(2)}) collective-permute-start(bf16[20,64,128]{2,1,0:T(8,128)(2,1)} %get-tuple-element.23), channel_id=1, source_target_pairs={{0,64},{64,128},{128,192},{192,256},{256,320},{320,384},{384,448},... | collective-permute-start | bytes 983048 | tf_op jit(solution)/shard_map/ppermute | solution.py:296
  28.4 10.1 %collective-permute-start.1 = (bf16[20,64,128]{2,1,0:T(8,128)(2,1)}, bf16[20,64,128]{2,1,0:T(8,128)(2,1)S(1)}, u32[]{:S(2)}, u32[]{:S(2)}) collective-permute-start(bf16[20,64,128]{2,1,0:T(8,128)(2,1)} %get-tuple-element.25), channel_id=1, source_target_pairs={{64,0},{128,64},{192,128},{256,192},{320,256},{384,320},{448,384},... | collective-permute-start | bytes 983048 | tf_op jit(solution)/shard_map/ppermute | solution.py:297
  38.5 1.0 copy-start.6
  39.5 26.3 %copy-start.9 = (s32[1,1,1,3]{3,2,1,0:T(1,128)S(1)}, s32[1,1,1,3]{3,2,1,0:T(1,128)}, u32[]{:S(2)}) copy-start(s32[1,1,1,3]{3,2,1,0:T(1,128)} %param.11) | copy-start | bytes 40
  39.7 1.0 copy-start
  40.6 33.0 %copy-start.8 = (bf16[128,384]{1,0:T(8,128)(2,1)S(1)}, bf16[128,384]{1,0:T(8,128)(2,1)}, u32[]{:S(2)}) copy-start(bf16[128,384]{1,0:T(8,128)(2,1)} %constant.18.clone.map_ref) | copy-start | bytes 294916
  40.7 1.0 copy-start.13
  41.7 0.6 copy-start.14
  44.3 22.1 %collective-permute-start.6 = (bf16[10,64,128]{2,1,0:T(8,128)(2,1)}, bf16[10,64,128]{2,1,0:T(8,128)(2,1)S(1)}, u32[]{:S(2)}, u32[]{:S(2)}) collective-permute-start(bf16[10,64,128]{2,1,0:T(8,128)(2,1)} %get-tuple-element.31), channel_id=1, source_target_pairs={{0,64},{64,128},{128,192},{192,256},{256,320},{320,384},{384,448},... | collective-permute-start | bytes 491528 | tf_op jit(solution)/shard_map/ppermute | solution.py:296
  50.2 16.3 %collective-permute-start.7 = (bf16[10,64,128]{2,1,0:T(8,128)(2,1)}, bf16[10,64,128]{2,1,0:T(8,128)(2,1)S(1)}, u32[]{:S(2)}, u32[]{:S(2)}) collective-permute-start(bf16[10,64,128]{2,1,0:T(8,128)(2,1)} %get-tuple-element.33), channel_id=1, source_target_pairs={{64,0},{128,64},{192,128},{256,192},{320,256},{384,320},{448,384},... | collective-permute-start | bytes 491528 | tf_op jit(solution)/shard_map/ppermute | solution.py:297
  53.5 30.6 %collective-permute-start.2 = (bf16[16,208,128]{2,1,0:T(8,128)(2,1)S(1)}, bf16[16,208,128]{2,1,0:T(8,128)(2,1)S(1)}, u32[]{:S(2)}, u32[]{:S(2)}) collective-permute-start(bf16[16,208,128]{2,1,0:T(8,128)(2,1)S(1)} %get-tuple-element.26), channel_id=1, source_target_pairs={{0,8},{8,16},{16,24},{24,32},{32,40},{40,48},{48,56},{1,9},{9,17},... | collective-permute-start | bytes 2555912 | tf_op jit(solution)/shard_map/ppermute | solution.py:296
  59.0 25.0 %collective-permute-start.3 = (bf16[16,208,128]{2,1,0:T(8,128)(2,1)S(1)}, bf16[16,208,128]{2,1,0:T(8,128)(2,1)}, u32[]{:S(2)}, u32[]{:S(2)}) collective-permute-start(bf16[16,208,128]{2,1,0:T(8,128)(2,1)S(1)} %get-tuple-element.28), channel_id=1, source_target_pairs={{8,0},{16,8},{24,16},{32,24},{40,32},{48,40},{56,48},{9,1},{17,9},... | collective-permute-start | bytes 2555912 | tf_op jit(solution)/shard_map/ppermute | solution.py:297
  61.0 12.6 %collective-permute-start.12 = (bf16[16,1536]{1,0:T(8,128)(2,1)S(1)}, bf16[16,1536]{1,0:T(8,128)(2,1)S(1)}, u32[]{:S(2)}, u32[]{:S(2)}) collective-permute-start(bf16[16,1536]{1,0:T(8,128)(2,1)S(1)} %pad_maximum_fusion.1), channel_id=1, source_target_pairs={{0,32},{8,40},{16,48},{24,56},{32,0},{40,8},{48,16},{56,24},{1,33}... | collective-permute-start | bytes 147464 | tf_op jit(solution)/shard_map/ppermute | solution.py:283
  66.4 0.9 copy-start.7
  67.5 0.8 copy-start.5
  68.3 15.7 %collective-permute-start.8 = (bf16[8,208,128]{2,1,0:T(8,128)(2,1)S(1)}, bf16[8,208,128]{2,1,0:T(8,128)(2,1)S(1)}, u32[]{:S(2)}, u32[]{:S(2)}) collective-permute-start(bf16[8,208,128]{2,1,0:T(8,128)(2,1)S(1)} %get-tuple-element.34), channel_id=1, source_target_pairs={{0,8},{8,16},{16,24},{24,32},{32,40},{40,48},{48,56},{1,9},{9,17},... | collective-permute-start | bytes 1277960 | tf_op jit(solution)/shard_map/ppermute | solution.py:296
  71.6 12.4 %collective-permute-start.9 = (bf16[8,208,128]{2,1,0:T(8,128)(2,1)S(1)}, bf16[8,208,128]{2,1,0:T(8,128)(2,1)S(1)}, u32[]{:S(2)}, u32[]{:S(2)}) collective-permute-start(bf16[8,208,128]{2,1,0:T(8,128)(2,1)S(1)} %get-tuple-element.36), channel_id=1, source_target_pairs={{8,0},{16,8},{24,16},{32,24},{40,32},{48,40},{56,48},{9,1},{17,9},... | collective-permute-start | bytes 1277960 | tf_op jit(solution)/shard_map/ppermute | solution.py:297
  80.2 1.0 copy-start.1
  81.2 1.0 copy-start.2
  82.2 0.9 copy-start.3
  83.1 0.9 copy-start.4
  84.0 0.8 copy-start.11
  84.0 0.9 copy-start.12
  84.0 1.2 copy-start.10

commit v5 on v4

--- a/solution.py
+++ b/solution.py
@@ -168,7 +168,7 @@
 
 
 def blur_kernel(
-    live_ref, left_ref, own_ref, right_ref, left_tail, own_tail, right_tail, a1_ref, a2_ref, a2b_ref, mask_ref, bz_ref,
+    live_ref, left_ref, own_ref, right_ref, a1_ref, a2_ref, a2b_ref, mask_ref, bz_ref,
     weights_ref, slot_ref, out_ref, line_x, line_y, band_y,
 ):
     out_ref[...] = jnp.zeros_like(out_ref)
@@ -177,11 +177,13 @@
     low_b = lax.broadcasted_iota(jnp.int32, ((Y - TOP) * XO, NARROW), 1) < 64
 
     def one_slot(slot, carry):
-        def stage_x(part, tail, offset):
+        def stage_x(part, offset):
+            pairs = part.shape[0] * 2 // 3
+
             def step(i, carry):
                 g = 2 * i
                 rhs = jnp.concatenate(
-                    [part[4 * i], part[4 * i + 1], part[4 * i + 2], part[4 * i + 3], tail[g], tail[g + 1]],
+                    [part[4 * i], part[4 * i + 1], part[4 * i + 2], part[4 * i + 3], part[pairs + g], part[pairs + g + 1]],
                     axis=1,
                 )
                 made = jnp.dot(a1_ref[slot], rhs, preferred_element_type=jnp.float32)
@@ -209,11 +211,11 @@
                             )
                 return carry
 
-            lax.fori_loop(0, part.shape[0] // 4, step, 0)
-
-        stage_x(left_ref, left_tail, 0)
-        stage_x(own_ref, own_tail, 8)
-        stage_x(right_ref, right_tail, 18)
+            lax.fori_loop(0, pairs // 4, step, 0)
+
+        stage_x(left_ref, 0)
+        stage_x(own_ref, 8)
+        stage_x(right_ref, 18)
 
         def pair(q, carry):
             made = []
@@ -264,14 +266,14 @@
     return pl.pallas_call(
         blur_kernel,
         out_shape=jax.ShapeDtypeStruct((X, Y, Z), jnp.float32),
-        in_specs=[pl.BlockSpec(memory_space=pltpu.SMEM)] + [vmem] * 13,
+        in_specs=[pl.BlockSpec(memory_space=pltpu.SMEM)] + [vmem] * 10,
         out_specs=vmem,
         scratch_shapes=[
             pltpu.VMEM((R, EXT * XO, LANES), jnp.bfloat16),
             pltpu.VMEM((1600, 1536), jnp.bfloat16),
             pltpu.VMEM((2, Y * XO, EXT * XO), jnp.bfloat16),
         ],
-        compiler_params=pltpu.CompilerParams(vmem_limit_bytes=60 * 1024 * 1024),
+        compiler_params=pltpu.CompilerParams(vmem_limit_bytes=40 * 1024 * 1024),
     )(live, *cells, a1, a2, a2b, mask, bz, weights, cell_slot)
 
 
@@ -292,10 +294,9 @@
 def both_ways(to_next, to_last, axis):
     count = lax.axis_size(axis)
     ends = count - 1
-    return (
-        lax.ppermute(to_next, axis, [(i, (i + 1) % count) for i in range(ends)]),
-        lax.ppermute(to_last, axis, [((i + 1) % count, i) for i in range(ends)]),
-    )
+    after = lax.ppermute(to_last, axis, [((i + 1) % count, i) for i in range(ends)])
+    before = lax.ppermute(to_next, axis, [(i, (i + 1) % count) for i in range(ends)])
+    return before, after
 
 
 def lane_part():
@@ -335,8 +336,10 @@
     )(reflect)
 
 
-def tail_kernel(left_ref, right_ref, after_ref, own_ref, next_ref, last_ref):
+def tail_kernel(left_ref, right_ref, main_next, main_last, own_ref, next_ref, last_ref):
     part = lane_part()
+    next_ref[:20] = main_next[...]
+    last_ref[:20] = main_last[...]
     for g in range(5):
         left = left_ref[g].astype(jnp.float32)
         right = right_ref[g].astype(jnp.float32)
@@ -347,59 +350,62 @@
                 turned = pltpu.roll(source, shift, 1) if shift else source
                 value = jnp.where(part == k, turned, value)
             own_ref[2 * g + a] = value.astype(jnp.bfloat16)
-            next_ref[2 * g + a] = jnp.concatenate(
+            next_ref[20 + 2 * g + a] = jnp.concatenate(
                 [value[X - HALF : X], value[2 * X - HALF :]], axis=0
             ).astype(jnp.bfloat16)
-            last_ref[2 * g + a] = jnp.concatenate(
+            last_ref[20 + 2 * g + a] = jnp.concatenate(
                 [value[:HALF], value[X : X + HALF]], axis=0
             ).astype(jnp.bfloat16)
 
 
-def unpack_tail(left, right, after):
-    shapes = [(10, 80, NARROW), (10, 64, NARROW), (10, 64, NARROW)]
+def unpack_tail(left, right, main_next, main_last):
+    shapes = [(10, 80, NARROW), (30, 64, NARROW), (30, 64, NARROW)]
     vmem = pl.BlockSpec(memory_space=pltpu.VMEM)
     return pl.pallas_call(
         tail_kernel,
         out_shape=[jax.ShapeDtypeStruct(shape, jnp.bfloat16) for shape in shapes],
-        in_specs=[vmem, vmem, pl.BlockSpec(memory_space=pl.ANY)],
+        in_specs=[vmem] * 4,
         out_specs=[vmem] * 3,
-    )(left, right, after)
-
-
-def join_kernel(before_ref, own_ref, after_ref, all_ref, next_ref, last_ref):
-    count = own_ref.shape[0]
-    edge = next_ref.shape[0]
-    for ref, start in ((all_ref, 0), (next_ref, count - edge), (last_ref, 0)):
-        rows = slice(start, start + ref.shape[0])
-        ref[:, 0:64, :] = before_ref[rows]
-        ref[:, 64:144, :] = own_ref[rows]
-        ref[:, 144:208, :] = after_ref[rows]
-
-
-def join(before, own, after):
-    count = own.shape[0]
-    counts = (count, count * 4 // 5, count * 4 // 5)
+    )(left, right, main_next, main_last)
+
+
+def join_kernel(before_ref, own_ref, tail_ref, after_ref, all_ref, next_ref, last_ref):
+    for ref, to, at, count in (
+        (all_ref, 0, 0, 30),
+        (next_ref, 0, 4, 16),
+        (next_ref, 16, 22, 8),
+        (last_ref, 0, 0, 16),
+        (last_ref, 16, 20, 8),
+    ):
+        ref[to : to + count, 0:64, :] = before_ref[at : at + count]
+        ref[to : to + count, 144:208, :] = after_ref[at : at + count]
+        mains = min(max(20 - at, 0), count)
+        if mains:
+            ref[to : to + mains, 64:144, :] = own_ref[at : at + mains]
+        if count > mains:
+            first = max(at - 20, 0)
+            ref[to + mains : to + count, 64:144, :] = tail_ref[first : first + count - mains]
+
+
+def join(before, own, tail, after):
     vmem = pl.BlockSpec(memory_space=pltpu.VMEM)
     return pl.pallas_call(
         join_kernel,
-        out_shape=[jax.ShapeDtypeStruct((n, ROWS, NARROW), jnp.bfloat16) for n in counts],
-        in_specs=[vmem] * 3,
+        out_shape=[jax.ShapeDtypeStruct((n, ROWS, NARROW), jnp.bfloat16) for n in (30, 24, 24)],
+        in_specs=[vmem] * 4,
         out_specs=[vmem] * 3,
-        compiler_params=pltpu.CompilerParams(vmem_limit_bytes=32 * 1024 * 1024),
-    )(before, own, after)
+        compiler_params=pltpu.CompilerParams(vmem_limit_bytes=24 * 1024 * 1024),
+    )(before, own, tail, after)
 
 
 def halo(reflect):
     own, to_next, to_last, deeper, shallower = cut(reflect)
     above, below = both_ways(deeper, shallower, "gz")
+    tail, to_next, to_last = unpack_tail(above, below, to_next, to_last)
     before, after = both_ways(to_next, to_last, "il")
-    main, to_next, to_last = join(before, own, after)
+    block, to_next, to_last = join(before, own, tail, after)
     left, right = both_ways(to_next, to_last, "xl")
-    tail, to_next, to_last = unpack_tail(above, below, main)
-    before, after = both_ways(to_next, to_last, "il")
-    tail, to_next, to_last = join(before, tail, after)
-    left_tail, right_tail = both_ways(to_next, to_last, "xl")
-    return left, main, right, left_tail, tail, right_tail
+    return left, block, right
 
 
 def per_device(reflect, weights, cell_slot, factors, reader_list):

time: 127 us -> 137 us (1.079)
  the two profiles are of different devices: /device:TPU:71 before, /device:TPU:78 now
where the time goes in v5:
time: 137 us; the launch traced here: 136 us
  Pallas kernels  52.6 us (38%)
  starting transfers between devices  39.3 us (29%)
  waiting for transfers between devices  36 us (26%)
  local copies, waits for them, and re-layouts  7.35 us (5%)
    pallas_call x1, Pallas kernels, blur(): pl.pallas_call(blur_kernel, out_shape=jax.ShapeDtypeStruct((X, Y, Z), jnp...  39.1 us
    ppermute x3, starting transfers between devices, both_ways(): lax.ppermute(to_next, axis, [(i, (i + 1) % count) for i in range(ends)])  21.3 us
    ppermute x3, waiting for transfers between devices, both_ways(): lax.ppermute(to_last, axis, [((i + 1) % count, i) for i in range(ends)])  15.5 us
    ppermute x3, waiting for transfers between devices, gathered(): other = lax.ppermute(rows, axis, [(i, i ^ bit) for i in range(count)])  13.8 us
    ppermute x3, starting transfers between devices, both_ways(): lax.ppermute(to_last, axis, [((i + 1) % count, i) for i in range(ends)])  9.57 us
    ppermute x3, starting transfers between devices, gathered(): other = lax.ppermute(rows, axis, [(i, i ^ bit) for i in range(count)])  8.48 us
    unnamed x28, local copies, waits for them, and re-layouts  7.35 us
    ppermute x3, waiting for transfers between devices, both_ways(): lax.ppermute(to_next, axis, [(i, (i + 1) % count) for i in range(ends)])  6.73 us
  transfers between devices with their start and end apart: 9, of which 5 were waited for; matrix products, arithmetic and copies ran while one was open for 1% of the time, Pallas kernels for 8%

profile of v5, /device:TPU:78, one launch (start us, length us, event | category | flops | bytes accessed | tf_op | source)
XLA Modules:
  0.0 136.3 jit_solution(18432856890304368428)
XLA Ops:
  0.0 0.0 copy-start.13
  0.0 2.7 %shard_map.73 = (bf16[20,80,128]{2,1,0:T(8,128)(2,1)}, bf16[20,64,128]{2,1,0:T(8,128)(2,1)}, bf16[20,64,128]{2,1,0:T(8,128)(2,1)}, bf16[5,80,128]{2,1,0:T(8,128)(2,1)}, bf16[5,80,128]{2,1,0:T(8,128)(2,1)}) custom-call(f32[40,40,128]{2,1,0:T(8,128)} %reflect_ref.1), custom_call_target="tpu_custom_call" | custom-call | tf_op jit(solution)/shard_map/pallas_call | solution.py:331
  2.7 13.8 %collective-permute-start = (bf16[5,80,128]{2,1,0:T(8,128)(2,1)}, bf16[5,80,128]{2,1,0:T(8,128)(2,1)S(1)}, u32[]{:S(2)}, u32[]{:S(2)}) collective-permute-start(bf16[5,80,128]{2,1,0:T(8,128)(2,1)} %get-tuple-element.20), channel_id=1, source_target_pairs={{0,1},{1,2},{2,3},{3,4},{4,5},{5,6},{6,7},{8,9},{9,10},{10,11},{11... | collective-permute-start | bytes 307208 | tf_op jit(solution)/shard_map/ppermute | solution.py:298
  16.5 1.9 %collective-permute-start.1 = (bf16[5,80,128]{2,1,0:T(8,128)(2,1)}, bf16[5,80,128]{2,1,0:T(8,128)(2,1)S(1)}, u32[]{:S(2)}, u32[]{:S(2)}) collective-permute-start(bf16[5,80,128]{2,1,0:T(8,128)(2,1)} %get-tuple-element.21), channel_id=1, source_target_pairs={{1,0},{2,1},{3,2},{4,3},{5,4},{6,5},{7,6},{9,8},{10,9},{11,10},{12... | collective-permute-start | bytes 307208 | tf_op jit(solution)/shard_map/ppermute | solution.py:297
  18.4 1.9 %collective-permute-start.6 = (bf16[4,1536]{1,0:T(4,128)(2,1)}, bf16[4,1536]{1,0:T(4,128)(2,1)S(1)}, u32[]{:S(2)}, u32[]{:S(2)}) collective-permute-start(bf16[4,1536]{1,0:T(4,128)(2,1)} %param.10), channel_id=1, source_target_pairs={{0,8},{8,0},{16,24},{24,16},{32,40},{40,32},{48,56},{56,48},{1,9},... | collective-permute-start | bytes 36872 | tf_op jit(solution)/shard_map/ppermute | solution.py:285
  20.4 0.8 collective-permute-done.left_ref
  21.1 0.0 copy-start.11
  21.1 15.0 %collective-permute-done.1.right_ref = bf16[5,80,128]{2,1,0:T(8,128)(2,1)S(1)} collective-permute-done((bf16[5,80,128]{2,1,0:T(8,128)(2,1)}, bf16[5,80,128]{2,1,0:T(8,128)(2,1)S(1)}, u32[]{:S(2)}, u32[]{:S(2)}) %collective-permute-start.1) | collective-permute-done | bytes 102432 | tf_op jit(solution)/shard_map/ppermute | solution.py:297
  36.1 0.0 copy-start.12
  36.1 0.0 copy-done.11
  36.1 0.6 copy-done.12
  36.7 0.0 copy-start.10
  36.7 0.0 copy-start.8
  36.7 0.0 copy-start.9
  36.7 2.5 %shard_map.74 = (bf16[10,80,128]{2,1,0:T(8,128)(2,1)}, bf16[30,64,128]{2,1,0:T(8,128)(2,1)}, bf16[30,64,128]{2,1,0:T(8,128)(2,1)}) custom-call(bf16[5,80,128]{2,1,0:T(8,128)(2,1)} %copy-done.11, bf16[5,80,128]{2,1,0:T(8,128)(2,1)} %copy-done.12, bf16[20,64,128]{2,1,0:T(8,128)(2,1)} %get-tuple-element.22.main_next, ...), custom_call_target="tpu_custom_call" | custom-call | tf_op jit(solution)/shard_map/pallas_call | solution.py:364
  39.2 0.0 copy-start
  39.2 5.5 %collective-permute-start.2 = (bf16[30,64,128]{2,1,0:T(8,128)(2,1)}, bf16[30,64,128]{2,1,0:T(8,128)(2,1)S(1)}, u32[]{:S(2)}, u32[]{:S(2)}) collective-permute-start(bf16[30,64,128]{2,1,0:T(8,128)(2,1)} %get-tuple-element.24), channel_id=1, source_target_pairs={{0,64},{64,128},{128,192},{192,256},{256,320},{320,384},{384,448},... | collective-permute-start | bytes 1474568 | tf_op jit(solution)/shard_map/ppermute | solution.py:298
  44.8 4.0 %collective-permute-start.3 = (bf16[30,64,128]{2,1,0:T(8,128)(2,1)}, bf16[30,64,128]{2,1,0:T(8,128)(2,1)S(1)}, u32[]{:S(2)}, u32[]{:S(2)}) collective-permute-start(bf16[30,64,128]{2,1,0:T(8,128)(2,1)} %get-tuple-element.27), channel_id=1, source_target_pairs={{64,0},{128,64},{192,128},{256,192},{320,256},{384,320},{448,384},... | collective-permute-start | bytes 1474568 | tf_op jit(solution)/shard_map/ppermute | solution.py:297
  48.8 0.0 collective-permute-done.6
  48.8 0.0 copy-done.13
  48.9 2.4 %collective-permute-start.7 = (bf16[8,1536]{1,0:T(8,128)(2,1)S(1)}, bf16[8,1536]{1,0:T(8,128)(2,1)S(1)}, u32[]{:S(2)}, u32[]{:S(2)}) collective-permute-start(bf16[8,1536]{1,0:T(8,128)(2,1)S(1)} %pad_maximum_fusion.2), channel_id=1, source_target_pairs={{0,16},{8,24},{16,0},{24,8},{32,48},{40,56},{48,32},{56,40},{1,17}... | collective-permute-start | bytes 73736 | tf_op jit(solution)/shard_map/ppermute | solution.py:285
  51.2 6.0 %collective-permute-done.2.before_ref = bf16[30,64,128]{2,1,0:T(8,128)(2,1)S(1)} collective-permute-done((bf16[30,64,128]{2,1,0:T(8,128)(2,1)}, bf16[30,64,128]{2,1,0:T(8,128)(2,1)S(1)}, u32[]{:S(2)}, u32[]{:S(2)}) %collective-permute-start.2) | collective-permute-done | bytes 491552 | tf_op jit(solution)/shard_map/ppermute | solution.py:298
  57.2 0.0 copy-start.2
  57.2 0.8 copy-done.2
  58.0 0.5 collective-permute-done.3.after_ref
  58.5 0.0 copy-start.4
  58.5 0.8 copy-done.4
  59.3 0.0 copy-start.3
  59.3 1.0 copy-done.3
  60.3 0.0 copy-start.5
  60.3 1.0 copy-done.5
  61.3 0.0 copy-start.6
  61.3 1.0 copy-done.6
  62.3 0.0 copy-start.7
  62.3 0.9 copy-done.7
  63.3 1.7 %shard_map.75 = (bf16[30,208,128]{2,1,0:T(8,128)(2,1)S(1)}, bf16[24,208,128]{2,1,0:T(8,128)(2,1)}, bf16[24,208,128]{2,1,0:T(8,128)(2,1)}) custom-call(bf16[30,64,128]{2,1,0:T(8,128)(2,1)S(1)} %copy-done.3, bf16[20,80,128]{2,1,0:T(8,128)(2,1)S(1)} %copy-done.6, bf16[10,80,128]{2,1,0:T(8,128)(2,1)S(1)} %copy-done.7, bf16[30,64,128]{2,1,0:T(8,128)(2,1)S(1)} %copy-done.5), custom_call_target="tpu_custom_call" | custom-call | tf_op jit(solution)/shard_map/pallas_call | solution.py:392
  65.0 1.9 %collective-permute-start.4 = (bf16[24,208,128]{2,1,0:T(8,128)(2,1)}, bf16[24,208,128]{2,1,0:T(8,128)(2,1)}, u32[]{:S(2)}, u32[]{:S(2)}) collective-permute-start(bf16[24,208,128]{2,1,0:T(8,128)(2,1)} %get-tuple-element.28), channel_id=1, source_target_pairs={{0,8},{8,16},{16,24},{24,32},{32,40},{40,48},{48,56},{1,9},{9,17},... | collective-permute-start | bytes 3833864 | tf_op jit(solution)/shard_map/ppermute | solution.py:298
  66.9 3.6 %collective-permute-start.5 = (bf16[24,208,128]{2,1,0:T(8,128)(2,1)}, bf16[24,208,128]{2,1,0:T(8,128)(2,1)}, u32[]{:S(2)}, u32[]{:S(2)}) collective-permute-start(bf16[24,208,128]{2,1,0:T(8,128)(2,1)} %get-tuple-element.30), channel_id=1, source_target_pairs={{8,0},{16,8},{24,16},{32,24},{40,32},{48,40},{56,48},{9,1},{17,9},... | collective-permute-start | bytes 3833864 | tf_op jit(solution)/shard_map/ppermute | solution.py:297
  70.6 0.0 collective-permute-done.7
  70.6 4.2 %collective-permute-start.8 = (bf16[16,1536]{1,0:T(8,128)(2,1)S(1)}, bf16[16,1536]{1,0:T(8,128)(2,1)S(1)}, u32[]{:S(2)}, u32[]{:S(2)}) collective-permute-start(bf16[16,1536]{1,0:T(8,128)(2,1)S(1)} %pad_maximum_fusion.1), channel_id=1, source_target_pairs={{0,32},{8,40},{16,48},{24,56},{32,0},{40,8},{48,16},{56,24},{1,33}... | collective-permute-start | bytes 147464 | tf_op jit(solution)/shard_map/ppermute | solution.py:285
  74.8 0.0 copy-done.10
  74.9 0.7 fusion
  75.6 13.8 %collective-permute-done.8 = bf16[16,1536]{1,0:T(8,128)(2,1)S(1)} collective-permute-done((bf16[16,1536]{1,0:T(8,128)(2,1)S(1)}, bf16[16,1536]{1,0:T(8,128)(2,1)S(1)}, u32[]{:S(2)}, u32[]{:S(2)}) %collective-permute-start.8) | collective-permute-done | bytes 49184 | tf_op jit(solution)/shard_map/ppermute | solution.py:285
  89.4 0.0 copy-done.8
  89.4 6.6 %shard_map.76 = (bf16[3,640,208]{2,1,0:T(8,128)(2,1)S(1)}, bf16[24,32,416]{2,1,0:T(8,128)(2,1)S(1)}, bf16[24,32,416]{2,1,0:T(8,128)(2,1)S(1)}, bf16[3,1536,128]{2,1,0:T(8,128)(2,1)S(1)}) custom-call(s32[3]{0:T(128)S(1)} %bitcast.3, bf16[32,1536]{1,0:T(8,128)(2,1)S(1)} %pad_maximum_fusion.table_ref, bf16[128,384]{1,0:T(8,128)(2,1)S(1)} %copy-done.8), custom_call_target="tpu_custom_call" | custom-call | tf_op jit(solution)/shard_map/pallas_call | solution.py:152
  96.0 0.0 collective-permute-done.4.left_ref
  96.0 0.0 collective-permute-done.5.right_ref
  96.0 0.0 copy-done.9
  96.0 0.0 copy-done
  96.0 0.0 copy-start.1
  96.0 1.1 copy-done.1
  97.2 39.1 %shard_map.77 = f32[40,40,128]{2,1,0:T(8,128)} custom-call(s32[1]{0:T(128)} %bitcast.1.live_ref, bf16[24,208,128]{2,1,0:T(8,128)(2,1)} %collective-permute-done.4.left_ref, bf16[30,208,128]{2,1,0:T(8,128)(2,1)S(1)} %get-tuple-element.29.own_ref, bf16[24,208,128]{2,1,0:T(8,128)(2,1)} %collective-permute-done.5.right_ref, ...), custom_call_target="tpu_custom_call" | custom-call | tf_op jit(solution)/shard_map/pallas_call | solution.py:266
  (6 shorter events, 0.1 us)
Async XLA Ops:
  0.0 48.8 %copy-start.13 = (bf16[4,1536]{1,0:T(4,128)(2,1)S(1)}, bf16[4,1536]{1,0:T(4,128)(2,1)}, u32[]{:S(2)}) copy-start(bf16[4,1536]{1,0:T(4,128)(2,1)} %param.10) | copy-start | bytes 36868
  2.7 18.5 %collective-permute-start = (bf16[5,80,128]{2,1,0:T(8,128)(2,1)}, bf16[5,80,128]{2,1,0:T(8,128)(2,1)S(1)}, u32[]{:S(2)}, u32[]{:S(2)}) collective-permute-start(bf16[5,80,128]{2,1,0:T(8,128)(2,1)} %get-tuple-element.20), channel_id=1, source_target_pairs={{0,1},{1,2},{2,3},{3,4},{4,5},{5,6},{6,7},{8,9},{9,10},{10,11},{11... | collective-permute-start | bytes 307208 | tf_op jit(solution)/shard_map/ppermute | solution.py:298
  16.5 19.6 %collective-permute-start.1 = (bf16[5,80,128]{2,1,0:T(8,128)(2,1)}, bf16[5,80,128]{2,1,0:T(8,128)(2,1)S(1)}, u32[]{:S(2)}, u32[]{:S(2)}) collective-permute-start(bf16[5,80,128]{2,1,0:T(8,128)(2,1)} %get-tuple-element.21), channel_id=1, source_target_pairs={{1,0},{2,1},{3,2},{4,3},{5,4},{6,5},{7,6},{9,8},{10,9},{11,10},{12... | collective-permute-start | bytes 307208 | tf_op jit(solution)/shard_map/ppermute | solution.py:297
  18.4 30.4 %collective-permute-start.6 = (bf16[4,1536]{1,0:T(4,128)(2,1)}, bf16[4,1536]{1,0:T(4,128)(2,1)S(1)}, u32[]{:S(2)}, u32[]{:S(2)}) collective-permute-start(bf16[4,1536]{1,0:T(4,128)(2,1)} %param.10), channel_id=1, source_target_pairs={{0,8},{8,0},{16,24},{24,16},{32,40},{40,32},{48,56},{56,48},{1,9},... | collective-permute-start | bytes 36872 | tf_op jit(solution)/shard_map/ppermute | solution.py:285
  21.1 15.0 %copy-start.11 = (bf16[5,80,128]{2,1,0:T(8,128)(2,1)}, bf16[5,80,128]{2,1,0:T(8,128)(2,1)S(1)}, u32[]{:S(2)}) copy-start(bf16[5,80,128]{2,1,0:T(8,128)(2,1)S(1)} %collective-permute-done.left_ref) | copy-start | bytes 307204
  36.1 0.6 copy-start.12
  36.7 38.1 %copy-start.10 = (s32[1,1,1,3]{3,2,1,0:T(1,128)S(1)}, s32[1,1,1,3]{3,2,1,0:T(1,128)}, u32[]{:S(2)}) copy-start(s32[1,1,1,3]{3,2,1,0:T(1,128)} %param.11) | copy-start | bytes 40
  36.7 52.6 %copy-start.8 = (bf16[128,384]{1,0:T(8,128)(2,1)S(1)}, bf16[128,384]{1,0:T(8,128)(2,1)}, u32[]{:S(2)}) copy-start(bf16[128,384]{1,0:T(8,128)(2,1)} %constant.18.clone.map_ref) | copy-start | bytes 294916
  36.7 59.3 %copy-start.9 = (bf16[4,416]{1,0:T(4,128)(2,1)S(1)}, bf16[4,416]{1,0:T(4,128)(2,1)}, u32[]{:S(2)}) copy-start(bf16[4,416]{1,0:T(4,128)(2,1)} %constant.19.clone.mask_ref) | copy-start | bytes 9988
  39.2 56.8 %copy-start = (s32[2,40,40,128]{3,2,1,0:T(8,128)S(1)}, s32[2,40,40,128]{3,2,1,0:T(8,128)}, u32[]{:S(2)}) copy-start(s32[2,40,40,128]{3,2,1,0:T(8,128)} %slot_ref.1) | copy-start | bytes 4915204
  39.2 18.0 %collective-permute-start.2 = (bf16[30,64,128]{2,1,0:T(8,128)(2,1)}, bf16[30,64,128]{2,1,0:T(8,128)(2,1)S(1)}, u32[]{:S(2)}, u32[]{:S(2)}) collective-permute-start(bf16[30,64,128]{2,1,0:T(8,128)(2,1)} %get-tuple-element.24), channel_id=1, source_target_pairs={{0,64},{64,128},{128,192},{192,256},{256,320},{320,384},{384,448},... | collective-permute-start | bytes 1474568 | tf_op jit(solution)/shard_map/ppermute | solution.py:298
  44.8 13.7 %collective-permute-start.3 = (bf16[30,64,128]{2,1,0:T(8,128)(2,1)}, bf16[30,64,128]{2,1,0:T(8,128)(2,1)S(1)}, u32[]{:S(2)}, u32[]{:S(2)}) collective-permute-start(bf16[30,64,128]{2,1,0:T(8,128)(2,1)} %get-tuple-element.27), channel_id=1, source_target_pairs={{64,0},{128,64},{192,128},{256,192},{320,256},{384,320},{448,384},... | collective-permute-start | bytes 1474568 | tf_op jit(solution)/shard_map/ppermute | solution.py:297
  48.9 21.7 %collective-permute-start.7 = (bf16[8,1536]{1,0:T(8,128)(2,1)S(1)}, bf16[8,1536]{1,0:T(8,128)(2,1)S(1)}, u32[]{:S(2)}, u32[]{:S(2)}) collective-permute-start(bf16[8,1536]{1,0:T(8,128)(2,1)S(1)} %pad_maximum_fusion.2), channel_id=1, source_target_pairs={{0,16},{8,24},{16,0},{24,8},{32,48},{40,56},{48,32},{56,40},{1,17}... | collective-permute-start | bytes 73736 | tf_op jit(solution)/shard_map/ppermute | solution.py:285
  57.2 0.8 copy-start.2
  58.5 0.8 copy-start.4
  59.3 1.0 copy-start.3
  60.3 1.0 copy-start.5
  61.3 1.0 copy-start.6
  62.3 0.9 copy-start.7
  65.0 31.0 %collective-permute-start.4 = (bf16[24,208,128]{2,1,0:T(8,128)(2,1)}, bf16[24,208,128]{2,1,0:T(8,128)(2,1)}, u32[]{:S(2)}, u32[]{:S(2)}) collective-permute-start(bf16[24,208,128]{2,1,0:T(8,128)(2,1)} %get-tuple-element.28), channel_id=1, source_target_pairs={{0,8},{8,16},{16,24},{24,32},{32,40},{40,48},{48,56},{1,9},{9,17},... | collective-permute-start | bytes 3833864 | tf_op jit(solution)/shard_map/ppermute | solution.py:298
  66.9 29.1 %collective-permute-start.5 = (bf16[24,208,128]{2,1,0:T(8,128)(2,1)}, bf16[24,208,128]{2,1,0:T(8,128)(2,1)}, u32[]{:S(2)}, u32[]{:S(2)}) collective-permute-start(bf16[24,208,128]{2,1,0:T(8,128)(2,1)} %get-tuple-element.30), channel_id=1, source_target_pairs={{8,0},{16,8},{24,16},{32,24},{40,32},{48,40},{56,48},{9,1},{17,9},... | collective-permute-start | bytes 3833864 | tf_op jit(solution)/shard_map/ppermute | solution.py:297
  70.6 18.7 %collective-permute-start.8 = (bf16[16,1536]{1,0:T(8,128)(2,1)S(1)}, bf16[16,1536]{1,0:T(8,128)(2,1)S(1)}, u32[]{:S(2)}, u32[]{:S(2)}) collective-permute-start(bf16[16,1536]{1,0:T(8,128)(2,1)S(1)} %pad_maximum_fusion.1), channel_id=1, source_target_pairs={{0,32},{8,40},{16,48},{24,56},{32,0},{40,8},{48,16},{56,24},{1,33}... | collective-permute-start | bytes 147464 | tf_op jit(solution)/shard_map/ppermute | solution.py:285
  96.0 1.1 copy-start.1

commit v6 on v5

--- a/solution.py
+++ b/solution.py
@@ -15,6 +15,8 @@
 XO = 4
 XB = X // XO
 LANES = XB * 192
+OWN_LIMIT = 24 * 1024 * 1024
+BLUR_LIMIT = 22 * 1024 * 1024
 EXT = 104
 ROWS = 2 * EXT
 NARROW = 128
@@ -159,12 +161,76 @@
             pltpu.VMEM((3 * NEED * R, 128), jnp.float32),
             pltpu.VMEM((3, 3 * NEED * R, 128), jnp.float32),
         ],
-        compiler_params=pltpu.CompilerParams(vmem_limit_bytes=32 * 1024 * 1024),
+        compiler_params=pltpu.CompilerParams(vmem_limit_bytes=14 * 1024 * 1024),
     )(listed, table, tap_maps())
 
 
 def roll_half(value):
     return pltpu.roll(value, 64, 1)
+
+
+def stage_x(slot, part, a1_ref, put, offset):
+    low = lax.broadcasted_iota(jnp.int32, (8, NARROW), 1) < 64
+    pairs = part.shape[0] * 2 // 3
+
+    def step(i, carry):
+        g = 2 * i
+        rhs = jnp.concatenate(
+            [part[4 * i], part[4 * i + 1], part[4 * i + 2], part[4 * i + 3], part[pairs + g], part[pairs + g + 1]],
+            axis=1,
+        )
+        made = jnp.dot(a1_ref[slot], rhs, preferred_element_type=jnp.float32)
+        base = pl.multiple_of((offset + g) * 16, 32)
+
+        def cell(r, b, k):
+            row = (r * XB + b) * 8
+            return made[row : row + 8, k * 128 : (k + 1) * 128]
+
+        def place(r, k, column, first, second):
+            put(
+                r,
+                pl.ds(base + k * 16, 16),
+                slice(column * 128, (column + 1) * 128),
+                jnp.concatenate([first, second], axis=0).astype(jnp.bfloat16),
+            )
+
+        for r in range(R):
+            for k in range(2):
+                for b in range(XB):
+                    place(r, k, b, cell(r, b, 2 * k), cell(r, b, 2 * k + 1))
+                for c in range(XB // 2):
+                    one, two = cell(r, 2 * c, 4 + k), cell(r, 2 * c + 1, 4 + k)
+                    place(
+                        r, k, XB + c,
+                        jnp.where(low, one, roll_half(two)),
+                        jnp.where(low, roll_half(one), two),
+                    )
+        return carry
+
+    lax.fori_loop(0, pairs // 4, step, 0)
+
+
+def own_kernel(live_ref, own_ref, a1_ref, out_ref):
+    def one_slot(slot, carry):
+        def put(r, rows, lanes, value):
+            out_ref[slot, r, rows, lanes] = value
+
+        stage_x(slot, own_ref, a1_ref, put, 0)
+        return carry
+
+    lax.fori_loop(0, live_ref[0], one_slot, 0)
+
+
+def blur_own(live, own, a1):
+    vmem = pl.BlockSpec(memory_space=pltpu.VMEM)
+    return pl.pallas_call(
+        own_kernel,
+        out_shape=jax.ShapeDtypeStruct((NEED, R, Y * XO, LANES), jnp.bfloat16),
+        in_specs=[pl.BlockSpec(memory_space=pltpu.SMEM), vmem, vmem],
+        out_specs=vmem,
+        compiler_params=pltpu.CompilerParams(vmem_limit_bytes=OWN_LIMIT),
+        cost_estimate=pl.CostEstimate(flops=8_000_000_000, bytes_accessed=2_000_000, transcendentals=0),
+    )(live, own, a1)
 
 
 def blur_kernel(
@@ -172,50 +238,16 @@
     weights_ref, slot_ref, out_ref, line_x, line_y, band_y,
 ):
     out_ref[...] = jnp.zeros_like(out_ref)
-    low_x = lax.broadcasted_iota(jnp.int32, (8, NARROW), 1) < 64
     low_y = lax.broadcasted_iota(jnp.int32, (TOP * XO, NARROW), 1) < 64
     low_b = lax.broadcasted_iota(jnp.int32, ((Y - TOP) * XO, NARROW), 1) < 64
+    side = HALF * XO
 
     def one_slot(slot, carry):
-        def stage_x(part, offset):
-            pairs = part.shape[0] * 2 // 3
-
-            def step(i, carry):
-                g = 2 * i
-                rhs = jnp.concatenate(
-                    [part[4 * i], part[4 * i + 1], part[4 * i + 2], part[4 * i + 3], part[pairs + g], part[pairs + g + 1]],
-                    axis=1,
-                )
-                made = jnp.dot(a1_ref[slot], rhs, preferred_element_type=jnp.float32)
-                base = pl.multiple_of((offset + g) * 16, 32)
-
-                def cell(r, b, k):
-                    row = (r * XB + b) * 8
-                    return made[row : row + 8, k * 128 : (k + 1) * 128]
-
-                def put(r, k, column, first, second):
-                    line_x[r, pl.ds(base + k * 16, 16), column * 128 : (column + 1) * 128] = (
-                        jnp.concatenate([first, second], axis=0).astype(jnp.bfloat16)
-                    )
-
-                for r in range(R):
-                    for k in range(2):
-                        for b in range(XB):
-                            put(r, k, b, cell(r, b, 2 * k), cell(r, b, 2 * k + 1))
-                        for c in range(XB // 2):
-                            one, two = cell(r, 2 * c, 4 + k), cell(r, 2 * c + 1, 4 + k)
-                            put(
-                                r, k, XB + c,
-                                jnp.where(low_x, one, roll_half(two)),
-                                jnp.where(low_x, roll_half(one), two),
-                            )
-                return carry
-
-            lax.fori_loop(0, pairs // 4, step, 0)
-
-        stage_x(left_ref, 0)
-        stage_x(own_ref, 8)
-        stage_x(right_ref, 18)
+        def put(r, rows, lanes, value):
+            line_x[r, rows, lanes] = value
+
+        stage_x(slot, left_ref, a1_ref, put, 0)
+        stage_x(slot, right_ref, a1_ref, put, 8)
 
         def pair(q, carry):
             made = []
@@ -225,7 +257,8 @@
                 for o in range(XO):
                     band_y[h, o * TOP : (o + 1) * TOP, :] = top * mask_ref[o : o + 1, :]
                 band_y[h, TOP * XO :, :] = a2b_ref[slot * R + r]
-                made.append(jnp.dot(band_y[h], line_x[r], preferred_element_type=jnp.float32))
+                lines = jnp.concatenate([line_x[r, :side], own_ref[slot, r], line_x[r, side:]], axis=0)
+                made.append(jnp.dot(band_y[h], lines, preferred_element_type=jnp.float32))
             lanes = pl.multiple_of(q * 384, 128)
             tail = pl.ds(lanes + 256, 128)
             for first, count, start, low in ((0, TOP * XO, 0, low_y), (TOP * XO, (Y - TOP) * XO, TOP * X, low_b)):
@@ -261,6 +294,8 @@
 
 def blur(live, cells, bands, weights, cell_slot):
     a1, a2, a2b, bz = bands
+    left, own, right = cells
+    own = blur_own(live, own, a1)
     vmem = pl.BlockSpec(memory_space=pltpu.VMEM)
     mask = same_lane()
     return pl.pallas_call(
@@ -269,26 +304,21 @@
         in_specs=[pl.BlockSpec(memory_space=pltpu.SMEM)] + [vmem] * 10,
         out_specs=vmem,
         scratch_shapes=[
-            pltpu.VMEM((R, EXT * XO, LANES), jnp.bfloat16),
+            pltpu.VMEM((R, 2 * HALF * XO, LANES), jnp.bfloat16),
             pltpu.VMEM((1600, 1536), jnp.bfloat16),
             pltpu.VMEM((2, Y * XO, EXT * XO), jnp.bfloat16),
         ],
-        compiler_params=pltpu.CompilerParams(vmem_limit_bytes=40 * 1024 * 1024),
-    )(live, *cells, a1, a2, a2b, mask, bz, weights, cell_slot)
-
-
-def gathered(rows, axis):
+        compiler_params=pltpu.CompilerParams(vmem_limit_bytes=BLUR_LIMIT),
+    )(live, left, own, right, a1, a2, a2b, mask, bz, weights, cell_slot)
+
+
+def doubled(rows, axis, bit):
     count = lax.axis_size(axis)
-    position = lax.axis_index(axis)
-    bit = 1
-    while bit < count:
-        other = lax.ppermute(rows, axis, [(i, i ^ bit) for i in range(count)])
-        upper = (position & bit) != 0
-        rows = jnp.concatenate(
-            [jnp.where(upper, other, rows), jnp.where(upper, rows, other)], axis=0
-        )
-        bit *= 2
-    return rows
+    other = lax.ppermute(rows, axis, [(i, i ^ bit) for i in range(count)])
+    upper = (lax.axis_index(axis) & bit) != 0
+    return jnp.concatenate(
+        [jnp.where(upper, other, rows), jnp.where(upper, rows, other)], axis=0
+    )
 
 
 def both_ways(to_next, to_last, axis):
@@ -303,15 +333,10 @@
     return lax.broadcasted_iota(jnp.int32, (1, NARROW), 1) // HALF
 
 
-def cut_kernel(reflect_ref, own_ref, next_ref, last_ref, deeper_ref, shallower_ref):
+def ends_kernel(reflect_ref, shallower_ref, deeper_ref):
     part = lane_part()
     for g in range(Y // 8):
         rows = [reflect_ref[:, 8 * g + k, :] for k in range(8)]
-        for pair in range(4):
-            two = rows[2 * pair : 2 * pair + 2]
-            own_ref[4 * g + pair] = jnp.concatenate(two, axis=0).astype(jnp.bfloat16)
-            next_ref[4 * g + pair] = jnp.concatenate([v[X - HALF :] for v in two], axis=0).astype(jnp.bfloat16)
-            last_ref[4 * g + pair] = jnp.concatenate([v[:HALF] for v in two], axis=0).astype(jnp.bfloat16)
         for ref, first in ((deeper_ref, Z - HALF), (shallower_ref, 0)):
             packed = []
             for s in range(2):
@@ -325,15 +350,34 @@
             ref[g] = jnp.concatenate(packed, axis=0).astype(jnp.bfloat16)
 
 
-def cut(reflect):
-    shapes = [(20, 80, Z), (20, 64, Z), (20, 64, Z), (5, 80, NARROW), (5, 80, NARROW)]
+def depth_ends(reflect):
+    vmem = pl.BlockSpec(memory_space=pltpu.VMEM)
+    return pl.pallas_call(
+        ends_kernel,
+        out_shape=[jax.ShapeDtypeStruct((5, 80, NARROW), jnp.bfloat16)] * 2,
+        in_specs=[vmem],
+        out_specs=[vmem] * 2,
+    )(reflect)
+
+
+def cut_kernel(reflect_ref, factors_ref, after_ref, own_ref, next_ref, last_ref, rows_ref):
+    rows_ref[...] = factors_ref[...]
+    for pair in range(Y // 2):
+        two = [reflect_ref[:, 2 * pair + k, :] for k in range(2)]
+        own_ref[pair] = jnp.concatenate(two, axis=0).astype(jnp.bfloat16)
+        next_ref[pair] = jnp.concatenate([v[X - HALF :] for v in two], axis=0).astype(jnp.bfloat16)
+        last_ref[pair] = jnp.concatenate([v[:HALF] for v in two], axis=0).astype(jnp.bfloat16)
+
+
+def cut(reflect, factors, after):
+    shapes = [(20, 80, Z), (20, 64, Z), (20, 64, Z), factors.shape]
     vmem = pl.BlockSpec(memory_space=pltpu.VMEM)
     return pl.pallas_call(
         cut_kernel,
         out_shape=[jax.ShapeDtypeStruct(shape, jnp.bfloat16) for shape in shapes],
-        in_specs=[vmem],
-        out_specs=[vmem] * 5,
-    )(reflect)
+        in_specs=[vmem] * 2 + [pl.BlockSpec(memory_space=pl.ANY)],
+        out_specs=[vmem] * 4,
+    )(reflect, factors, after)
 
 
 def tail_kernel(left_ref, right_ref, main_next, main_last, own_ref, next_ref, last_ref):
@@ -369,7 +413,7 @@
     )(left, right, main_next, main_last)
 
 
-def join_kernel(before_ref, own_ref, tail_ref, after_ref, all_ref, next_ref, last_ref):
+def join_kernel(before_ref, own_ref, tail_ref, after_ref, rows_ref, all_ref, next_ref, last_ref):
     for ref, to, at, count in (
         (all_ref, 0, 0, 30),
         (next_ref, 0, 4, 16),
@@ -387,32 +431,36 @@
             ref[to + mains : to + count, 64:144, :] = tail_ref[first : first + count - mains]
 
 
-def join(before, own, tail, after):
+def join(before, own, tail, after, rows):
     vmem = pl.BlockSpec(memory_space=pltpu.VMEM)
     return pl.pallas_call(
         join_kernel,
         out_shape=[jax.ShapeDtypeStruct((n, ROWS, NARROW), jnp.bfloat16) for n in (30, 24, 24)],
-        in_specs=[vmem] * 4,
+        in_specs=[vmem] * 4 + [pl.BlockSpec(memory_space=pl.ANY)],
         out_specs=[vmem] * 3,
-        compiler_params=pltpu.CompilerParams(vmem_limit_bytes=24 * 1024 * 1024),
-    )(before, own, tail, after)
-
-
-def halo(reflect):
-    own, to_next, to_last, deeper, shallower = cut(reflect)
+        compiler_params=pltpu.CompilerParams(vmem_limit_bytes=12 * 1024 * 1024),
+    )(before, own, tail, after, rows)
+
+
+def exchange(reflect, factors):
+    shallower, deeper = depth_ends(reflect)
     above, below = both_ways(deeper, shallower, "gz")
+    own, to_next, to_last, rows = cut(reflect, factors, shallower)
+    rows = doubled(doubled(rows, "xl", 1), "xl", 2)
     tail, to_next, to_last = unpack_tail(above, below, to_next, to_last)
     before, after = both_ways(to_next, to_last, "il")
-    block, to_next, to_last = join(before, own, tail, after)
+    block, to_next, to_last = join(before, own, tail, after, rows)
+    rows = doubled(rows, "xl", 4)
     left, right = both_ways(to_next, to_last, "xl")
-    return left, block, right
+    return (left, block, right), rows
 
 
 def per_device(reflect, weights, cell_slot, factors, reader_list):
     listed = reader_list.reshape(NEED)
     live_count = jnp.sum((listed >= 0).astype(jnp.int32))
-    bands = make_bands(listed, gathered(factors, "xl"))
-    return blur(live_count.reshape(1), halo(reflect), bands, weights, cell_slot)
+    cells, rows = exchange(reflect, factors)
+    bands = make_bands(listed, rows)
+    return blur(live_count.reshape(1), cells, bands, weights, cell_slot)
 
 
 def solution(mesh):

time: 137 us -> 112 us (0.82)
  the two profiles are of different devices: /device:TPU:78 before, /device:TPU:449 now
where the time goes in v6:
time: 112 us
  Pallas kernels  52.6 us (47%)
  starting transfers between devices  32.1 us (29%)
  waiting for transfers between devices  23.5 us (21%)
  local copies, waits for them, and re-layouts  1.64 us (1%)
  other arithmetic  1.53 us (1%)
    pallas_call x1, Pallas kernels, blur(): pl.pallas_call(blur_kernel, out_shape=jax.ShapeDtypeStruct((X, Y, Z), jnp...  30.1 us
    ppermute x3, waiting for transfers between devices, both_ways(): lax.ppermute(to_next, axis, [(i, (i + 1) % count) for i in range(ends)])  19.9 us
    ppermute x3, starting transfers between devices, both_ways(): lax.ppermute(to_last, axis, [((i + 1) % count, i) for i in range(ends)])  12.6 us
    ppermute x3, starting transfers between devices, doubled(): other = lax.ppermute(rows, axis, [(i, i ^ bit) for i in range(count)])  10.7 us
    ppermute x3, starting transfers between devices, both_ways(): lax.ppermute(to_next, axis, [(i, (i + 1) % count) for i in range(ends)])  8.7 us
    pallas_call x1, Pallas kernels, blur_own(): pl.pallas_call(own_kernel, out_shape=jax.ShapeDtypeStruct((NEED, R, Y * X...  8.3 us
    pallas_call x1, Pallas kernels, make_bands(): pl.pallas_call(bands_kernel, out_shape=[jax.ShapeDtypeStruct(shape, jnp.b...  6.58 us
    ppermute x3, waiting for transfers between devices, both_ways(): lax.ppermute(to_last, axis, [((i + 1) % count, i) for i in range(ends)])  3.56 us
  transfers between devices with their start and end apart: 9, of which 4 were waited for; matrix products, arithmetic and copies ran while one was open for 1% of the time, Pallas kernels for 16%

profile of v6, /device:TPU:449, one launch (start us, length us, event | category | flops | bytes accessed | tf_op | source)
XLA Modules:
  0.0 111.6 jit_solution(4257068446890851284)
XLA Ops:
  0.0 0.0 copy-start.6
  0.0 2.3 %shard_map.73 = (bf16[5,80,128]{2,1,0:T(8,128)(2,1)}, bf16[5,80,128]{2,1,0:T(8,128)(2,1)}) custom-call(f32[40,40,128]{2,1,0:T(8,128)} %reflect_ref.3), custom_call_target="tpu_custom_call" | custom-call | tf_op jit(solution)/shard_map/pallas_call | solution.py:355
  2.3 2.6 %shard_map.74 = (bf16[20,80,128]{2,1,0:T(8,128)(2,1)}, bf16[20,64,128]{2,1,0:T(8,128)(2,1)}, bf16[20,64,128]{2,1,0:T(8,128)(2,1)}, bf16[4,1536]{1,0:T(4,128)(2,1)}) custom-call(f32[40,40,128]{2,1,0:T(8,128)} %reflect_ref.3, bf16[4,1536]{1,0:T(4,128)(2,1)} %factors_ref.1, bf16[5,80,128]{2,1,0:T(8,128)(2,1)} %get-tuple-element.22.after_ref), custom_call_target="tpu_custom_call" | custom-call | tf_op jit(solution)/shard_map/pallas_call | solution.py:375
  4.9 0.0 copy-start.2
  4.9 2.7 %collective-permute-start.4 = (bf16[4,1536]{1,0:T(4,128)(2,1)}, bf16[4,1536]{1,0:T(4,128)(2,1)S(1)}, u32[]{:S(2)}, u32[]{:S(2)}) collective-permute-start(bf16[4,1536]{1,0:T(4,128)(2,1)} %get-tuple-element.29), channel_id=1, source_target_pairs={{0,8},{8,0},{16,24},{24,16},{32,40},{40,32},{48,56},{56,48},{1,9},... | collective-permute-start | bytes 36872 | tf_op jit(solution)/shard_map/ppermute | solution.py:317
  7.6 7.4 %collective-permute-start.1 = (bf16[5,80,128]{2,1,0:T(8,128)(2,1)}, bf16[5,80,128]{2,1,0:T(8,128)(2,1)S(1)}, u32[]{:S(2)}, u32[]{:S(2)}) collective-permute-start(bf16[5,80,128]{2,1,0:T(8,128)(2,1)} %get-tuple-element.22.after_ref), channel_id=1, source_target_pairs={{1,0},{2,1},{3,2},{4,3},{5,4},{6,5},{7,6},{9,8},{10,9},{11,10},{12... | collective-permute-start | bytes 307208 | tf_op jit(solution)/shard_map/ppermute | solution.py:327
  15.0 1.9 %collective-permute-start = (bf16[5,80,128]{2,1,0:T(8,128)(2,1)}, bf16[5,80,128]{2,1,0:T(8,128)(2,1)S(1)}, u32[]{:S(2)}, u32[]{:S(2)}) collective-permute-start(bf16[5,80,128]{2,1,0:T(8,128)(2,1)} %get-tuple-element.21), channel_id=1, source_target_pairs={{0,1},{1,2},{2,3},{3,4},{4,5},{5,6},{6,7},{8,9},{9,10},{10,11},{11... | collective-permute-start | bytes 307208 | tf_op jit(solution)/shard_map/ppermute | solution.py:328
  16.9 0.0 collective-permute-done.4
  16.9 0.7 broadcast_select_fusion.5
  17.7 3.2 %collective-permute-start.5 = (bf16[8,1536]{1,0:T(8,128)(2,1)S(1)}, bf16[8,1536]{1,0:T(8,128)(2,1)S(1)}, u32[]{:S(2)}, u32[]{:S(2)}) collective-permute-start(bf16[8,1536]{1,0:T(8,128)(2,1)S(1)} %pad_maximum_fusion.2), channel_id=1, source_target_pairs={{0,16},{8,24},{16,0},{24,8},{32,48},{40,56},{48,32},{56,40},{1,17}... | collective-permute-start | bytes 73736 | tf_op jit(solution)/shard_map/ppermute | solution.py:317
  20.9 16.8 %collective-permute-done.left_ref = bf16[5,80,128]{2,1,0:T(8,128)(2,1)S(1)} collective-permute-done((bf16[5,80,128]{2,1,0:T(8,128)(2,1)}, bf16[5,80,128]{2,1,0:T(8,128)(2,1)S(1)}, u32[]{:S(2)}, u32[]{:S(2)}) %collective-permute-start) | collective-permute-done | bytes 102432 | tf_op jit(solution)/shard_map/ppermute | solution.py:328
  37.7 0.0 copy-start.8
  37.7 0.0 collective-permute-done.1.right_ref
  37.7 0.0 copy-start.7
  37.7 0.6 copy-done.8
  38.3 0.1 copy-done.7
  38.4 2.4 %shard_map.75 = (bf16[10,80,128]{2,1,0:T(8,128)(2,1)}, bf16[30,64,128]{2,1,0:T(8,128)(2,1)}, bf16[30,64,128]{2,1,0:T(8,128)(2,1)}) custom-call(bf16[5,80,128]{2,1,0:T(8,128)(2,1)} %copy-done.8, bf16[5,80,128]{2,1,0:T(8,128)(2,1)} %copy-done.7, bf16[20,64,128]{2,1,0:T(8,128)(2,1)} %get-tuple-element.23.main_next, bf16[20,64,128]{2,1,0:T(8,128)(2,1)} %get-tuple-element.24.main_last), custom_call_target="tpu_custom_call" | custom-call | tf_op jit(solution)/shard_map/pallas_call | solution.py:408
  40.8 0.0 copy-start.4
  40.8 2.0 %collective-permute-start.2 = (bf16[30,64,128]{2,1,0:T(8,128)(2,1)}, bf16[30,64,128]{2,1,0:T(8,128)(2,1)S(1)}, u32[]{:S(2)}, u32[]{:S(2)}) collective-permute-start(bf16[30,64,128]{2,1,0:T(8,128)(2,1)} %get-tuple-element.25), channel_id=1, source_target_pairs={{0,64},{64,128},{128,192},{192,256},{256,320},{320,384},{384,448},... | collective-permute-start | bytes 1474568 | tf_op jit(solution)/shard_map/ppermute | solution.py:328
  42.8 3.4 %collective-permute-start.3 = (bf16[30,64,128]{2,1,0:T(8,128)(2,1)}, bf16[30,64,128]{2,1,0:T(8,128)(2,1)S(1)}, u32[]{:S(2)}, u32[]{:S(2)}) collective-permute-start(bf16[30,64,128]{2,1,0:T(8,128)(2,1)} %get-tuple-element.28), channel_id=1, source_target_pairs={{64,0},{128,64},{192,128},{256,192},{320,256},{384,320},{448,384},... | collective-permute-start | bytes 1474568 | tf_op jit(solution)/shard_map/ppermute | solution.py:327
  46.2 0.0 collective-permute-done.5
  46.3 4.8 %collective-permute-start.7 = (bf16[16,1536]{1,0:T(8,128)(2,1)S(1)}, bf16[16,1536]{1,0:T(8,128)(2,1)S(1)}, u32[]{:S(2)}, u32[]{:S(2)}) collective-permute-start(bf16[16,1536]{1,0:T(8,128)(2,1)S(1)} %pad_maximum_fusion.1.rows_ref), channel_id=1, source_target_pairs={{0,32},{8,40},{16,48},{24,56},{32,0},{40,8},{48,16},{56,24},{1,33}... | collective-permute-start | bytes 147464 | tf_op jit(solution)/shard_map/ppermute | solution.py:317
  51.1 0.0 copy-done.6
  51.1 0.7 fusion
  51.8 3.2 %collective-permute-done.2.before_ref = bf16[30,64,128]{2,1,0:T(8,128)(2,1)S(1)} collective-permute-done((bf16[30,64,128]{2,1,0:T(8,128)(2,1)}, bf16[30,64,128]{2,1,0:T(8,128)(2,1)S(1)}, u32[]{:S(2)}, u32[]{:S(2)}) %collective-permute-start.2) | collective-permute-done | bytes 491552 | tf_op jit(solution)/shard_map/ppermute | solution.py:328
  55.0 1.9 %collective-permute-done.3.after_ref = bf16[30,64,128]{2,1,0:T(8,128)(2,1)S(1)} collective-permute-done((bf16[30,64,128]{2,1,0:T(8,128)(2,1)}, bf16[30,64,128]{2,1,0:T(8,128)(2,1)S(1)}, u32[]{:S(2)}, u32[]{:S(2)}) %collective-permute-start.3) | collective-permute-done | bytes 491552 | tf_op jit(solution)/shard_map/ppermute | solution.py:327
  56.9 0.0 copy-done.2
  56.9 0.0 copy-start.3
  56.9 0.9 copy-done.3
  57.9 0.3 shard_map.76
  58.1 4.7 %collective-permute-start.6 = (bf16[24,208,128]{2,1,0:T(8,128)(2,1)S(1)}, bf16[24,208,128]{2,1,0:T(8,128)(2,1)S(1)}, u32[]{:S(2)}, u32[]{:S(2)}) collective-permute-start(bf16[24,208,128]{2,1,0:T(8,128)(2,1)S(1)} %get-tuple-element.30), channel_id=1, source_target_pairs={{0,8},{8,16},{16,24},{24,32},{32,40},{40,48},{48,56},{1,9},{9,17},... | collective-permute-start | bytes 3833864 | tf_op jit(solution)/shard_map/ppermute | solution.py:328
  62.9 1.9 %collective-permute-start.8 = (bf16[24,208,128]{2,1,0:T(8,128)(2,1)S(1)}, bf16[24,208,128]{2,1,0:T(8,128)(2,1)S(1)}, u32[]{:S(2)}, u32[]{:S(2)}) collective-permute-start(bf16[24,208,128]{2,1,0:T(8,128)(2,1)S(1)} %get-tuple-element.33), channel_id=1, source_target_pairs={{8,0},{16,8},{24,16},{32,24},{40,32},{48,40},{56,48},{9,1},{17,9},... | collective-permute-start | bytes 3833864 | tf_op jit(solution)/shard_map/ppermute | solution.py:327
  64.8 0.0 collective-permute-done.7
  64.9 0.0 copy-done.4
  64.9 6.6 %shard_map.77 = (bf16[3,640,208]{2,1,0:T(8,128)(2,1)S(1)}, bf16[24,32,416]{2,1,0:T(8,128)(2,1)S(1)}, bf16[24,32,416]{2,1,0:T(8,128)(2,1)S(1)}, bf16[3,1536,128]{2,1,0:T(8,128)(2,1)S(1)}) custom-call(s32[3]{0:T(128)S(1)} %bitcast.3, bf16[32,1536]{1,0:T(8,128)(2,1)S(1)} %pad_maximum_fusion.table_ref, bf16[128,384]{1,0:T(8,128)(2,1)S(1)} %copy-done.4), custom_call_target="tpu_custom_call" | custom-call | tf_op jit(solution)/shard_map/pallas_call | solution.py:154
  71.5 0.0 copy-start
  71.5 0.0 copy-start.1
  71.5 0.0 copy-start.5
  71.5 8.3 %shard_map.78.own_ref = bf16[3,8,160,1920]{3,2,1,0:T(8,128)(2,1)S(1)} custom-call(s32[1]{0:T(128)} %bitcast.1.live_ref, bf16[30,208,128]{2,1,0:T(8,128)(2,1)S(1)} %get-tuple-element.31.own_ref, bf16[3,640,208]{2,1,0:T(8,128)(2,1)S(1)} %get-tuple-element.32.a1_ref), custom_call_target="tpu_custom_call" | custom-call | flops 8000000000 | bytes 2000000 | tf_op jit(solution)/shard_map/pallas_call | solution.py:226
  79.8 0.0 collective-permute-done.6.left_ref
  79.8 1.6 %collective-permute-done.8.right_ref = bf16[24,208,128]{2,1,0:T(8,128)(2,1)S(1)} collective-permute-done((bf16[24,208,128]{2,1,0:T(8,128)(2,1)S(1)}, bf16[24,208,128]{2,1,0:T(8,128)(2,1)S(1)}, u32[]{:S(2)}, u32[]{:S(2)}) %collective-permute-start.8) | collective-permute-done | bytes 1277984 | tf_op jit(solution)/shard_map/ppermute | solution.py:327
  81.5 0.0 copy-done
  81.5 0.0 copy-done.1
  81.5 0.0 copy-done.5
  81.5 30.1 %shard_map.79 = f32[40,40,128]{2,1,0:T(8,128)} custom-call(s32[1]{0:T(128)} %bitcast.1.live_ref, bf16[24,208,128]{2,1,0:T(8,128)(2,1)S(1)} %collective-permute-done.6.left_ref, bf16[3,8,160,1920]{3,2,1,0:T(8,128)(2,1)S(1)} %shard_map.78.own_ref, bf16[24,208,128]{2,1,0:T(8,128)(2,1)S(1)} %collective-permute-done.8.right_ref, ...), custom_call_target="tpu_custom_call" | custom-call | tf_op jit(solution)/shard_map/pallas_call | solution.py:301
  (5 shorter events, 0.1 us)
Async XLA Ops:
  0.0 51.1 %copy-start.6 = (s32[1,1,1,3]{3,2,1,0:T(1,128)S(1)}, s32[1,1,1,3]{3,2,1,0:T(1,128)}, u32[]{:S(2)}) copy-start(s32[1,1,1,3]{3,2,1,0:T(1,128)} %param.11) | copy-start | bytes 40
  4.9 52.0 %copy-start.2 = (bf16[20,80,128]{2,1,0:T(8,128)(2,1)S(1)}, bf16[20,80,128]{2,1,0:T(8,128)(2,1)}, u32[]{:S(2)}) copy-start(bf16[20,80,128]{2,1,0:T(8,128)(2,1)} %get-tuple-element.26.own_ref) | copy-start | bytes 1228804
  4.9 12.0 %collective-permute-start.4 = (bf16[4,1536]{1,0:T(4,128)(2,1)}, bf16[4,1536]{1,0:T(4,128)(2,1)S(1)}, u32[]{:S(2)}, u32[]{:S(2)}) collective-permute-start(bf16[4,1536]{1,0:T(4,128)(2,1)} %get-tuple-element.29), channel_id=1, source_target_pairs={{0,8},{8,0},{16,24},{24,16},{32,40},{40,32},{48,56},{56,48},{1,9},... | collective-permute-start | bytes 36872 | tf_op jit(solution)/shard_map/ppermute | solution.py:317
  7.6 30.0 %collective-permute-start.1 = (bf16[5,80,128]{2,1,0:T(8,128)(2,1)}, bf16[5,80,128]{2,1,0:T(8,128)(2,1)S(1)}, u32[]{:S(2)}, u32[]{:S(2)}) collective-permute-start(bf16[5,80,128]{2,1,0:T(8,128)(2,1)} %get-tuple-element.22.after_ref), channel_id=1, source_target_pairs={{1,0},{2,1},{3,2},{4,3},{5,4},{6,5},{7,6},{9,8},{10,9},{11,10},{12... | collective-permute-start | bytes 307208 | tf_op jit(solution)/shard_map/ppermute | solution.py:327
  15.0 22.7 %collective-permute-start = (bf16[5,80,128]{2,1,0:T(8,128)(2,1)}, bf16[5,80,128]{2,1,0:T(8,128)(2,1)S(1)}, u32[]{:S(2)}, u32[]{:S(2)}) collective-permute-start(bf16[5,80,128]{2,1,0:T(8,128)(2,1)} %get-tuple-element.21), channel_id=1, source_target_pairs={{0,1},{1,2},{2,3},{3,4},{4,5},{5,6},{6,7},{8,9},{9,10},{10,11},{11... | collective-permute-start | bytes 307208 | tf_op jit(solution)/shard_map/ppermute | solution.py:328
  17.7 28.5 %collective-permute-start.5 = (bf16[8,1536]{1,0:T(8,128)(2,1)S(1)}, bf16[8,1536]{1,0:T(8,128)(2,1)S(1)}, u32[]{:S(2)}, u32[]{:S(2)}) collective-permute-start(bf16[8,1536]{1,0:T(8,128)(2,1)S(1)} %pad_maximum_fusion.2), channel_id=1, source_target_pairs={{0,16},{8,24},{16,0},{24,8},{32,48},{40,56},{48,32},{56,40},{1,17}... | collective-permute-start | bytes 73736 | tf_op jit(solution)/shard_map/ppermute | solution.py:317
  37.7 0.6 copy-start.8
  37.7 0.7 copy-start.7
  40.8 24.1 %copy-start.4 = (bf16[128,384]{1,0:T(8,128)(2,1)S(1)}, bf16[128,384]{1,0:T(8,128)(2,1)}, u32[]{:S(2)}) copy-start(bf16[128,384]{1,0:T(8,128)(2,1)} %constant.18.clone.map_ref) | copy-start | bytes 294916
  40.8 14.2 %collective-permute-start.2 = (bf16[30,64,128]{2,1,0:T(8,128)(2,1)}, bf16[30,64,128]{2,1,0:T(8,128)(2,1)S(1)}, u32[]{:S(2)}, u32[]{:S(2)}) collective-permute-start(bf16[30,64,128]{2,1,0:T(8,128)(2,1)} %get-tuple-element.25), channel_id=1, source_target_pairs={{0,64},{64,128},{128,192},{192,256},{256,320},{320,384},{384,448},... | collective-permute-start | bytes 1474568 | tf_op jit(solution)/shard_map/ppermute | solution.py:328
  42.8 14.1 %collective-permute-start.3 = (bf16[30,64,128]{2,1,0:T(8,128)(2,1)}, bf16[30,64,128]{2,1,0:T(8,128)(2,1)S(1)}, u32[]{:S(2)}, u32[]{:S(2)}) collective-permute-start(bf16[30,64,128]{2,1,0:T(8,128)(2,1)} %get-tuple-element.28), channel_id=1, source_target_pairs={{64,0},{128,64},{192,128},{256,192},{320,256},{384,320},{448,384},... | collective-permute-start | bytes 1474568 | tf_op jit(solution)/shard_map/ppermute | solution.py:327
  46.3 18.5 %collective-permute-start.7 = (bf16[16,1536]{1,0:T(8,128)(2,1)S(1)}, bf16[16,1536]{1,0:T(8,128)(2,1)S(1)}, u32[]{:S(2)}, u32[]{:S(2)}) collective-permute-start(bf16[16,1536]{1,0:T(8,128)(2,1)S(1)} %pad_maximum_fusion.1.rows_ref), channel_id=1, source_target_pairs={{0,32},{8,40},{16,48},{24,56},{32,0},{40,8},{48,16},{56,24},{1,33}... | collective-permute-start | bytes 147464 | tf_op jit(solution)/shard_map/ppermute | solution.py:317
  56.9 0.9 copy-start.3
  58.1 21.7 %collective-permute-start.6 = (bf16[24,208,128]{2,1,0:T(8,128)(2,1)S(1)}, bf16[24,208,128]{2,1,0:T(8,128)(2,1)S(1)}, u32[]{:S(2)}, u32[]{:S(2)}) collective-permute-start(bf16[24,208,128]{2,1,0:T(8,128)(2,1)S(1)} %get-tuple-element.30), channel_id=1, source_target_pairs={{0,8},{8,16},{16,24},{24,32},{32,40},{40,48},{48,56},{1,9},{9,17},... | collective-permute-start | bytes 3833864 | tf_op jit(solution)/shard_map/ppermute | solution.py:328
  62.9 18.6 %collective-permute-start.8 = (bf16[24,208,128]{2,1,0:T(8,128)(2,1)S(1)}, bf16[24,208,128]{2,1,0:T(8,128)(2,1)S(1)}, u32[]{:S(2)}, u32[]{:S(2)}) collective-permute-start(bf16[24,208,128]{2,1,0:T(8,128)(2,1)S(1)} %get-tuple-element.33), channel_id=1, source_target_pairs={{8,0},{16,8},{24,16},{32,24},{40,32},{48,40},{56,48},{9,1},{17,9},... | collective-permute-start | bytes 3833864 | tf_op jit(solution)/shard_map/ppermute | solution.py:327
  71.5 10.0 %copy-start = (s32[2,40,40,128]{3,2,1,0:T(8,128)S(1)}, s32[2,40,40,128]{3,2,1,0:T(8,128)}, u32[]{:S(2)}) copy-start(s32[2,40,40,128]{3,2,1,0:T(8,128)} %slot_ref.1) | copy-start | bytes 4915204
  71.5 10.0 %copy-start.1 = (bf16[2,40,40,128]{3,2,1,0:T(8,128)(2,1)S(1)}, bf16[2,40,40,128]{3,2,1,0:T(8,128)(2,1)}, u32[]{:S(2)}) copy-start(bf16[2,40,40,128]{3,2,1,0:T(8,128)(2,1)} %weights_ref.1) | copy-start | bytes 2457604
  71.5 10.0 %copy-start.5 = (bf16[4,416]{1,0:T(4,128)(2,1)S(1)}, bf16[4,416]{1,0:T(4,128)(2,1)}, u32[]{:S(2)}) copy-start(bf16[4,416]{1,0:T(4,128)(2,1)} %constant.19.clone.mask_ref) | copy-start | bytes 9988

commit v7 on v6

--- a/solution.py
+++ b/solution.py
@@ -15,6 +15,7 @@
 XO = 4
 XB = X // XO
 LANES = XB * 192
+SMALL_LIMIT = 10 * 1024 * 1024
 OWN_LIMIT = 24 * 1024 * 1024
 BLUR_LIMIT = 22 * 1024 * 1024
 EXT = 104
@@ -140,7 +141,7 @@
         bz_ref[slot, pl.ds(ends + 32, 32), :] = second[32:64]
         return carry
 
-    lax.fori_loop(0, NEED * R, one_term, 0)
+    lax.fori_loop(0, NEED * R, one_term, 0, unroll=4)
 
 
 def make_bands(listed, table):
@@ -333,7 +334,8 @@
     return lax.broadcasted_iota(jnp.int32, (1, NARROW), 1) // HALF
 
 
-def ends_kernel(reflect_ref, shallower_ref, deeper_ref):
+def ends_kernel(reflect_ref, factors_ref, shallower_ref, deeper_ref, rows_ref):
+    rows_ref[...] = factors_ref[...]
     part = lane_part()
     for g in range(Y // 8):
         rows = [reflect_ref[:, 8 * g + k, :] for k in range(8)]
@@ -350,18 +352,19 @@
             ref[g] = jnp.concatenate(packed, axis=0).astype(jnp.bfloat16)
 
 
-def depth_ends(reflect):
-    vmem = pl.BlockSpec(memory_space=pltpu.VMEM)
+def depth_ends(reflect, factors):
+    vmem = pl.BlockSpec(memory_space=pltpu.VMEM)
+    shapes = [(5, 80, NARROW), (5, 80, NARROW), factors.shape]
     return pl.pallas_call(
         ends_kernel,
-        out_shape=[jax.ShapeDtypeStruct((5, 80, NARROW), jnp.bfloat16)] * 2,
-        in_specs=[vmem],
-        out_specs=[vmem] * 2,
-    )(reflect)
-
-
-def cut_kernel(reflect_ref, factors_ref, after_ref, own_ref, next_ref, last_ref, rows_ref):
-    rows_ref[...] = factors_ref[...]
+        out_shape=[jax.ShapeDtypeStruct(shape, jnp.bfloat16) for shape in shapes],
+        in_specs=[vmem] * 2,
+        out_specs=[vmem] * 3,
+        compiler_params=pltpu.CompilerParams(vmem_limit_bytes=SMALL_LIMIT),
+    )(reflect, factors)
+
+
+def cut_kernel(reflect_ref, after_ref, own_ref, next_ref, last_ref):
     for pair in range(Y // 2):
         two = [reflect_ref[:, 2 * pair + k, :] for k in range(2)]
         own_ref[pair] = jnp.concatenate(two, axis=0).astype(jnp.bfloat16)
@@ -369,15 +372,17 @@
         last_ref[pair] = jnp.concatenate([v[:HALF] for v in two], axis=0).astype(jnp.bfloat16)
 
 
-def cut(reflect, factors, after):
-    shapes = [(20, 80, Z), (20, 64, Z), (20, 64, Z), factors.shape]
+def cut(reflect, after):
+    shapes = [(20, 80, Z), (20, 64, Z), (20, 64, Z)]
     vmem = pl.BlockSpec(memory_space=pltpu.VMEM)
     return pl.pallas_call(
         cut_kernel,
         out_shape=[jax.ShapeDtypeStruct(shape, jnp.bfloat16) for shape in shapes],
-        in_specs=[vmem] * 2 + [pl.BlockSpec(memory_space=pl.ANY)],
-        out_specs=[vmem] * 4,
-    )(reflect, factors, after)
+        in_specs=[vmem, pl.BlockSpec(memory_space=pl.ANY)],
+        out_specs=[vmem] * 3,
+        compiler_params=pltpu.CompilerParams(vmem_limit_bytes=SMALL_LIMIT),
+        cost_estimate=pl.CostEstimate(flops=8_000_000_000, bytes_accessed=2_000_000, transcendentals=0),
+    )(reflect, after)
 
 
 def tail_kernel(left_ref, right_ref, main_next, main_last, own_ref, next_ref, last_ref):
@@ -410,6 +415,7 @@
         out_shape=[jax.ShapeDtypeStruct(shape, jnp.bfloat16) for shape in shapes],
         in_specs=[vmem] * 4,
         out_specs=[vmem] * 3,
+        compiler_params=pltpu.CompilerParams(vmem_limit_bytes=SMALL_LIMIT),
     )(left, right, main_next, main_last)
 
 
@@ -443,9 +449,9 @@
 
 
 def exchange(reflect, factors):
-    shallower, deeper = depth_ends(reflect)
+    shallower, deeper, rows = depth_ends(reflect, factors)
     above, below = both_ways(deeper, shallower, "gz")
-    own, to_next, to_last, rows = cut(reflect, factors, shallower)
+    own, to_next, to_last = cut(reflect, deeper)
     rows = doubled(doubled(rows, "xl", 1), "xl", 2)
     tail, to_next, to_last = unpack_tail(above, below, to_next, to_last)
     before, after = both_ways(to_next, to_last, "il")

time: 112 us -> 106 us (0.946)
  the two profiles are of different devices: /device:TPU:449 before, /device:TPU:425 now
where the time goes in v7:
time: 106 us; the launch traced here: 105 us
  Pallas kernels  43.1 us (41%)
  starting transfers between devices  35 us (33%)
  waiting for transfers between devices  23.2 us (22%)
  local copies, waits for them, and re-layouts  3.02 us (3%)
    pallas_call x1, Pallas kernels, blur(): pl.pallas_call(blur_kernel, out_shape=jax.ShapeDtypeStruct((X, Y, Z), jnp...  30 us
    ppermute x3, starting transfers between devices, both_ways(): lax.ppermute(to_next, axis, [(i, (i + 1) % count) for i in range(ends)])  16.1 us
    ppermute x3, waiting for transfers between devices, both_ways(): lax.ppermute(to_next, axis, [(i, (i + 1) % count) for i in range(ends)])  14.9 us
    ppermute x3, starting transfers between devices, both_ways(): lax.ppermute(to_last, axis, [((i + 1) % count, i) for i in range(ends)])  10.3 us
    ppermute x3, starting transfers between devices, doubled(): other = lax.ppermute(rows, axis, [(i, i ^ bit) for i in range(count)])  8.58 us
    pallas_call x1, Pallas kernels, blur_own(): pl.pallas_call(own_kernel, out_shape=jax.ShapeDtypeStruct((NEED, R, Y * X...  8.23 us
    ppermute x3, waiting for transfers between devices, both_ways(): lax.ppermute(to_last, axis, [((i + 1) % count, i) for i in range(ends)])  8.2 us
    pallas_call x1, Pallas kernels, make_bands(): pl.pallas_call(bands_kernel, out_shape=[jax.ShapeDtypeStruct(shape, jnp.b...  3.33 us
  transfers between devices with their start and end apart: 9, of which 5 were waited for; matrix products, arithmetic and copies ran while one was open for 1% of the time, Pallas kernels for 12%

profile of v7, /device:TPU:425, one launch (start us, length us, event | category | flops | bytes accessed | tf_op | source)
XLA Modules:
  0.0 105.2 jit_solution(10281621579126387845)
XLA Ops:
  0.0 0.0 copy-start.1
  0.0 1.1 %copy-done.1 = f32[40,40,128]{2,1,0:T(8,128)S(1)} copy-done((f32[40,40,128]{2,1,0:T(8,128)S(1)}, f32[40,40,128]{2,1,0:T(8,128)}, u32[]{:S(2)}) %copy-start.1) | copy-done | bytes 819224
  1.1 0.0 copy-start.5
  1.1 0.7 copy-done.5
  1.9 0.5 shard_map.73
  2.4 2.6 %collective-permute-start.4 = (bf16[4,1536]{1,0:T(4,128)(2,1)S(1)}, bf16[4,1536]{1,0:T(4,128)(2,1)S(1)}, u32[]{:S(2)}, u32[]{:S(2)}) collective-permute-start(bf16[4,1536]{1,0:T(4,128)(2,1)S(1)} %get-tuple-element.29), channel_id=1, source_target_pairs={{0,8},{8,0},{16,24},{24,16},{32,40},{40,32},{48,56},{56,48},{1,9},... | collective-permute-start | bytes 36872 | tf_op jit(solution)/shard_map/ppermute | solution.py:318
  5.0 6.5 %collective-permute-start.1 = (bf16[5,80,128]{2,1,0:T(8,128)(2,1)S(1)}, bf16[5,80,128]{2,1,0:T(8,128)(2,1)S(1)}, u32[]{:S(2)}, u32[]{:S(2)}) collective-permute-start(bf16[5,80,128]{2,1,0:T(8,128)(2,1)S(1)} %get-tuple-element.22), channel_id=1, source_target_pairs={{1,0},{2,1},{3,2},{4,3},{5,4},{6,5},{7,6},{9,8},{10,9},{11,10},{12... | collective-permute-start | bytes 307208 | tf_op jit(solution)/shard_map/ppermute | solution.py:328
  11.4 1.9 %collective-permute-start = (bf16[5,80,128]{2,1,0:T(8,128)(2,1)S(1)}, bf16[5,80,128]{2,1,0:T(8,128)(2,1)S(1)}, u32[]{:S(2)}, u32[]{:S(2)}) collective-permute-start(bf16[5,80,128]{2,1,0:T(8,128)(2,1)S(1)} %get-tuple-element.21.after_ref), channel_id=1, source_target_pairs={{0,1},{1,2},{2,3},{3,4},{4,5},{5,6},{6,7},{8,9},{9,10},{10,11},{11... | collective-permute-start | bytes 307208 | tf_op jit(solution)/shard_map/ppermute | solution.py:329
  13.4 0.0 collective-permute-done.4
  13.4 2.1 %collective-permute-start.5 = (bf16[8,1536]{1,0:T(8,128)(2,1)S(1)}, bf16[8,1536]{1,0:T(8,128)(2,1)S(1)}, u32[]{:S(2)}, u32[]{:S(2)}) collective-permute-start(bf16[8,1536]{1,0:T(8,128)(2,1)S(1)} %pad_maximum_fusion.2), channel_id=1, source_target_pairs={{0,16},{8,24},{16,0},{24,8},{32,48},{40,56},{48,32},{56,40},{1,17}... | collective-permute-start | bytes 73736 | tf_op jit(solution)/shard_map/ppermute | solution.py:318
  15.5 0.0 copy-start.2
  15.5 1.1 %copy-done.2 = f32[40,40,128]{2,1,0:T(8,128)S(1)} copy-done((f32[40,40,128]{2,1,0:T(8,128)S(1)}, f32[40,40,128]{2,1,0:T(8,128)}, u32[]{:S(2)}) %copy-start.2) | copy-done | bytes 819224
  16.7 0.0 copy-start.7
  16.7 0.4 shard_map.74
  17.1 0.0 collective-permute-done.1.right_ref
  17.1 11.2 %collective-permute-done.left_ref = bf16[5,80,128]{2,1,0:T(8,128)(2,1)S(1)} collective-permute-done((bf16[5,80,128]{2,1,0:T(8,128)(2,1)S(1)}, bf16[5,80,128]{2,1,0:T(8,128)(2,1)S(1)}, u32[]{:S(2)}, u32[]{:S(2)}) %collective-permute-start) | collective-permute-done | bytes 102432 | tf_op jit(solution)/shard_map/ppermute | solution.py:329
  28.3 0.2 shard_map.75
  28.6 0.0 copy-start.4
  28.6 9.1 %collective-permute-start.2 = (bf16[30,64,128]{2,1,0:T(8,128)(2,1)S(1)}, bf16[30,64,128]{2,1,0:T(8,128)(2,1)S(1)}, u32[]{:S(2)}, u32[]{:S(2)}) collective-permute-start(bf16[30,64,128]{2,1,0:T(8,128)(2,1)S(1)} %get-tuple-element.25), channel_id=1, source_target_pairs={{0,64},{64,128},{128,192},{192,256},{256,320},{320,384},{384,448},... | collective-permute-start | bytes 1474568 | tf_op jit(solution)/shard_map/ppermute | solution.py:329
  37.7 1.9 %collective-permute-start.3 = (bf16[30,64,128]{2,1,0:T(8,128)(2,1)S(1)}, bf16[30,64,128]{2,1,0:T(8,128)(2,1)S(1)}, u32[]{:S(2)}, u32[]{:S(2)}) collective-permute-start(bf16[30,64,128]{2,1,0:T(8,128)(2,1)S(1)} %get-tuple-element.28), channel_id=1, source_target_pairs={{64,0},{128,64},{192,128},{256,192},{320,256},{384,320},{448,384},... | collective-permute-start | bytes 1474568 | tf_op jit(solution)/shard_map/ppermute | solution.py:328
  39.6 0.0 collective-permute-done.5
  39.7 3.9 %collective-permute-start.7 = (bf16[16,1536]{1,0:T(8,128)(2,1)S(1)}, bf16[16,1536]{1,0:T(8,128)(2,1)S(1)}, u32[]{:S(2)}, u32[]{:S(2)}) collective-permute-start(bf16[16,1536]{1,0:T(8,128)(2,1)S(1)} %pad_maximum_fusion.1.rows_ref), channel_id=1, source_target_pairs={{0,32},{8,40},{16,48},{24,56},{32,0},{40,8},{48,16},{56,24},{1,33}... | collective-permute-start | bytes 147464 | tf_op jit(solution)/shard_map/ppermute | solution.py:318
  43.6 0.0 copy-done.7
  43.6 0.7 fusion
  44.3 3.2 %collective-permute-done.2.before_ref = bf16[30,64,128]{2,1,0:T(8,128)(2,1)S(1)} collective-permute-done((bf16[30,64,128]{2,1,0:T(8,128)(2,1)S(1)}, bf16[30,64,128]{2,1,0:T(8,128)(2,1)S(1)}, u32[]{:S(2)}, u32[]{:S(2)}) %collective-permute-start.2) | collective-permute-done | bytes 491552 | tf_op jit(solution)/shard_map/ppermute | solution.py:329
  47.5 3.8 %collective-permute-done.3.after_ref = bf16[30,64,128]{2,1,0:T(8,128)(2,1)S(1)} collective-permute-done((bf16[30,64,128]{2,1,0:T(8,128)(2,1)S(1)}, bf16[30,64,128]{2,1,0:T(8,128)(2,1)S(1)}, u32[]{:S(2)}, u32[]{:S(2)}) %collective-permute-start.3) | collective-permute-done | bytes 491552 | tf_op jit(solution)/shard_map/ppermute | solution.py:328
  51.3 0.3 shard_map.76
  51.5 5.1 %collective-permute-start.6 = (bf16[24,208,128]{2,1,0:T(8,128)(2,1)S(1)}, bf16[24,208,128]{2,1,0:T(8,128)(2,1)S(1)}, u32[]{:S(2)}, u32[]{:S(2)}) collective-permute-start(bf16[24,208,128]{2,1,0:T(8,128)(2,1)S(1)} %get-tuple-element.30), channel_id=1, source_target_pairs={{0,8},{8,16},{16,24},{24,32},{32,40},{40,48},{48,56},{1,9},{9,17},... | collective-permute-start | bytes 3833864 | tf_op jit(solution)/shard_map/ppermute | solution.py:329
  56.6 1.9 %collective-permute-start.8 = (bf16[24,208,128]{2,1,0:T(8,128)(2,1)S(1)}, bf16[24,208,128]{2,1,0:T(8,128)(2,1)S(1)}, u32[]{:S(2)}, u32[]{:S(2)}) collective-permute-start(bf16[24,208,128]{2,1,0:T(8,128)(2,1)S(1)} %get-tuple-element.33), channel_id=1, source_target_pairs={{8,0},{16,8},{24,16},{32,24},{40,32},{48,40},{56,48},{9,1},{17,9},... | collective-permute-start | bytes 3833864 | tf_op jit(solution)/shard_map/ppermute | solution.py:328
  58.5 0.0 collective-permute-done.7
  58.6 0.0 copy-done.4
  58.6 3.3 %shard_map.77 = (bf16[3,640,208]{2,1,0:T(8,128)(2,1)S(1)}, bf16[24,32,416]{2,1,0:T(8,128)(2,1)S(1)}, bf16[24,32,416]{2,1,0:T(8,128)(2,1)S(1)}, bf16[3,1536,128]{2,1,0:T(8,128)(2,1)S(1)}) custom-call(s32[3]{0:T(128)S(1)} %bitcast.3, bf16[32,1536]{1,0:T(8,128)(2,1)S(1)} %pad_maximum_fusion.table_ref, bf16[128,384]{1,0:T(8,128)(2,1)S(1)} %copy-done.4), custom_call_target="tpu_custom_call" | custom-call | tf_op jit(solution)/shard_map/pallas_call | solution.py:155
  61.9 0.0 copy-start
  61.9 0.0 copy-start.3
  62.0 0.0 copy-start.6
  62.0 8.2 %shard_map.78.own_ref = bf16[3,8,160,1920]{3,2,1,0:T(8,128)(2,1)S(1)} custom-call(s32[1]{0:T(128)} %bitcast.1.live_ref, bf16[30,208,128]{2,1,0:T(8,128)(2,1)S(1)} %get-tuple-element.31.own_ref, bf16[3,640,208]{2,1,0:T(8,128)(2,1)S(1)} %get-tuple-element.32.a1_ref), custom_call_target="tpu_custom_call" | custom-call | flops 8000000000 | bytes 2000000 | tf_op jit(solution)/shard_map/pallas_call | solution.py:227
  70.2 0.6 collective-permute-done.6.left_ref
  70.8 4.4 %collective-permute-done.8.right_ref = bf16[24,208,128]{2,1,0:T(8,128)(2,1)S(1)} collective-permute-done((bf16[24,208,128]{2,1,0:T(8,128)(2,1)S(1)}, bf16[24,208,128]{2,1,0:T(8,128)(2,1)S(1)}, u32[]{:S(2)}, u32[]{:S(2)}) %collective-permute-start.8) | collective-permute-done | bytes 1277984 | tf_op jit(solution)/shard_map/ppermute | solution.py:328
  75.2 0.0 copy-done
  75.2 0.0 copy-done.3
  75.2 0.0 copy-done.6
  75.2 30.0 %shard_map.79 = f32[40,40,128]{2,1,0:T(8,128)} custom-call(s32[1]{0:T(128)} %bitcast.1.live_ref, bf16[24,208,128]{2,1,0:T(8,128)(2,1)S(1)} %collective-permute-done.6.left_ref, bf16[3,8,160,1920]{3,2,1,0:T(8,128)(2,1)S(1)} %shard_map.78.own_ref, bf16[24,208,128]{2,1,0:T(8,128)(2,1)S(1)} %collective-permute-done.8.right_ref, ...), custom_call_target="tpu_custom_call" | custom-call | tf_op jit(solution)/shard_map/pallas_call | solution.py:302
  (6 shorter events, 0.1 us)
Async XLA Ops:
  0.0 1.1 %copy-start.1 = (f32[40,40,128]{2,1,0:T(8,128)S(1)}, f32[40,40,128]{2,1,0:T(8,128)}, u32[]{:S(2)}) copy-start(f32[40,40,128]{2,1,0:T(8,128)} %reflect_ref.3) | copy-start | bytes 2457604
  1.1 0.7 copy-start.5
  2.4 11.0 %collective-permute-start.4 = (bf16[4,1536]{1,0:T(4,128)(2,1)S(1)}, bf16[4,1536]{1,0:T(4,128)(2,1)S(1)}, u32[]{:S(2)}, u32[]{:S(2)}) collective-permute-start(bf16[4,1536]{1,0:T(4,128)(2,1)S(1)} %get-tuple-element.29), channel_id=1, source_target_pairs={{0,8},{8,0},{16,24},{24,16},{32,40},{40,32},{48,56},{56,48},{1,9},... | collective-permute-start | bytes 36872 | tf_op jit(solution)/shard_map/ppermute | solution.py:318
  5.0 12.1 %collective-permute-start.1 = (bf16[5,80,128]{2,1,0:T(8,128)(2,1)S(1)}, bf16[5,80,128]{2,1,0:T(8,128)(2,1)S(1)}, u32[]{:S(2)}, u32[]{:S(2)}) collective-permute-start(bf16[5,80,128]{2,1,0:T(8,128)(2,1)S(1)} %get-tuple-element.22), channel_id=1, source_target_pairs={{1,0},{2,1},{3,2},{4,3},{5,4},{6,5},{7,6},{9,8},{10,9},{11,10},{12... | collective-permute-start | bytes 307208 | tf_op jit(solution)/shard_map/ppermute | solution.py:328
  11.4 16.9 %collective-permute-start = (bf16[5,80,128]{2,1,0:T(8,128)(2,1)S(1)}, bf16[5,80,128]{2,1,0:T(8,128)(2,1)S(1)}, u32[]{:S(2)}, u32[]{:S(2)}) collective-permute-start(bf16[5,80,128]{2,1,0:T(8,128)(2,1)S(1)} %get-tuple-element.21.after_ref), channel_id=1, source_target_pairs={{0,1},{1,2},{2,3},{3,4},{4,5},{5,6},{6,7},{8,9},{9,10},{10,11},{11... | collective-permute-start | bytes 307208 | tf_op jit(solution)/shard_map/ppermute | solution.py:329
  13.4 26.2 %collective-permute-start.5 = (bf16[8,1536]{1,0:T(8,128)(2,1)S(1)}, bf16[8,1536]{1,0:T(8,128)(2,1)S(1)}, u32[]{:S(2)}, u32[]{:S(2)}) collective-permute-start(bf16[8,1536]{1,0:T(8,128)(2,1)S(1)} %pad_maximum_fusion.2), channel_id=1, source_target_pairs={{0,16},{8,24},{16,0},{24,8},{32,48},{40,56},{48,32},{56,40},{1,17}... | collective-permute-start | bytes 73736 | tf_op jit(solution)/shard_map/ppermute | solution.py:318
  15.5 1.1 %copy-start.2 = (f32[40,40,128]{2,1,0:T(8,128)S(1)}, f32[40,40,128]{2,1,0:T(8,128)}, u32[]{:S(2)}) copy-start(f32[40,40,128]{2,1,0:T(8,128)} %reflect_ref.3) | copy-start | bytes 2457604
  16.7 27.0 %copy-start.7 = (s32[1,1,1,3]{3,2,1,0:T(1,128)S(1)}, s32[1,1,1,3]{3,2,1,0:T(1,128)}, u32[]{:S(2)}) copy-start(s32[1,1,1,3]{3,2,1,0:T(1,128)} %param.11) | copy-start | bytes 40
  28.6 30.0 %copy-start.4 = (bf16[128,384]{1,0:T(8,128)(2,1)S(1)}, bf16[128,384]{1,0:T(8,128)(2,1)}, u32[]{:S(2)}) copy-start(bf16[128,384]{1,0:T(8,128)(2,1)} %constant.18.clone.map_ref) | copy-start | bytes 294916
  28.6 18.9 %collective-permute-start.2 = (bf16[30,64,128]{2,1,0:T(8,128)(2,1)S(1)}, bf16[30,64,128]{2,1,0:T(8,128)(2,1)S(1)}, u32[]{:S(2)}, u32[]{:S(2)}) collective-permute-start(bf16[30,64,128]{2,1,0:T(8,128)(2,1)S(1)} %get-tuple-element.25), channel_id=1, source_target_pairs={{0,64},{64,128},{128,192},{192,256},{256,320},{320,384},{384,448},... | collective-permute-start | bytes 1474568 | tf_op jit(solution)/shard_map/ppermute | solution.py:329
  37.7 13.6 %collective-permute-start.3 = (bf16[30,64,128]{2,1,0:T(8,128)(2,1)S(1)}, bf16[30,64,128]{2,1,0:T(8,128)(2,1)S(1)}, u32[]{:S(2)}, u32[]{:S(2)}) collective-permute-start(bf16[30,64,128]{2,1,0:T(8,128)(2,1)S(1)} %get-tuple-element.28), channel_id=1, source_target_pairs={{64,0},{128,64},{192,128},{256,192},{320,256},{384,320},{448,384},... | collective-permute-start | bytes 1474568 | tf_op jit(solution)/shard_map/ppermute | solution.py:328
  39.7 18.8 %collective-permute-start.7 = (bf16[16,1536]{1,0:T(8,128)(2,1)S(1)}, bf16[16,1536]{1,0:T(8,128)(2,1)S(1)}, u32[]{:S(2)}, u32[]{:S(2)}) collective-permute-start(bf16[16,1536]{1,0:T(8,128)(2,1)S(1)} %pad_maximum_fusion.1.rows_ref), channel_id=1, source_target_pairs={{0,32},{8,40},{16,48},{24,56},{32,0},{40,8},{48,16},{56,24},{1,33}... | collective-permute-start | bytes 147464 | tf_op jit(solution)/shard_map/ppermute | solution.py:318
  51.5 19.2 %collective-permute-start.6 = (bf16[24,208,128]{2,1,0:T(8,128)(2,1)S(1)}, bf16[24,208,128]{2,1,0:T(8,128)(2,1)S(1)}, u32[]{:S(2)}, u32[]{:S(2)}) collective-permute-start(bf16[24,208,128]{2,1,0:T(8,128)(2,1)S(1)} %get-tuple-element.30), channel_id=1, source_target_pairs={{0,8},{8,16},{16,24},{24,32},{32,40},{40,48},{48,56},{1,9},{9,17},... | collective-permute-start | bytes 3833864 | tf_op jit(solution)/shard_map/ppermute | solution.py:329
  56.6 18.6 %collective-permute-start.8 = (bf16[24,208,128]{2,1,0:T(8,128)(2,1)S(1)}, bf16[24,208,128]{2,1,0:T(8,128)(2,1)S(1)}, u32[]{:S(2)}, u32[]{:S(2)}) collective-permute-start(bf16[24,208,128]{2,1,0:T(8,128)(2,1)S(1)} %get-tuple-element.33), channel_id=1, source_target_pairs={{8,0},{16,8},{24,16},{32,24},{40,32},{48,40},{56,48},{9,1},{17,9},... | collective-permute-start | bytes 3833864 | tf_op jit(solution)/shard_map/ppermute | solution.py:328
  61.9 13.2 %copy-start = (s32[2,40,40,128]{3,2,1,0:T(8,128)S(1)}, s32[2,40,40,128]{3,2,1,0:T(8,128)}, u32[]{:S(2)}) copy-start(s32[2,40,40,128]{3,2,1,0:T(8,128)} %slot_ref.1) | copy-start | bytes 4915204
  61.9 13.2 %copy-start.3 = (bf16[2,40,40,128]{3,2,1,0:T(8,128)(2,1)S(1)}, bf16[2,40,40,128]{3,2,1,0:T(8,128)(2,1)}, u32[]{:S(2)}) copy-start(bf16[2,40,40,128]{3,2,1,0:T(8,128)(2,1)} %weights_ref.1) | copy-start | bytes 2457604
  62.0 13.2 %copy-start.6 = (bf16[4,416]{1,0:T(4,128)(2,1)S(1)}, bf16[4,416]{1,0:T(4,128)(2,1)}, u32[]{:S(2)}) copy-start(bf16[4,416]{1,0:T(4,128)(2,1)} %constant.19.clone.mask_ref) | copy-start | bytes 9988

commit v8 on v7

--- a/solution.py
+++ b/solution.py
@@ -65,11 +65,14 @@
     def between(first, last):
         return (lane8 >= first) & (lane8 < last)
 
-    plain = low & between(0, 32)
-    by_32 = (low & between(64, 104)) | (~low & between(32, 64))
-    by_72 = ~low & between(104, 128)
-    end_72 = (low & between(16, 48)) | (~low & between(0, 16))
-    end_104 = ~low & between(48, 80)
+    parts = (
+        (96, low & between(0, 40), None),
+        (8, ~low & between(40, 80), None),
+        (80, low & between(80, 112), None),
+        (112, ~low & between(112, 128), ~low & between(0, 16)),
+        (72, None, low & between(16, 48)),
+        (104, None, ~low & between(48, 80)),
+    )
     row_z = lax.broadcasted_iota(jnp.int32, (128, 128), 0)
     lane_z = lax.broadcasted_iota(jnp.int32, (128, 128), 1)
     inside = lane_z <= row_z
@@ -87,14 +90,13 @@
         for b in range(0, XB, 2):
             ends = ([], [])
             for c in (b, b + 1):
-                turned = [
-                    pltpu.roll(base, (XO * c + k) % 128, 1) if (XO * c + k) % 128 else base
-                    for k in (0, 32, 72, 104)
-                ]
-                ends[0].append(
-                    jnp.where(plain, turned[0], jnp.where(by_32, turned[1], jnp.where(by_72, turned[2], 0.0)))
-                )
-                ends[1].append(jnp.where(end_72, turned[2], jnp.where(end_104, turned[3], 0.0)))
+                first = second = jnp.zeros((8, 128), jnp.float32)
+                for shift, here, there in parts:
+                    turned = pltpu.roll(base, (XO * c + shift) % 128, 1) if (XO * c + shift) % 128 else base
+                    first = first if here is None else jnp.where(here, turned, first)
+                    second = second if there is None else jnp.where(there, turned, second)
+                ends[0].append(first)
+                ends[1].append(second)
             rows = pl.ds(pl.multiple_of(r * (XB * 8) + b * 8, 16), 16)
             a1_ref[slot, rows, 0:128] = jnp.concatenate(ends[0], axis=0).astype(jnp.bfloat16)
             a1_ref[slot, rows, 128:ROWS] = jnp.concatenate(ends[1], axis=0)[:, : ROWS - 128].astype(jnp.bfloat16)
@@ -170,14 +172,13 @@
     return pltpu.roll(value, 64, 1)
 
 
-def stage_x(slot, part, a1_ref, put, offset):
+def stage_x(slot, pairs, fetch, a1_ref, put, offset):
     low = lax.broadcasted_iota(jnp.int32, (8, NARROW), 1) < 64
-    pairs = part.shape[0] * 2 // 3
 
     def step(i, carry):
         g = 2 * i
         rhs = jnp.concatenate(
-            [part[4 * i], part[4 * i + 1], part[4 * i + 2], part[4 * i + 3], part[pairs + g], part[pairs + g + 1]],
+            [fetch(4 * i + k) for k in range(4)] + [fetch(pairs + g + k) for k in range(2)],
             axis=1,
         )
         made = jnp.dot(a1_ref[slot], rhs, preferred_element_type=jnp.float32)
@@ -211,31 +212,38 @@
     lax.fori_loop(0, pairs // 4, step, 0)
 
 
-def own_kernel(live_ref, own_ref, a1_ref, out_ref):
+def own_kernel(live_ref, cells_ref, tail_ref, before_ref, after_ref, a1_ref, out_ref, own_ref):
+    own_ref[:20] = cells_ref[...]
+    own_ref[20:] = tail_ref[...]
+
+    def fetch(i):
+        return jnp.concatenate([own_ref[i], before_ref[i], after_ref[i]], axis=0)
+
     def one_slot(slot, carry):
         def put(r, rows, lanes, value):
             out_ref[slot, r, rows, lanes] = value
 
-        stage_x(slot, own_ref, a1_ref, put, 0)
+        stage_x(slot, 20, fetch, a1_ref, put, 0)
         return carry
 
     lax.fori_loop(0, live_ref[0], one_slot, 0)
 
 
-def blur_own(live, own, a1):
+def blur_own(live, cells, a1):
     vmem = pl.BlockSpec(memory_space=pltpu.VMEM)
     return pl.pallas_call(
         own_kernel,
         out_shape=jax.ShapeDtypeStruct((NEED, R, Y * XO, LANES), jnp.bfloat16),
-        in_specs=[pl.BlockSpec(memory_space=pltpu.SMEM), vmem, vmem],
+        in_specs=[pl.BlockSpec(memory_space=pltpu.SMEM)] + [vmem] * 5,
         out_specs=vmem,
+        scratch_shapes=[pltpu.VMEM((30, 80, NARROW), jnp.bfloat16)],
         compiler_params=pltpu.CompilerParams(vmem_limit_bytes=OWN_LIMIT),
         cost_estimate=pl.CostEstimate(flops=8_000_000_000, bytes_accessed=2_000_000, transcendentals=0),
-    )(live, own, a1)
+    )(live, *cells, a1)
 
 
 def blur_kernel(
-    live_ref, left_ref, own_ref, right_ref, a1_ref, a2_ref, a2b_ref, mask_ref, bz_ref,
+    live_ref, left_ref, left_ends, right_ref, right_ends, own_ref, a1_ref, a2_ref, a2b_ref, mask_ref, bz_ref,
     weights_ref, slot_ref, out_ref, line_x, line_y, band_y,
 ):
     out_ref[...] = jnp.zeros_like(out_ref)
@@ -247,8 +255,12 @@
         def put(r, rows, lanes, value):
             line_x[r, rows, lanes] = value
 
-        stage_x(slot, left_ref, a1_ref, put, 0)
-        stage_x(slot, right_ref, a1_ref, put, 8)
+        for cells, ends, offset in ((left_ref, left_ends, 0), (right_ref, right_ends, 8)):
+
+            def fetch(i):
+                return jnp.concatenate([cells[i], ends[i]], axis=0)
+
+            stage_x(slot, 16, fetch, a1_ref, put, offset)
 
         def pair(q, carry):
             made = []
@@ -295,14 +307,14 @@
 
 def blur(live, cells, bands, weights, cell_slot):
     a1, a2, a2b, bz = bands
-    left, own, right = cells
-    own = blur_own(live, own, a1)
+    inside, sides = cells
+    own = blur_own(live, inside, a1)
     vmem = pl.BlockSpec(memory_space=pltpu.VMEM)
     mask = same_lane()
     return pl.pallas_call(
         blur_kernel,
         out_shape=jax.ShapeDtypeStruct((X, Y, Z), jnp.float32),
-        in_specs=[pl.BlockSpec(memory_space=pltpu.SMEM)] + [vmem] * 10,
+        in_specs=[pl.BlockSpec(memory_space=pltpu.SMEM)] + [vmem] * 12,
         out_specs=vmem,
         scratch_shapes=[
             pltpu.VMEM((R, 2 * HALF * XO, LANES), jnp.bfloat16),
@@ -310,7 +322,7 @@
             pltpu.VMEM((2, Y * XO, EXT * XO), jnp.bfloat16),
         ],
         compiler_params=pltpu.CompilerParams(vmem_limit_bytes=BLUR_LIMIT),
-    )(live, left, own, right, a1, a2, a2b, mask, bz, weights, cell_slot)
+    )(live, *sides, own, a1, a2, a2b, mask, bz, weights, cell_slot)
 
 
 def doubled(rows, axis, bit):
@@ -334,8 +346,7 @@
     return lax.broadcasted_iota(jnp.int32, (1, NARROW), 1) // HALF
 
 
-def ends_kernel(reflect_ref, factors_ref, shallower_ref, deeper_ref, rows_ref):
-    rows_ref[...] = factors_ref[...]
+def ends_kernel(reflect_ref, shallower_ref, deeper_ref):
     part = lane_part()
     for g in range(Y // 8):
         rows = [reflect_ref[:, 8 * g + k, :] for k in range(8)]
@@ -352,16 +363,16 @@
             ref[g] = jnp.concatenate(packed, axis=0).astype(jnp.bfloat16)
 
 
-def depth_ends(reflect, factors):
-    vmem = pl.BlockSpec(memory_space=pltpu.VMEM)
-    shapes = [(5, 80, NARROW), (5, 80, NARROW), factors.shape]
+def depth_ends(reflect):
+    vmem = pl.BlockSpec(memory_space=pltpu.VMEM)
+    shapes = [(5, 80, NARROW), (5, 80, NARROW)]
     return pl.pallas_call(
         ends_kernel,
         out_shape=[jax.ShapeDtypeStruct(shape, jnp.bfloat16) for shape in shapes],
-        in_specs=[vmem] * 2,
-        out_specs=[vmem] * 3,
+        in_specs=[vmem],
+        out_specs=[vmem] * 2,
         compiler_params=pltpu.CompilerParams(vmem_limit_bytes=SMALL_LIMIT),
-    )(reflect, factors)
+    )(reflect)
 
 
 def cut_kernel(reflect_ref, after_ref, own_ref, next_ref, last_ref):
@@ -385,8 +396,12 @@
     )(reflect, after)
 
 
-def tail_kernel(left_ref, right_ref, main_next, main_last, own_ref, next_ref, last_ref):
+def tail_kernel(
+    left_ref, right_ref, cells_ref, main_next, main_last, own_ref, next_ref, last_ref, across_next, across_last
+):
     part = lane_part()
+    across_next[:16] = cells_ref[4:]
+    across_last[:16] = cells_ref[:16]
     next_ref[:20] = main_next[...]
     last_ref[:20] = main_last[...]
     for g in range(5):
@@ -398,7 +413,12 @@
                 shift = ((k - at) * HALF) % NARROW
                 turned = pltpu.roll(source, shift, 1) if shift else source
                 value = jnp.where(part == k, turned, value)
-            own_ref[2 * g + a] = value.astype(jnp.bfloat16)
+            tail = value.astype(jnp.bfloat16)
+            own_ref[2 * g + a] = tail
+            if g > 0:
+                across_next[16 + 2 * g + a - 2] = tail
+            if g < 4:
+                across_last[16 + 2 * g + a] = tail
             next_ref[20 + 2 * g + a] = jnp.concatenate(
                 [value[X - HALF : X], value[2 * X - HALF :]], axis=0
             ).astype(jnp.bfloat16)
@@ -407,58 +427,53 @@
             ).astype(jnp.bfloat16)
 
 
-def unpack_tail(left, right, main_next, main_last):
-    shapes = [(10, 80, NARROW), (30, 64, NARROW), (30, 64, NARROW)]
+def unpack_tail(left, right, own, main_next, main_last):
+    shapes = [(10, 80), (30, 64), (30, 64), (24, 80), (24, 80)]
     vmem = pl.BlockSpec(memory_space=pltpu.VMEM)
     return pl.pallas_call(
         tail_kernel,
-        out_shape=[jax.ShapeDtypeStruct(shape, jnp.bfloat16) for shape in shapes],
-        in_specs=[vmem] * 4,
-        out_specs=[vmem] * 3,
+        out_shape=[jax.ShapeDtypeStruct(shape + (NARROW,), jnp.bfloat16) for shape in shapes],
+        in_specs=[vmem] * 5,
+        out_specs=[vmem] * 5,
         compiler_params=pltpu.CompilerParams(vmem_limit_bytes=SMALL_LIMIT),
-    )(left, right, main_next, main_last)
-
-
-def join_kernel(before_ref, own_ref, tail_ref, after_ref, rows_ref, all_ref, next_ref, last_ref):
+    )(left, right, own, main_next, main_last)
+
+
+def join_kernel(before_ref, after_ref, rows_ref, left_ref, right_ref, next_ref, last_ref):
     for ref, to, at, count in (
-        (all_ref, 0, 0, 30),
         (next_ref, 0, 4, 16),
         (next_ref, 16, 22, 8),
         (last_ref, 0, 0, 16),
         (last_ref, 16, 20, 8),
     ):
         ref[to : to + count, 0:64, :] = before_ref[at : at + count]
-        ref[to : to + count, 144:208, :] = after_ref[at : at + count]
-        mains = min(max(20 - at, 0), count)
-        if mains:
-            ref[to : to + mains, 64:144, :] = own_ref[at : at + mains]
-        if count > mains:
-            first = max(at - 20, 0)
-            ref[to + mains : to + count, 64:144, :] = tail_ref[first : first + count - mains]
-
-
-def join(before, own, tail, after, rows):
+        ref[to : to + count, 64:128, :] = after_ref[at : at + count]
+
+
+def join(before, after, rows, left, right):
     vmem = pl.BlockSpec(memory_space=pltpu.VMEM)
     return pl.pallas_call(
         join_kernel,
-        out_shape=[jax.ShapeDtypeStruct((n, ROWS, NARROW), jnp.bfloat16) for n in (30, 24, 24)],
-        in_specs=[vmem] * 4 + [pl.BlockSpec(memory_space=pl.ANY)],
-        out_specs=[vmem] * 3,
-        compiler_params=pltpu.CompilerParams(vmem_limit_bytes=12 * 1024 * 1024),
-    )(before, own, tail, after, rows)
+        out_shape=[jax.ShapeDtypeStruct((24, 128, NARROW), jnp.bfloat16)] * 2,
+        in_specs=[vmem] * 2 + [pl.BlockSpec(memory_space=pl.ANY)] * 3,
+        out_specs=[vmem] * 2,
+        compiler_params=pltpu.CompilerParams(vmem_limit_bytes=SMALL_LIMIT),
+    )(before, after, rows, left, right)
 
 
 def exchange(reflect, factors):
-    shallower, deeper, rows = depth_ends(reflect, factors)
+    shallower, deeper = depth_ends(reflect)
     above, below = both_ways(deeper, shallower, "gz")
-    own, to_next, to_last = cut(reflect, deeper)
-    rows = doubled(doubled(rows, "xl", 1), "xl", 2)
-    tail, to_next, to_last = unpack_tail(above, below, to_next, to_last)
+    rows = doubled(factors, "xl", 1)
+    own, to_next, to_last = cut(reflect, shallower)
+    rows = doubled(rows, "xl", 2)
+    tail, to_next, to_last, across_next, across_last = unpack_tail(above, below, own, to_next, to_last)
     before, after = both_ways(to_next, to_last, "il")
-    block, to_next, to_last = join(before, own, tail, after, rows)
+    left, right = both_ways(across_next, across_last, "xl")
+    to_next, to_last = join(before, after, rows, left, right)
+    left_ends, right_ends = both_ways(to_next, to_last, "xl")
     rows = doubled(rows, "xl", 4)
-    left, right = both_ways(to_next, to_last, "xl")
-    return (left, block, right), rows
+    return ((own, tail, before, after), (left, left_ends, right, right_ends)), rows
 
 
 def per_device(reflect, weights, cell_slot, factors, reader_list):

time: 106 us -> 102 us (0.962)
  the two profiles are of different devices: /device:TPU:425 before, /device:TPU:424 now
where the time goes in v8:
time: 102 us; the launch traced here: 101 us
  Pallas kernels  43.9 us (43%)
  starting transfers between devices  39.2 us (38%)
  waiting for transfers between devices  12.5 us (12%)
  local copies, waits for them, and re-layouts  3.01 us (3%)
  other arithmetic  2.3 us (2%)
    pallas_call x1, Pallas kernels, blur(): pl.pallas_call(blur_kernel, out_shape=jax.ShapeDtypeStruct((X, Y, Z), jnp...  30.1 us
    ppermute x4, starting transfers between devices, both_ways(): lax.ppermute(to_next, axis, [(i, (i + 1) % count) for i in range(ends)])  15.8 us
    ppermute x4, starting transfers between devices, both_ways(): lax.ppermute(to_last, axis, [((i + 1) % count, i) for i in range(ends)])  14.9 us
    ppermute x3, starting transfers between devices, doubled(): other = lax.ppermute(rows, axis, [(i, i ^ bit) for i in range(count)])  8.47 us
    pallas_call x1, Pallas kernels, blur_own(): pl.pallas_call(own_kernel, out_shape=jax.ShapeDtypeStruct((NEED, R, Y * X...  8.28 us
    ppermute x4, waiting for transfers between devices, both_ways(): lax.ppermute(to_next, axis, [(i, (i + 1) % count) for i in range(ends)])  6.68 us
    ppermute x4, waiting for transfers between devices, both_ways(): lax.ppermute(to_last, axis, [((i + 1) % count, i) for i in range(ends)])  4.02 us
    pallas_call x1, Pallas kernels, make_bands(): pl.pallas_call(bands_kernel, out_shape=[jax.ShapeDtypeStruct(shape, jnp.b...  3.15 us
  transfers between devices with their start and end apart: 11, of which 4 were waited for; matrix products, arithmetic and copies ran while one was open for 2% of the time, Pallas kernels for 14%

profile of v8, /device:TPU:424, one launch (start us, length us, event | category | flops | bytes accessed | tf_op | source)
XLA Modules:
  0.0 101.1 jit_solution(5230766246736681208)
XLA Ops:
  0.0 1.9 %collective-permute-start.5 = (bf16[4,1536]{1,0:T(4,128)(2,1)}, bf16[4,1536]{1,0:T(4,128)(2,1)S(1)}, u32[]{:S(2)}, u32[]{:S(2)}) collective-permute-start(bf16[4,1536]{1,0:T(4,128)(2,1)} %param.10), channel_id=1, source_target_pairs={{0,8},{8,0},{16,24},{24,16},{32,40},{40,32},{48,56},{56,48},{1,9},... | collective-permute-start | bytes 36872 | tf_op jit(solution)/shard_map/ppermute | solution.py:330
  1.9 0.0 copy-start.1
  1.9 1.1 %copy-done.1 = f32[40,40,128]{2,1,0:T(8,128)S(1)} copy-done((f32[40,40,128]{2,1,0:T(8,128)S(1)}, f32[40,40,128]{2,1,0:T(8,128)}, u32[]{:S(2)}) %copy-start.1) | copy-done | bytes 819224
  3.1 0.5 shard_map.73
  3.6 6.7 %collective-permute-start.1 = (bf16[5,80,128]{2,1,0:T(8,128)(2,1)S(1)}, bf16[5,80,128]{2,1,0:T(8,128)(2,1)S(1)}, u32[]{:S(2)}, u32[]{:S(2)}) collective-permute-start(bf16[5,80,128]{2,1,0:T(8,128)(2,1)S(1)} %get-tuple-element.22.after_ref), channel_id=1, source_target_pairs={{1,0},{2,1},{3,2},{4,3},{5,4},{6,5},{7,6},{9,8},{10,9},{11,10},{12... | collective-permute-start | bytes 307208 | tf_op jit(solution)/shard_map/ppermute | solution.py:340
  10.3 1.9 %collective-permute-start = (bf16[5,80,128]{2,1,0:T(8,128)(2,1)S(1)}, bf16[5,80,128]{2,1,0:T(8,128)(2,1)S(1)}, u32[]{:S(2)}, u32[]{:S(2)}) collective-permute-start(bf16[5,80,128]{2,1,0:T(8,128)(2,1)S(1)} %get-tuple-element.21), channel_id=1, source_target_pairs={{0,1},{1,2},{2,3},{3,4},{4,5},{5,6},{6,7},{8,9},{9,10},{10,11},{11... | collective-permute-start | bytes 307208 | tf_op jit(solution)/shard_map/ppermute | solution.py:341
  12.3 0.0 collective-permute-done.5
  12.3 0.7 broadcast_select_fusion.5
  13.0 2.4 %collective-permute-start.6 = (bf16[8,1536]{1,0:T(8,128)(2,1)S(1)}, bf16[8,1536]{1,0:T(8,128)(2,1)S(1)}, u32[]{:S(2)}, u32[]{:S(2)}) collective-permute-start(bf16[8,1536]{1,0:T(8,128)(2,1)S(1)} %pad_maximum_fusion.2), channel_id=1, source_target_pairs={{0,16},{8,24},{16,0},{24,8},{32,48},{40,56},{48,32},{56,40},{1,17}... | collective-permute-start | bytes 73736 | tf_op jit(solution)/shard_map/ppermute | solution.py:330
  15.4 0.0 copy-start.2
  15.4 1.1 %copy-done.2 = f32[40,40,128]{2,1,0:T(8,128)S(1)} copy-done((f32[40,40,128]{2,1,0:T(8,128)S(1)}, f32[40,40,128]{2,1,0:T(8,128)}, u32[]{:S(2)}) %copy-start.2) | copy-done | bytes 819224
  16.5 0.0 copy-start.6
  16.5 0.4 shard_map.74
  17.0 1.8 %collective-permute-done.6 = bf16[8,1536]{1,0:T(8,128)(2,1)S(1)} collective-permute-done((bf16[8,1536]{1,0:T(8,128)(2,1)S(1)}, bf16[8,1536]{1,0:T(8,128)(2,1)S(1)}, u32[]{:S(2)}, u32[]{:S(2)}) %collective-permute-start.6) | collective-permute-done | bytes 24608 | tf_op jit(solution)/shard_map/ppermute | solution.py:330
  18.8 0.0 copy-start.9
  18.8 4.2 %collective-permute-start.10 = (bf16[16,1536]{1,0:T(8,128)(2,1)S(1)}, bf16[16,1536]{1,0:T(8,128)(2,1)}, u32[]{:S(2)}, u32[]{:S(2)}) collective-permute-start(bf16[16,1536]{1,0:T(8,128)(2,1)S(1)} %pad_maximum_fusion.1.rows_ref), channel_id=1, source_target_pairs={{0,32},{8,40},{16,48},{24,56},{32,0},{40,8},{48,16},{56,24},{1,33}... | collective-permute-start | bytes 147464 | tf_op jit(solution)/shard_map/ppermute | solution.py:330
  23.0 0.0 collective-permute-done.1.right_ref
  23.0 5.0 %collective-permute-done.left_ref = bf16[5,80,128]{2,1,0:T(8,128)(2,1)S(1)} collective-permute-done((bf16[5,80,128]{2,1,0:T(8,128)(2,1)S(1)}, bf16[5,80,128]{2,1,0:T(8,128)(2,1)S(1)}, u32[]{:S(2)}, u32[]{:S(2)}) %collective-permute-start) | collective-permute-done | bytes 102432 | tf_op jit(solution)/shard_map/ppermute | solution.py:341
  28.1 0.0 copy-done.9
  28.1 0.0 copy-start.4
  28.1 1.3 %shard_map.75 = (bf16[10,80,128]{2,1,0:T(8,128)(2,1)S(1)}, bf16[30,64,128]{2,1,0:T(8,128)(2,1)}, bf16[30,64,128]{2,1,0:T(8,128)(2,1)}, bf16[24,80,128]{2,1,0:T(8,128)(2,1)S(1)}, bf16[24,80,128]{2,1,0:T(8,128)(2,1)S(1)}) custom-call(bf16[5,80,128]{2,1,0:T(8,128)(2,1)S(1)} %collective-permute-done.left_ref, ...), custom_call_target="tpu_custom_call" | custom-call | tf_op jit(solution)/shard_map/pallas_call | solution.py:433
  29.3 0.0 copy-start.7
  29.3 0.7 copy-done.7
  30.0 9.0 %collective-permute-start.3 = (bf16[30,64,128]{2,1,0:T(8,128)(2,1)}, bf16[30,64,128]{2,1,0:T(8,128)(2,1)S(1)}, u32[]{:S(2)}, u32[]{:S(2)}) collective-permute-start(bf16[30,64,128]{2,1,0:T(8,128)(2,1)} %get-tuple-element.27), channel_id=1, source_target_pairs={{0,64},{64,128},{128,192},{192,256},{256,320},{320,384},{384,448},... | collective-permute-start | bytes 1474568 | tf_op jit(solution)/shard_map/ppermute | solution.py:341
  39.0 1.9 %collective-permute-start.4 = (bf16[30,64,128]{2,1,0:T(8,128)(2,1)}, bf16[30,64,128]{2,1,0:T(8,128)(2,1)S(1)}, u32[]{:S(2)}, u32[]{:S(2)}) collective-permute-start(bf16[30,64,128]{2,1,0:T(8,128)(2,1)} %get-tuple-element.28), channel_id=1, source_target_pairs={{64,0},{128,64},{192,128},{256,192},{320,256},{384,320},{448,384},... | collective-permute-start | bytes 1474568 | tf_op jit(solution)/shard_map/ppermute | solution.py:340
  40.9 1.9 %collective-permute-start.2 = (bf16[24,80,128]{2,1,0:T(8,128)(2,1)S(1)}, bf16[24,80,128]{2,1,0:T(8,128)(2,1)S(1)}, u32[]{:S(2)}, u32[]{:S(2)}) collective-permute-start(bf16[24,80,128]{2,1,0:T(8,128)(2,1)S(1)} %get-tuple-element.26), channel_id=1, source_target_pairs={{0,8},{8,16},{16,24},{24,32},{32,40},{40,48},{48,56},{1,9},{9,17},... | collective-permute-start | bytes 1474568 | tf_op jit(solution)/shard_map/ppermute | solution.py:341
  42.9 3.6 %collective-permute-start.7 = (bf16[24,80,128]{2,1,0:T(8,128)(2,1)S(1)}, bf16[24,80,128]{2,1,0:T(8,128)(2,1)S(1)}, u32[]{:S(2)}, u32[]{:S(2)}) collective-permute-start(bf16[24,80,128]{2,1,0:T(8,128)(2,1)S(1)} %get-tuple-element.29), channel_id=1, source_target_pairs={{8,0},{16,8},{24,16},{32,24},{40,32},{48,40},{56,48},{9,1},{17,9},... | collective-permute-start | bytes 1474568 | tf_op jit(solution)/shard_map/ppermute | solution.py:340
  46.5 0.0 copy-done.6
  46.5 0.7 fusion
  47.2 0.0 copy-start.8
  47.2 0.0 collective-permute-done.10
  47.2 0.9 broadcast_select_fusion.1
  48.1 1.6 %collective-permute-done.3.before_ref = bf16[30,64,128]{2,1,0:T(8,128)(2,1)S(1)} collective-permute-done((bf16[30,64,128]{2,1,0:T(8,128)(2,1)}, bf16[30,64,128]{2,1,0:T(8,128)(2,1)S(1)}, u32[]{:S(2)}, u32[]{:S(2)}) %collective-permute-start.3) | collective-permute-done | bytes 491552 | tf_op jit(solution)/shard_map/ppermute | solution.py:341
  49.7 4.0 %collective-permute-done.4.after_ref = bf16[30,64,128]{2,1,0:T(8,128)(2,1)S(1)} collective-permute-done((bf16[30,64,128]{2,1,0:T(8,128)(2,1)}, bf16[30,64,128]{2,1,0:T(8,128)(2,1)S(1)}, u32[]{:S(2)}, u32[]{:S(2)}) %collective-permute-start.4) | collective-permute-done | bytes 491552 | tf_op jit(solution)/shard_map/ppermute | solution.py:340
  53.7 0.0 collective-permute-done.2.left_ref
  53.7 0.0 collective-permute-done.7.right_ref
  53.7 0.1 shard_map.76
  53.8 2.9 %collective-permute-start.8 = (bf16[24,128,128]{2,1,0:T(8,128)(2,1)S(1)}, bf16[24,128,128]{2,1,0:T(8,128)(2,1)S(1)}, u32[]{:S(2)}, u32[]{:S(2)}) collective-permute-start(bf16[24,128,128]{2,1,0:T(8,128)(2,1)S(1)} %get-tuple-element.30), channel_id=1, source_target_pairs={{0,8},{8,16},{16,24},{24,32},{32,40},{40,48},{48,56},{1,9},{9,17},... | collective-permute-start | bytes 2359304 | tf_op jit(solution)/shard_map/ppermute | solution.py:341
  56.8 2.6 %collective-permute-start.9 = (bf16[24,128,128]{2,1,0:T(8,128)(2,1)S(1)}, bf16[24,128,128]{2,1,0:T(8,128)(2,1)S(1)}, u32[]{:S(2)}, u32[]{:S(2)}) collective-permute-start(bf16[24,128,128]{2,1,0:T(8,128)(2,1)S(1)} %get-tuple-element.31), channel_id=1, source_target_pairs={{8,0},{16,8},{24,16},{32,24},{40,32},{48,40},{56,48},{9,1},{17,9},... | collective-permute-start | bytes 2359304 | tf_op jit(solution)/shard_map/ppermute | solution.py:340
  59.4 0.0 copy-done.4
  59.4 3.1 %shard_map.77 = (bf16[3,640,208]{2,1,0:T(8,128)(2,1)S(1)}, bf16[24,32,416]{2,1,0:T(8,128)(2,1)S(1)}, bf16[24,32,416]{2,1,0:T(8,128)(2,1)S(1)}, bf16[3,1536,128]{2,1,0:T(8,128)(2,1)S(1)}) custom-call(s32[3]{0:T(128)S(1)} %bitcast.3, bf16[32,1536]{1,0:T(8,128)(2,1)S(1)} %pad_maximum_fusion.table_ref, bf16[128,384]{1,0:T(8,128)(2,1)S(1)} %copy-done.4), custom_call_target="tpu_custom_call" | custom-call | tf_op jit(solution)/shard_map/pallas_call | solution.py:157
  62.6 0.0 copy-done.8
  62.6 0.0 copy-start
  62.6 0.0 copy-start.3
  62.6 0.0 copy-start.5
  62.6 8.3 %shard_map.78.own_ref = bf16[3,8,160,1920]{3,2,1,0:T(8,128)(2,1)S(1)} custom-call(s32[1]{0:T(128)} %bitcast.1.live_ref, bf16[20,80,128]{2,1,0:T(8,128)(2,1)S(1)} %get-tuple-element.23.cells_ref, bf16[10,80,128]{2,1,0:T(8,128)(2,1)S(1)} %copy-done.8, bf16[30,64,128]{2,1,0:T(8,128)(2,1)S(1)} %collective-permute-done.3.before_ref, ...), custom_call_target="tpu_custom_call" | custom-call | flops 8000000000 | bytes 2000000 | tf_op jit(solution)/shard_map/pallas_call | solution.py:234
  70.9 0.0 collective-permute-done.8.left_ends
  70.9 0.0 collective-permute-done.9.right_ends
  70.9 0.0 copy-done
  71.0 0.0 copy-done.3
  71.0 0.0 copy-done.5
  71.0 30.1 %shard_map.79 = f32[40,40,128]{2,1,0:T(8,128)} custom-call(s32[1]{0:T(128)} %bitcast.1.live_ref, bf16[24,80,128]{2,1,0:T(8,128)(2,1)S(1)} %collective-permute-done.2.left_ref, bf16[24,128,128]{2,1,0:T(8,128)(2,1)S(1)} %collective-permute-done.8.left_ends, bf16[24,80,128]{2,1,0:T(8,128)(2,1)S(1)} %collective-permute-done.7.right_ref, ...), custom_call_target="tpu_custom_call" | custom-call | tf_op jit(solution)/shard_map/pallas_call | solution.py:314
  (4 shorter events, 0.1 us)
Async XLA Ops:
  0.0 12.3 %collective-permute-start.5 = (bf16[4,1536]{1,0:T(4,128)(2,1)}, bf16[4,1536]{1,0:T(4,128)(2,1)S(1)}, u32[]{:S(2)}, u32[]{:S(2)}) collective-permute-start(bf16[4,1536]{1,0:T(4,128)(2,1)} %param.10), channel_id=1, source_target_pairs={{0,8},{8,0},{16,24},{24,16},{32,40},{40,32},{48,56},{56,48},{1,9},... | collective-permute-start | bytes 36872 | tf_op jit(solution)/shard_map/ppermute | solution.py:330
  1.9 1.1 %copy-start.1 = (f32[40,40,128]{2,1,0:T(8,128)S(1)}, f32[40,40,128]{2,1,0:T(8,128)}, u32[]{:S(2)}) copy-start(f32[40,40,128]{2,1,0:T(8,128)} %reflect_ref.3) | copy-start | bytes 2457604
  3.6 19.4 %collective-permute-start.1 = (bf16[5,80,128]{2,1,0:T(8,128)(2,1)S(1)}, bf16[5,80,128]{2,1,0:T(8,128)(2,1)S(1)}, u32[]{:S(2)}, u32[]{:S(2)}) collective-permute-start(bf16[5,80,128]{2,1,0:T(8,128)(2,1)S(1)} %get-tuple-element.22.after_ref), channel_id=1, source_target_pairs={{1,0},{2,1},{3,2},{4,3},{5,4},{6,5},{7,6},{9,8},{10,9},{11,10},{12... | collective-permute-start | bytes 307208 | tf_op jit(solution)/shard_map/ppermute | solution.py:340
  10.3 17.7 %collective-permute-start = (bf16[5,80,128]{2,1,0:T(8,128)(2,1)S(1)}, bf16[5,80,128]{2,1,0:T(8,128)(2,1)S(1)}, u32[]{:S(2)}, u32[]{:S(2)}) collective-permute-start(bf16[5,80,128]{2,1,0:T(8,128)(2,1)S(1)} %get-tuple-element.21), channel_id=1, source_target_pairs={{0,1},{1,2},{2,3},{3,4},{4,5},{5,6},{6,7},{8,9},{9,10},{10,11},{11... | collective-permute-start | bytes 307208 | tf_op jit(solution)/shard_map/ppermute | solution.py:341
  13.0 5.7 %collective-permute-start.6 = (bf16[8,1536]{1,0:T(8,128)(2,1)S(1)}, bf16[8,1536]{1,0:T(8,128)(2,1)S(1)}, u32[]{:S(2)}, u32[]{:S(2)}) collective-permute-start(bf16[8,1536]{1,0:T(8,128)(2,1)S(1)} %pad_maximum_fusion.2), channel_id=1, source_target_pairs={{0,16},{8,24},{16,0},{24,8},{32,48},{40,56},{48,32},{56,40},{1,17}... | collective-permute-start | bytes 73736 | tf_op jit(solution)/shard_map/ppermute | solution.py:330
  15.4 1.1 %copy-start.2 = (f32[40,40,128]{2,1,0:T(8,128)S(1)}, f32[40,40,128]{2,1,0:T(8,128)}, u32[]{:S(2)}) copy-start(f32[40,40,128]{2,1,0:T(8,128)} %reflect_ref.3) | copy-start | bytes 2457604
  16.5 30.0 %copy-start.6 = (s32[1,1,1,3]{3,2,1,0:T(1,128)S(1)}, s32[1,1,1,3]{3,2,1,0:T(1,128)}, u32[]{:S(2)}) copy-start(s32[1,1,1,3]{3,2,1,0:T(1,128)} %param.11) | copy-start | bytes 40
  18.8 9.3 %copy-start.9 = (bf16[8,1536]{1,0:T(8,128)(2,1)}, bf16[8,1536]{1,0:T(8,128)(2,1)S(1)}, u32[]{:S(2)}) copy-start(bf16[8,1536]{1,0:T(8,128)(2,1)S(1)} %get-tuple-element.40) | copy-start | bytes 73732
  18.8 28.4 %collective-permute-start.10 = (bf16[16,1536]{1,0:T(8,128)(2,1)S(1)}, bf16[16,1536]{1,0:T(8,128)(2,1)}, u32[]{:S(2)}, u32[]{:S(2)}) collective-permute-start(bf16[16,1536]{1,0:T(8,128)(2,1)S(1)} %pad_maximum_fusion.1.rows_ref), channel_id=1, source_target_pairs={{0,32},{8,40},{16,48},{24,56},{32,0},{40,8},{48,16},{56,24},{1,33}... | collective-permute-start | bytes 147464 | tf_op jit(solution)/shard_map/ppermute | solution.py:330
  28.1 31.4 %copy-start.4 = (bf16[128,384]{1,0:T(8,128)(2,1)S(1)}, bf16[128,384]{1,0:T(8,128)(2,1)}, u32[]{:S(2)}) copy-start(bf16[128,384]{1,0:T(8,128)(2,1)} %constant.18.clone.map_ref) | copy-start | bytes 294916
  29.3 0.7 copy-start.7
  30.0 19.7 %collective-permute-start.3 = (bf16[30,64,128]{2,1,0:T(8,128)(2,1)}, bf16[30,64,128]{2,1,0:T(8,128)(2,1)S(1)}, u32[]{:S(2)}, u32[]{:S(2)}) collective-permute-start(bf16[30,64,128]{2,1,0:T(8,128)(2,1)} %get-tuple-element.27), channel_id=1, source_target_pairs={{0,64},{64,128},{128,192},{192,256},{256,320},{320,384},{384,448},... | collective-permute-start | bytes 1474568 | tf_op jit(solution)/shard_map/ppermute | solution.py:341
  39.0 14.7 %collective-permute-start.4 = (bf16[30,64,128]{2,1,0:T(8,128)(2,1)}, bf16[30,64,128]{2,1,0:T(8,128)(2,1)S(1)}, u32[]{:S(2)}, u32[]{:S(2)}) collective-permute-start(bf16[30,64,128]{2,1,0:T(8,128)(2,1)} %get-tuple-element.28), channel_id=1, source_target_pairs={{64,0},{128,64},{192,128},{256,192},{320,256},{384,320},{448,384},... | collective-permute-start | bytes 1474568 | tf_op jit(solution)/shard_map/ppermute | solution.py:340
  40.9 12.8 %collective-permute-start.2 = (bf16[24,80,128]{2,1,0:T(8,128)(2,1)S(1)}, bf16[24,80,128]{2,1,0:T(8,128)(2,1)S(1)}, u32[]{:S(2)}, u32[]{:S(2)}) collective-permute-start(bf16[24,80,128]{2,1,0:T(8,128)(2,1)S(1)} %get-tuple-element.26), channel_id=1, source_target_pairs={{0,8},{8,16},{16,24},{24,32},{32,40},{40,48},{48,56},{1,9},{9,17},... | collective-permute-start | bytes 1474568 | tf_op jit(solution)/shard_map/ppermute | solution.py:341
  42.9 10.8 %collective-permute-start.7 = (bf16[24,80,128]{2,1,0:T(8,128)(2,1)S(1)}, bf16[24,80,128]{2,1,0:T(8,128)(2,1)S(1)}, u32[]{:S(2)}, u32[]{:S(2)}) collective-permute-start(bf16[24,80,128]{2,1,0:T(8,128)(2,1)S(1)} %get-tuple-element.29), channel_id=1, source_target_pairs={{8,0},{16,8},{24,16},{32,24},{40,32},{48,40},{56,48},{9,1},{17,9},... | collective-permute-start | bytes 1474568 | tf_op jit(solution)/shard_map/ppermute | solution.py:340
  47.2 15.4 %copy-start.8 = (bf16[10,80,128]{2,1,0:T(8,128)(2,1)S(1)}, bf16[10,80,128]{2,1,0:T(8,128)(2,1)}, u32[]{:S(2)}) copy-start(bf16[10,80,128]{2,1,0:T(8,128)(2,1)} %copy-done.7) | copy-start | bytes 614404
  53.8 17.1 %collective-permute-start.8 = (bf16[24,128,128]{2,1,0:T(8,128)(2,1)S(1)}, bf16[24,128,128]{2,1,0:T(8,128)(2,1)S(1)}, u32[]{:S(2)}, u32[]{:S(2)}) collective-permute-start(bf16[24,128,128]{2,1,0:T(8,128)(2,1)S(1)} %get-tuple-element.30), channel_id=1, source_target_pairs={{0,8},{8,16},{16,24},{24,32},{32,40},{40,48},{48,56},{1,9},{9,17},... | collective-permute-start | bytes 2359304 | tf_op jit(solution)/shard_map/ppermute | solution.py:341
  56.8 14.2 %collective-permute-start.9 = (bf16[24,128,128]{2,1,0:T(8,128)(2,1)S(1)}, bf16[24,128,128]{2,1,0:T(8,128)(2,1)S(1)}, u32[]{:S(2)}, u32[]{:S(2)}) collective-permute-start(bf16[24,128,128]{2,1,0:T(8,128)(2,1)S(1)} %get-tuple-element.31), channel_id=1, source_target_pairs={{8,0},{16,8},{24,16},{32,24},{40,32},{48,40},{56,48},{9,1},{17,9},... | collective-permute-start | bytes 2359304 | tf_op jit(solution)/shard_map/ppermute | solution.py:340
  62.6 8.3 %copy-start = (s32[2,40,40,128]{3,2,1,0:T(8,128)S(1)}, s32[2,40,40,128]{3,2,1,0:T(8,128)}, u32[]{:S(2)}) copy-start(s32[2,40,40,128]{3,2,1,0:T(8,128)} %slot_ref.1) | copy-start | bytes 4915204
  62.6 8.3 %copy-start.3 = (bf16[2,40,40,128]{3,2,1,0:T(8,128)(2,1)S(1)}, bf16[2,40,40,128]{3,2,1,0:T(8,128)(2,1)}, u32[]{:S(2)}) copy-start(bf16[2,40,40,128]{3,2,1,0:T(8,128)(2,1)} %weights_ref.1) | copy-start | bytes 2457604
  62.6 8.3 %copy-start.5 = (bf16[4,416]{1,0:T(4,128)(2,1)S(1)}, bf16[4,416]{1,0:T(4,128)(2,1)}, u32[]{:S(2)}) copy-start(bf16[4,416]{1,0:T(4,128)(2,1)} %constant.19.clone.mask_ref) | copy-start | bytes 9988
